TPU v7x, 128 devices: a whole 4x4x4 slice. The times are simulated.
128 devices in a mesh: dp: 8 (over y_hi, x), ctx: 2 (over core), tensor: 8 (over z, y_lo).
Axes of the slice: x: 4, y: 4 (y_hi: 2, y_lo: 2; y = y_hi * 2 + y_lo), z: 4, core: 2. Of those that a mesh axis runs over, the one named last changes fastest.
Arguments:
- hidden_in: bfloat16 [16384, 1024], P(('dp', 'ctx', 'tensor')), may hold values from -6 to 6
- segment: int32 [16384], P('dp'), may hold values from 0 to 7, as said below
- norm1_gain: float32 [1024], replicated, may hold values from 0.25 to 1.75
- w_query: bfloat16 [1024, 1024], P(None, 'tensor'), may hold values from -0.1875 to 0.1875
- w_key: bfloat16 [1024, 512], P(None, 'tensor'), may hold values from -0.1875 to 0.1875
- w_value: bfloat16 [1024, 512], P(None, 'tensor'), may hold values from -0.1875 to 0.1875
- q_gain: float32 [1024], P('tensor'), may hold values from 0.25 to 1.75
- k_gain: float32 [512], P('tensor'), may hold values from 0.25 to 1.75
- w_out: bfloat16 [1024, 1024], P('tensor'), may hold values from -0.75 to 0.75
- norm2_gain: float32 [1024], replicated, may hold values from 0.25 to 1.75
- router: bfloat16 [1024, 32], replicated, may hold values from -0.09375 to 0.09375
- w_gate: bfloat16 [32, 1024, 512], P(('dp', 'ctx')), may hold values from -0.1875 to 0.1875
- w_up: bfloat16 [32, 1024, 512], P(('dp', 'ctx')), may hold values from -0.1875 to 0.1875
- w_down: bfloat16 [32, 512, 1024], P(('dp', 'ctx')), may hold values from -1.5 to 1.5
- routes: int32 [16384, 8], P(('dp', 'ctx', 'tensor')), may hold values from 0 to 31, all different within a row; in each aligned block of 128 rows (0 to 127, 128 to 255, ...) at most 64 rows name the same one
- cotangent: bfloat16 [16384, 1024], P(('dp', 'ctx', 'tensor')), may hold values from -6 to 6
Outputs:
- output: bfloat16 [16384, 1024], P(('dp', 'ctx', 'tensor'))
- grad_x: bfloat16 [16384, 1024], P(('dp', 'ctx', 'tensor'))
- grad_norm1_gain: float32 [1024], replicated
- grad_w_query: float32 [1024, 1024], P(None, 'tensor')
- grad_w_key: float32 [1024, 512], P(None, 'tensor')
- grad_w_value: float32 [1024, 512], P(None, 'tensor')
- grad_q_gain: float32 [1024], P('tensor')
- grad_k_gain: float32 [512], P('tensor')
- grad_w_out: float32 [1024, 1024], P('tensor')
- grad_norm2_gain: float32 [1024], replicated
- grad_router: float32 [1024, 32], replicated
- grad_w_gate: float32 [32, 1024, 512], P(('dp', 'ctx'))
- grad_w_up: float32 [32, 1024, 512], P(('dp', 'ctx'))
- grad_w_down: float32 [32, 512, 1024], P(('dp', 'ctx'))
Inputs may be any that keep to these rules, and one draw needn't show every extreme that they name: `segment`: document number of each position within its sequence of 2048 positions: 0 at the first position, 7 at the last, never falling along the sequence. `routes`: each row names 8 different experts. Among the 128 rows of one device no expert is named more than 64 times, a bound that some block reaches.
All inputs are finite; a program needn't handle non-finite values.
Results may differ from a plain program's by a relative error of at most 0.033.
Values may be sent and summed in bfloat16 or wider, within the bound.
A program may use at most 128 MiB of HBM per device.

v0:
```python
import jax
import jax.numpy as jnp
from jax import lax
from jax.sharding import PartitionSpec as P

HEAD_DIM = 64


EPS = 1e-06
THETA = 10000.0
MASKED = -1e30


def split_up(x, dim, count):
    before, after = (x.shape[:dim], x.shape[dim + 1 :])
    return jnp.moveaxis(x.reshape(*before, count, -1, *after), dim, 0)


def in_order(blocks, dim):
    lengths = list(blocks.shape[1:])
    lengths[dim] *= blocks.shape[0]
    return jnp.moveaxis(blocks, 0, dim).reshape(lengths)


def joined_exchange(x, axis, axes, splits, concats):
    sizes = [lax.axis_size(a) for a in axes]
    blocks = split_up(x, splits[0], sizes[0])
    blocks = jnp.moveaxis(split_up(blocks, splits[1] + 1, sizes[1]), 0, 1)
    inside = blocks.shape[2:]
    blocks = blocks.reshape(-1, *inside)
    blocks = lax.all_to_all(blocks, axis, split_axis=0, concat_axis=0, tiled=True)
    blocks = in_order(blocks.reshape(*sizes, *inside), concats[0] + 1)
    return in_order(blocks, concats[1])


def from_everyone(x, axis):
    copies = jnp.broadcast_to(x, (lax.axis_size(axis), *x.shape))
    return lax.all_to_all(copies, axis, split_axis=0, concat_axis=0, tiled=True)


def collect(x, axis, dim):
    blocks = from_everyone(x, axis)
    return in_order(blocks, dim)


def taken_together(x, axis):
    everything = from_everyone(x, axis)
    return jnp.sum(everything, axis=0)


def packed_total(arrays, axis):
    line, at, finished = (jnp.concatenate([a.reshape(-1) for a in arrays]), 0, [])
    so_far = taken_together(line, axis)
    for a in arrays:
        finished.append(so_far[at : at + a.size].reshape(a.shape))
        at += a.size
    return tuple(finished)


def sent_and_summed(x, axis, dim):
    count = lax.axis_size(axis)
    blocks = lax.all_to_all(split_up(x, dim, count), axis, 0, 0, tiled=True)
    return jnp.sum(blocks.astype(jnp.float32), axis=0)


def matmul(left, right):
    return jnp.dot(left, right, preferred_element_type=jnp.float32)


def matmul_tn(left, right):
    return lax.dot_general(
        left, right, (((0,), (0,)), ((), ())), preferred_element_type=jnp.float32
    )


def matmul_nt(left, right):
    return lax.dot_general(
        left, right, (((1,), (1,)), ((), ())), preferred_element_type=jnp.float32
    )


def rope_tables(positions, half_dim):
    inverse = THETA ** (-(jnp.arange(half_dim, dtype=jnp.float32) * 2.0 / (2 * half_dim)))
    angles = positions.astype(jnp.float32)[:, None] * inverse[None, :]
    return (jnp.cos(angles), jnp.sin(angles))


def rotate(values, cos_table, sin_table, flip_sign):
    half_dim = values.shape[-1] // 2
    first_half = values[..., :half_dim]
    second_half = values[..., half_dim:]
    cos_part = cos_table[:, None, :]
    sin_part = sin_table[:, None, :] * flip_sign
    return jnp.concatenate(
        [
            first_half * cos_part - second_half * sin_part,
            second_half * cos_part + first_half * sin_part,
        ],
        -1,
    )


def route_rows(buffer):
    reshaped = buffer.reshape((lax.axis_size("dp"), lax.axis_size("ctx")) + buffer.shape[1:])
    arrived = joined_exchange(reshaped, ("dp", "ctx"), ("dp", "ctx"), (0, 1), (0, 1))
    return arrived.reshape(buffer.shape)


def shards(
    hidden_in,
    segment,
    norm1_gain,
    w_query,
    w_key,
    w_value,
    q_gain,
    k_gain,
    w_out,
    norm2_gain,
    router,
    w_gate,
    w_up,
    w_down,
    routes,
    cotangent,
):
    tok_rows = hidden_in.shape[0]
    model_dim = hidden_in.shape[1]
    n_tensor = lax.axis_size("tensor")
    n_groups = lax.axis_size(("dp", "ctx"))
    seq_len = segment.shape[0]
    slab_rows = tok_rows * n_tensor
    ctx_index = lax.axis_index("ctx")
    head_dim = HEAD_DIM
    q_cols = w_query.shape[1]
    kv_cols = w_key.shape[1]
    q_heads = q_cols // head_dim
    kv_heads = kv_cols // head_dim
    group_size = q_heads // kv_heads
    q_width = q_cols * n_tensor
    k_width = kv_cols * n_tensor
    block_rows = min(512, slab_rows)
    n_blocks = slab_rows // block_rows
    scaling = head_dim ** (-0.5)
    top_k = routes.shape[1]
    exp_dev = w_gate.shape[0]
    n_experts = exp_dev * n_groups
    capacity = max(2, 2 * tok_rows * top_k // n_experts)
    x_float = hidden_in.astype(jnp.float32)
    inv_one = lax.rsqrt(jnp.mean(x_float * x_float, -1, keepdims=True) + EPS)
    x_hat = x_float * inv_one
    normed_one = (x_hat * norm1_gain).astype(jnp.bfloat16)
    rows_all = collect(normed_one, "tensor", 0)
    w_qkv = jnp.concatenate([w_query, w_key, w_value], 1)
    projected = matmul(rows_all, w_qkv)
    q_raw = projected[:, :q_cols]
    k_raw = projected[:, q_cols : q_cols + kv_cols]
    v_raw = projected[:, q_cols + kv_cols :]
    q_square, k_square = packed_total(
        (jnp.sum(q_raw * q_raw, 1), jnp.sum(k_raw * k_raw, 1)), "tensor"
    )
    inv_q = lax.rsqrt(q_square / q_width + EPS)[:, None]
    inv_k = lax.rsqrt(k_square / k_width + EPS)[:, None]
    q_hat = q_raw * inv_q
    k_hat = k_raw * inv_k
    positions = ctx_index * slab_rows + jnp.arange(slab_rows, dtype=jnp.int32)
    cos_table, sin_table = rope_tables(positions, head_dim // 2)
    queries = rotate(
        (q_hat * q_gain).reshape(slab_rows, q_heads, head_dim), cos_table, sin_table, 1.0
    ).astype(jnp.bfloat16)
    keys_local = rotate(
        (k_hat * k_gain).reshape(slab_rows, kv_heads, head_dim), cos_table, sin_table, 1.0
    ).astype(jnp.bfloat16)
    kv_local = jnp.concatenate(
        [keys_local.reshape(slab_rows, kv_cols), v_raw.astype(jnp.bfloat16)], 1
    )
    kv_all = collect(kv_local, "ctx", 0)
    key_pos = jnp.arange(seq_len, dtype=jnp.int32)
    query_seg = lax.dynamic_slice_in_dim(segment, ctx_index * slab_rows, slab_rows)
    keys_all = kv_all[:, :kv_cols].reshape(seq_len, kv_heads, head_dim)
    values_all = kv_all[:, kv_cols:].reshape(seq_len, kv_heads, head_dim)
    q_blocks = queries.reshape(n_blocks, block_rows, kv_heads, group_size, head_dim)
    seg_blocks = query_seg.reshape(n_blocks, block_rows)
    pos_blocks = positions.reshape(n_blocks, block_rows)

    def block_scores(q_block, seg_block, pos_block, keys_now):
        raw_scores = (
            jnp.einsum("qkgd,tkd->kgqt", q_block, keys_now, preferred_element_type=jnp.float32)
            * scaling
        )
        allowed = (seg_block[:, None] == segment[None, :]) & (
            key_pos[None, :] <= pos_block[:, None]
        )
        return jnp.where(allowed, raw_scores, MASKED)

    def forward_block(block_args):
        q_block, seg_block, pos_block = block_args
        scores = block_scores(q_block, seg_block, pos_block, keys_all)
        largest = jnp.max(scores, -1, keepdims=True)
        exponent = jnp.exp(scores - largest)
        row_sums = jnp.sum(exponent, -1, keepdims=True)
        probabilities = exponent / row_sums
        head_vals = jnp.einsum(
            "kgqt,tkd->qkgd",
            probabilities.astype(jnp.bfloat16),
            values_all,
            preferred_element_type=jnp.float32,
        )
        return (head_vals.reshape(block_rows, q_cols), (largest + jnp.log(row_sums))[..., 0])

    head_blocks, lse_blocks = lax.map(forward_block, (q_blocks, seg_blocks, pos_blocks))
    heads_out = head_blocks.reshape(slab_rows, q_cols).astype(jnp.bfloat16)
    attended = lax.psum_scatter(
        matmul(heads_out, w_out).astype(jnp.bfloat16), "tensor", scatter_dimension=0, tiled=True
    ).astype(jnp.float32)
    residual = x_float + attended
    inv_two = lax.rsqrt(jnp.mean(residual * residual, -1, keepdims=True) + EPS)
    res_hat = residual * inv_two
    normed_two = (res_hat * norm2_gain).astype(jnp.bfloat16)
    logits = matmul(normed_two, router)
    expert_ids = jnp.arange(n_experts, dtype=jnp.int32)
    route_hot = routes[:, :, None] == expert_ids[None, None, :]
    chosen = jnp.sum(jnp.where(route_hot, logits[:, None, :], 0.0), -1)
    top_logit = jnp.max(chosen, -1, keepdims=True)
    gate_exp = jnp.exp(chosen - top_logit)
    gate_weights = gate_exp / jnp.sum(gate_exp, -1, keepdims=True)
    flat_ids = routes.reshape(-1)
    flat_hot = route_hot.reshape(-1, n_experts).astype(jnp.int32)
    earlier = jnp.cumsum(flat_hot, 0) - flat_hot
    slot_index = jnp.sum(earlier * flat_hot, 1)
    targets = flat_ids * capacity + slot_index
    source_rows = jnp.arange(tok_rows * top_k, dtype=jnp.int32) // top_k
    send_rows = (
        jnp.zeros((n_experts * capacity, model_dim), jnp.bfloat16)
        .at[targets]
        .set(normed_two[source_rows])
    )
    arrived = route_rows(send_rows.reshape(n_groups, exp_dev, capacity, model_dim))
    gate_h = jnp.einsum("gjcd,jdf->gjcf", arrived, w_gate, preferred_element_type=jnp.float32)
    up_h = jnp.einsum("gjcd,jdf->gjcf", arrived, w_up, preferred_element_type=jnp.float32)
    sig_gate = jax.nn.sigmoid(gate_h)
    silu_gate = gate_h * sig_gate
    activation = (silu_gate * up_h).astype(jnp.bfloat16)
    expert_out = jnp.einsum(
        "gjcf,jfd->gjcd", activation, w_down, preferred_element_type=jnp.float32
    ).astype(jnp.bfloat16)
    returned = route_rows(expert_out).reshape(n_experts * capacity, model_dim)
    picked = returned[targets].reshape(tok_rows, top_k, model_dim).astype(jnp.float32)
    output = (residual + jnp.sum(gate_weights[:, :, None] * picked, 1)).astype(jnp.bfloat16)
    grad_out = cotangent.astype(jnp.float32)
    d_gate = jnp.sum(picked * grad_out[:, None, :], -1)
    d_choice = gate_weights * (d_gate - jnp.sum(gate_weights * d_gate, -1, keepdims=True))
    d_logits = jnp.sum(jnp.where(route_hot, d_choice[:, :, None], 0.0), 1)
    router_part = lax.dot_general(
        normed_two.astype(jnp.float32),
        d_logits,
        (((0,), (0,)), ((), ())),
        precision=lax.Precision.HIGHEST,
    )
    d_normed = jnp.dot(d_logits, router.astype(jnp.float32).T, precision=lax.Precision.HIGHEST)
    d_picked = (
        (gate_weights[:, :, None] * grad_out[:, None, :])
        .astype(jnp.bfloat16)
        .reshape(-1, model_dim)
    )
    d_send = jnp.zeros((n_experts * capacity, model_dim), jnp.bfloat16).at[targets].set(d_picked)
    d_arrived = route_rows(d_send.reshape(n_groups, exp_dev, capacity, model_dim))
    d_act = jnp.einsum("gjcd,jfd->gjcf", d_arrived, w_down, preferred_element_type=jnp.float32)
    grad_down = jnp.einsum(
        "gjcf,gjcd->jfd", activation, d_arrived, preferred_element_type=jnp.float32
    )
    d_gate_h = (d_act * up_h * sig_gate * (1.0 + gate_h * (1.0 - sig_gate))).astype(jnp.bfloat16)
    d_up_h = (d_act * silu_gate).astype(jnp.bfloat16)
    grad_gate = jnp.einsum("gjcd,gjcf->jdf", arrived, d_gate_h, preferred_element_type=jnp.float32)
    grad_up = jnp.einsum("gjcd,gjcf->jdf", arrived, d_up_h, preferred_element_type=jnp.float32)
    d_inputs = jnp.einsum("gjcf,jdf->gjcd", d_gate_h, w_gate, preferred_element_type=jnp.float32)
    d_inputs = (
        d_inputs + jnp.einsum("gjcf,jdf->gjcd", d_up_h, w_up, preferred_element_type=jnp.float32)
    ).astype(jnp.bfloat16)
    d_back = route_rows(d_inputs).reshape(n_experts * capacity, model_dim)
    d_normed = d_normed + jnp.sum(
        d_back[targets].reshape(tok_rows, top_k, model_dim).astype(jnp.float32), 1
    )
    norm2_part = jnp.sum(d_normed * res_hat, 0)
    d_scaled_two = d_normed * norm2_gain
    d_resid = grad_out + inv_two * (
        d_scaled_two - res_hat * jnp.mean(d_scaled_two * res_hat, -1, keepdims=True)
    )
    d_att_all = collect(d_resid.astype(jnp.bfloat16), "tensor", 0)
    grad_wo_part = matmul_tn(heads_out, d_att_all)
    d_heads = matmul_nt(d_att_all, w_out).astype(jnp.bfloat16)
    keys_back, values_back = (keys_all, values_all)
    d_blocks = d_heads.reshape(n_blocks, block_rows, kv_heads, group_size, head_dim)

    def backward_block(carried, block_args):
        d_keys, d_values = carried
        q_block, seg_block, pos_block, lse_block, dh_block = block_args
        scores = block_scores(q_block, seg_block, pos_block, keys_back)
        probabilities = jnp.exp(scores - lse_block[..., None])
        d_probs = jnp.einsum(
            "qkgd,tkd->kgqt", dh_block, values_back, preferred_element_type=jnp.float32
        )
        d_scores = (
            probabilities * (d_probs - jnp.sum(probabilities * d_probs, -1, keepdims=True))
        ).astype(jnp.bfloat16)
        d_query = (
            jnp.einsum("kgqt,tkd->qkgd", d_scores, keys_back, preferred_element_type=jnp.float32)
            * scaling
        )
        d_keys = (
            d_keys
            + jnp.einsum("kgqt,qkgd->tkd", d_scores, q_block, preferred_element_type=jnp.float32)
            * scaling
        )
        d_values = d_values + jnp.einsum(
            "kgqt,qkgd->tkd",
            probabilities.astype(jnp.bfloat16),
            dh_block,
            preferred_element_type=jnp.float32,
        )
        return ((d_keys, d_values), d_query.reshape(block_rows, q_cols))

    zero_kv = jnp.zeros((seq_len, kv_heads, head_dim), jnp.float32)
    (d_keys_all, d_values_all), d_query_blocks = lax.scan(
        backward_block, (zero_kv, zero_kv), (q_blocks, seg_blocks, pos_blocks, lse_blocks, d_blocks)
    )
    d_kv = jnp.concatenate(
        [d_keys_all.reshape(seq_len, kv_cols), d_values_all.reshape(seq_len, kv_cols)], 1
    )
    d_kv_own = sent_and_summed(d_kv.astype(jnp.bfloat16), "ctx", 0)
    d_v_raw = d_kv_own[:, kv_cols:].astype(jnp.bfloat16)
    d_q_norm = rotate(
        d_query_blocks.reshape(slab_rows, q_heads, head_dim), cos_table, sin_table, -1.0
    ).reshape(slab_rows, q_cols)
    d_k_norm = rotate(
        d_kv_own[:, :kv_cols].reshape(slab_rows, kv_heads, head_dim), cos_table, sin_table, -1.0
    ).reshape(slab_rows, kv_cols)
    qgain_part = jnp.sum(d_q_norm * q_hat, 0)
    kgain_part = jnp.sum(d_k_norm * k_hat, 0)
    q_term = d_q_norm * q_gain
    k_term = d_k_norm * k_gain
    q_inner, k_inner = packed_total(
        (jnp.sum(q_term * q_hat, 1), jnp.sum(k_term * k_hat, 1)), "tensor"
    )
    d_q_raw = (inv_q * (q_term - q_hat * (q_inner / q_width)[:, None])).astype(jnp.bfloat16)
    d_k_raw = (inv_k * (k_term - k_hat * (k_inner / k_width)[:, None])).astype(jnp.bfloat16)
    d_qkv = jnp.concatenate([d_q_raw, d_k_raw, d_v_raw], 1)
    grad_qkv = matmul_tn(rows_all, d_qkv)
    d_normed_one = lax.psum_scatter(
        matmul_nt(d_qkv, w_qkv).astype(jnp.bfloat16), "tensor", scatter_dimension=0, tiled=True
    ).astype(jnp.float32)
    norm1_part = jnp.sum(d_normed_one * x_hat, 0)
    d_scaled_one = d_normed_one * norm1_gain
    grad_x = (
        d_resid
        + inv_one * (d_scaled_one - x_hat * jnp.mean(d_scaled_one * x_hat, -1, keepdims=True))
    ).astype(jnp.bfloat16)
    grad_gate_all, grad_up_all, grad_down_all, router_sum, norm1_sum, norm2_sum = (
        lax.psum(grad_gate.astype(jnp.bfloat16), "tensor").astype(jnp.float32),
        lax.psum(grad_up.astype(jnp.bfloat16), "tensor").astype(jnp.float32),
        lax.psum(grad_down.astype(jnp.bfloat16), "tensor").astype(jnp.float32),
        lax.psum(router_part.astype(jnp.bfloat16), "tensor").astype(jnp.float32),
        lax.psum(norm1_part.astype(jnp.bfloat16), "tensor").astype(jnp.float32),
        lax.psum(norm2_part.astype(jnp.bfloat16), "tensor").astype(jnp.float32),
    )
    totals = (
        lax.psum(grad_qkv.astype(jnp.bfloat16), ("dp", "ctx")).astype(jnp.float32),
        lax.psum(grad_wo_part.astype(jnp.bfloat16), ("dp", "ctx")).astype(jnp.float32),
        lax.psum(qgain_part.astype(jnp.bfloat16), ("dp", "ctx")).astype(jnp.float32),
        lax.psum(kgain_part.astype(jnp.bfloat16), ("dp", "ctx")).astype(jnp.float32),
        lax.psum(router_sum.astype(jnp.bfloat16), ("dp", "ctx")).astype(jnp.float32),
        lax.psum(norm1_sum.astype(jnp.bfloat16), ("dp", "ctx")).astype(jnp.float32),
        lax.psum(norm2_sum.astype(jnp.bfloat16), ("dp", "ctx")).astype(jnp.float32),
    )
    grad_qkv_all = totals[0]
    return (
        output,
        grad_x,
        totals[5],
        grad_qkv_all[:, :q_cols],
        grad_qkv_all[:, q_cols : q_cols + kv_cols],
        grad_qkv_all[:, q_cols + kv_cols :],
        totals[2],
        totals[3],
        totals[1],
        totals[6],
        totals[4],
        grad_gate_all,
        grad_up_all,
        grad_down_all,
    )


def solution(mesh):
    return jax.shard_map(
        shards,
        mesh=mesh,
        in_specs=(
            P(("dp", "ctx", "tensor"), None),
            P("dp"),
            P(),
            P(None, "tensor"),
            P(None, "tensor"),
            P(None, "tensor"),
            P("tensor"),
            P("tensor"),
            P("tensor", None),
            P(),
            P(),
            P(("dp", "ctx"), None, None),
            P(("dp", "ctx"), None, None),
            P(("dp", "ctx"), None, None),
            P(("dp", "ctx", "tensor"), None),
            P(("dp", "ctx", "tensor"), None),
        ),
        out_specs=(
            P(("dp", "ctx", "tensor"), None),
            P(("dp", "ctx", "tensor"), None),
            P(),
            P(None, "tensor"),
            P(None, "tensor"),
            P(None, "tensor"),
            P("tensor"),
            P("tensor"),
            P("tensor", None),
            P(),
            P(),
            P(("dp", "ctx"), None, None),
            P(("dp", "ctx"), None, None),
            P(("dp", "ctx"), None, None),
        ),
        check_vma=False,
    )
```

profile of v0, /device:TPU:1, one launch (start us, length us, event | category | flops | bytes accessed | tf_op | source)
XLA Modules:
  0.0 947.7 jit_solution(13475474505167914838)
XLA Ops:
  11.2 6.9 all-to-all-start
  22.1 22.1 %all-to-all-done = bf16[8,128,1024]{2,1,0:T(8,128)(2,1)} async-done(((bf16[8,128,1024]{2,1,0:T(8,128)(2,1)}), bf16[8,128,1024]{2,1,0:T(8,128)(2,1)}, u32[]{:S(2)}, u32[]{:S(2)}) %all-to-all-start) | async-done | bytes 2097184 | tf_op jit(solution)/shard_map/all_to_all | solution.py:38
  68.0 7.7 all_to_all.52
  79.6 20.3 %while.28 = (s32[]{:T(128)}, bf16[2,512,128]{2,1,0:T(8,128)(2,1)}, f32[2,1,2,512]{3,2,1,0:T(2,128)}, s32[2,512]{1,0:T(2,128)S(1)}, s32[2048]{0:T(1024)S(1)}, /*i...) while((s32[]{:T(128)}, bf16[2,512,128]{2,1,0:T(8,128)(2,1)}, ...), condition=%wide.region_7.8_spmd.clone, body=%wide.region_4.7_spmd.clone.sunk | while | flops 565181440 | bytes 32887520 | solution.py:211
  103.8 9.0 reduce-window.6
  117.9 36.8 %reduce-scatter.3.cloned.1.call-done = bf16[128,1024]{1,0:T(8,128)(2,1)} async-done(((bf16[1024,1024]{1,0:T(8,128)(2,1)}), bf16[128,1024]{1,0:T(8,128)(2,1)}) %reduce-scatter.3.cloned.1.call-update) | async-done | bytes 262160 | tf_op jit(solution)/shard_map/reduce_scatter | solution.py:213
  160.1 8.8 scatter_custom_fusion.1
  168.9 7.2 all-to-all-start.5
  176.1 17.8 %scatter_custom_fusion = bf16[2048,1024]{1,0:T(8,128)(2,1)} fusion(s32[1024]{0:T(1024)S(1)} %bitcast.467, bf16[128,1024]{1,0:T(8,128)(2,1)} %copy-done.16, s32[1024]{0:T(1024)S(1)} %broadcast_clamp_fusion.1, bf16[]{:T(256)} %constant.110.clone.1), kind=kCustom, calls=%fused_computation.115 | custom fusion | bytes 4194816 | tf_op jit(solution)/shard_map/scatter | solution.py:236
  194.0 38.1 %all-to-all-done.5 = bf16[16,1,1,2,64,1024]{5,4,3,2,1,0:T(8,128)(2,1)} async-done(((bf16[16,1,1,2,64,1024]{5,4,3,2,1,0:T(8,128)(2,1)}), bf16[16,1,1,2,64,1024]{5,4,3,2,1,0:T(8,128)(2,1)}, u32[]{:S(2)}, u32[]{:S(2)}) %all-to-all-start.5) | async-done | bytes 4194336 | tf_op jit(solution)/shard_map/all_to_all | solution.py:31
  232.0 6.9 all-to-all-start.3
  243.9 50.9 %all-to-all-done.3 = bf16[16,1,1,2,64,1024]{5,4,3,2,1,0:T(8,128)(2,1)} async-done(((bf16[16,1,1,2,64,1024]{5,4,3,2,1,0:T(8,128)(2,1)}), bf16[16,1,1,2,64,1024]{5,4,3,2,1,0:T(8,128)(2,1)}, u32[]{:S(2)}, u32[]{:S(2)}) %all-to-all-start.3) | async-done | bytes 4194336 | tf_op jit(solution)/shard_map/all_to_all | solution.py:31
  302.3 5.8 fusion.63
  312.9 6.7 all-to-all-start.4
  328.7 46.8 %all-to-all-done.4 = bf16[16,1,1,2,64,1024]{5,4,3,2,1,0:T(8,128)(2,1)} async-done(((bf16[16,1,1,2,64,1024]{5,4,3,2,1,0:T(8,128)(2,1)}), bf16[16,1,1,2,64,1024]{5,4,3,2,1,0:T(8,128)(2,1)}, u32[]{:S(2)}, u32[]{:S(2)}) %all-to-all-start.4) | async-done | bytes 4194336 | tf_op jit(solution)/shard_map/all_to_all | solution.py:31
  375.5 7.1 all-to-all-start.6
  382.7 6.6 bitcast_convert_fusion.1
  389.3 8.7 gather_fusion
  402.2 36.2 %all-to-all-done.6 = bf16[16,1,1,2,64,1024]{5,4,3,2,1,0:T(8,128)(2,1)} async-done(((bf16[16,1,1,2,64,1024]{5,4,3,2,1,0:T(8,128)(2,1)}), bf16[16,1,1,2,64,1024]{5,4,3,2,1,0:T(8,128)(2,1)}, u32[]{:S(2)}, u32[]{:S(2)}) %all-to-all-start.6) | async-done | bytes 4194336 | tf_op jit(solution)/shard_map/all_to_all | solution.py:31
  438.5 8.8 gather_fusion.1
  457.9 6.7 bitcast_convert_fusion
  464.6 6.0 bitcast_convert_fusion.2
  471.4 12.8 %all-to-all-done.7 = bf16[8,128,1024]{2,1,0:T(8,128)(2,1)} async-done(((bf16[8,128,1024]{2,1,0:T(8,128)(2,1)}), bf16[8,128,1024]{2,1,0:T(8,128)(2,1)}, u32[]{:S(2)}, u32[]{:S(2)}) %all-to-all-start.7) | async-done | bytes 2097184 | tf_op jit(solution)/shard_map/all_to_all | solution.py:38
  487.1 55.6 %while.29 = (s32[]{:T(128)}, f32[2048,1,64]{0,2,1:T(8,128)S(1)}, f32[2048,1,64]{0,2,1:T(8,128)}, f32[2,512,128]{1,0,2:T(2,128)}, bf16[2,512,1,2,64]{1,4,3,2,0:T(...) while((s32[]{:T(128)}, f32[2048,1,64]{0,2,1:T(8,128)S(1)}, ...), condition=%wide.region_26.27_spmd.clone, body=%wide.region_24.26_spmd.clone.sunk | while | flops 1377500160 | bytes 124306208 | solution.py:324
  508.0 6.8 fusion.212
  535.7 6.9 fusion.212
  560.0 5.9 all-to-all-done.9
  575.6 162.8 %all-reduce.9.cloned.1.call-done = (bf16[1024,32]{0,1:T(8,128)(2,1)}, bf16[2,1024,512]{2,1,0:T(8,128)(2,1)}, bf16[2,1024,512]{2,1,0:T(8,128)(2,1)}, bf16[2,512,1024]{2,1,0:T(8,128)(2,1)}) async-done(((bf16[1024,32]{0,1:T(8,128)(2,1)}, bf16[2,1024,512]{2,1,0:T(8,128)(2,1)}, bf16[2,1024,512]{2,1,0:T(8,128)(2,1)}, bf16[2,512,1024]{2,1,0:T(8,128)(2,1)}), (bf16[1024,32]{0,1:T(8,128)(2,1)}, ...) | async-done | bytes 6357008 | tf_op jit(solution)/shard_map/psum | solution.py:362
  738.4 56.3 %reduce-scatter.5.cloned.1.call-done = bf16[128,1024]{1,0:T(8,128)(2,1)} async-done(((bf16[1024,1024]{1,0:T(8,128)(2,1)}), bf16[128,1024]{1,0:T(8,128)(2,1)}) %reduce-scatter.5.cloned.1.call-update) | async-done | bytes 262160 | tf_op jit(solution)/shard_map/reduce_scatter | solution.py:349
  796.0 13.1 %all-reduce.2 = (bf16[1024]{0:T(1024)(128)(2,1)S(1)}, bf16[1024]{0:T(1024)(128)(2,1)S(1)}) all-reduce(bf16[1024]{0:T(1024)(128)(2,1)S(1)} %get-tuple-element.411, bf16[1024]{0:T(1024)(128)(2,1)S(1)} %copy-done.57), channel_id=1, replica_groups=mesh['dp'=8,'ctx'=2,'tensor'=8] {'tensor'}, use_global_device_ids=true, to_apply=%region_34.35 | all-reduce | flops 2048 | bytes 8192 | tf_op jit(solution)/shard_map/psum | solution.py:363
  809.1 37.8 %all-reduce = (bf16[1024]{0:T(1024)(128)(2,1)S(1)}, bf16[128]{0:T(256)(128)(2,1)S(1)}, bf16[64]{0:T(256)(128)(2,1)S(1)}, bf16[1024]{0:T(1024)(128)(2,1)S(1)}) all-reduce(bf16[1024]{0:T(1024)(128)(2,1)S(1)} %get-tuple-element.462, bf16[128]{0:T(256)(128)(2,1)S(1)} %copy-done.69, ...), channel_id=1, replica_groups=mesh['dp'=8,'ctx'=2,'tensor'=8] {'dp','ctx'}, use_global_device_ids=true, to_apply=%region_35.36 | all-reduce | flops 2240 | bytes 8960 | tf_op jit(solution)/shard_map/psum | solution.py:372
  860.9 73.7 %all-reduce.7.cloned.1.call-done = (bf16[1024,256]{1,0:T(8,128)(2,1)}, bf16[128,1024]{1,0:T(8,128)(2,1)}, bf16[1024,32]{0,1:T(8,128)(2,1)}) async-done(((bf16[1024,256]{1,0:T(8,128)(2,1)}, bf16[128,1024]{1,0:T(8,128)(2,1)}, bf16[1024,32]{0,1:T(8,128)(2,1)}), (bf16[1024,256]{1,0:T(8,128)(2,1)}, bf16[128,1024]{1,0:T(8,128)(2,1)}, bf16[1024,32]{0,1:T(8,128)(2,1)})) %all-reduce.7.cloned.1.call-update) | async-done | bytes 851984 | tf_op jit(solution)/shard_map/psum | solution.py:367
  (344 shorter events, 204.5 us)
Async XLA Ops:
  7.2 295.1 %copy-start = (bf16[2,512,1024]{2,1,0:T(8,128)(2,1)S(1)}, bf16[2,512,1024]{2,1,0:T(8,128)(2,1)}, u32[]{:S(2)}) copy-start(bf16[2,512,1024]{2,1,0:T(8,128)(2,1)} %param.33) | copy-start | bytes 6291460
  8.5 35.7 %copy-start.67 = (f32[128]{0:T(128)}, f32[128]{0:T(128)S(1)}, u32[]{:S(2)}) copy-start(f32[128]{0:T(128)S(1)} %add_rsqrt_fusion.1) | copy-start | bytes 1540
  11.2 33.0 %all-to-all-start = ((bf16[8,128,1024]{2,1,0:T(8,128)(2,1)}), bf16[8,128,1024]{2,1,0:T(8,128)(2,1)}, u32[]{:S(2)}, u32[]{:S(2)}) async-start(bf16[8,128,1024]{2,1,0:T(8,128)(2,1)} %broadcast_in_dim.62), calls=%async_computation | async-start | bytes 4194304 | tf_op jit(solution)/shard_map/all_to_all | solution.py:38
  22.1 43.0 %copy-start.26 = (f32[1024,32]{0,1:T(8,128)}, f32[1024,32]{0,1:T(8,128)S(1)}, u32[]{:S(2)}) copy-start(f32[1024,32]{0,1:T(8,128)S(1)} %get-tuple-element.499) | copy-start | bytes 393220
  46.8 31.0 %copy-start.5 = (f32[1024,256]{0,1:T(8,128)}, f32[1024,256]{0,1:T(8,128)S(1)}, u32[]{:S(2)}) copy-start(f32[1024,256]{0,1:T(8,128)S(1)} %fusion.130) | copy-start | bytes 3145732
  47.7 9.2 all-to-all-start.1
  51.7 103.0 %reduce-scatter.3.cloned.1.call-start = ((), (), s32[]{:S(2)}) async-start(), calls=%async_computation.12 | async-start | bytes 2359296 | tf_op jit(solution)/shard_map/reduce_scatter | solution.py:213
  79.6 20.3 %copy-start.28 = (bf16[128,1024]{1,0:T(8,128)(2,1)S(1)}, bf16[128,1024]{1,0:T(8,128)(2,1)}, u32[]{:S(2)}) copy-start(bf16[128,1024]{1,0:T(8,128)(2,1)} %param.28) | copy-start | bytes 786436
  99.9 54.8 %copy-start.4 = (bf16[128,1024]{1,0:T(8,128)(2,1)S(1)}, bf16[128,1024]{1,0:T(8,128)(2,1)}, u32[]{:S(2)}) copy-start(bf16[128,1024]{1,0:T(8,128)(2,1)} %param.20) | copy-start | bytes 786436
  168.9 63.1 %all-to-all-start.5 = ((bf16[16,1,1,2,64,1024]{5,4,3,2,1,0:T(8,128)(2,1)}), bf16[16,1,1,2,64,1024]{5,4,3,2,1,0:T(8,128)(2,1)}, u32[]{:S(2)}, u32[]{:S(2)}) async-start(bf16[16,1,1,2,64,1024]{5,4,3,2,1,0:T(8,128)(2,1)} %bitcast.449), calls=%async_computation.6 | async-start | bytes 8388608 | tf_op jit(solution)/shard_map/all_to_all | solution.py:31
  232.0 62.7 %all-to-all-start.3 = ((bf16[16,1,1,2,64,1024]{5,4,3,2,1,0:T(8,128)(2,1)}), bf16[16,1,1,2,64,1024]{5,4,3,2,1,0:T(8,128)(2,1)}, u32[]{:S(2)}, u32[]{:S(2)}) async-start(bf16[16,1,1,2,64,1024]{5,4,3,2,1,0:T(8,128)(2,1)} %bitcast.448), calls=%async_computation.4 | async-start | bytes 8388608 | tf_op jit(solution)/shard_map/all_to_all | solution.py:31
  312.9 62.6 %all-to-all-start.4 = ((bf16[16,1,1,2,64,1024]{5,4,3,2,1,0:T(8,128)(2,1)}), bf16[16,1,1,2,64,1024]{5,4,3,2,1,0:T(8,128)(2,1)}, u32[]{:S(2)}, u32[]{:S(2)}) async-start(bf16[16,1,1,2,64,1024]{5,4,3,2,1,0:T(8,128)(2,1)} %copy.169), calls=%async_computation.5 | async-start | bytes 8388608 | tf_op jit(solution)/shard_map/all_to_all | solution.py:31
  375.5 62.9 %all-to-all-start.6 = ((bf16[16,1,1,2,64,1024]{5,4,3,2,1,0:T(8,128)(2,1)}), bf16[16,1,1,2,64,1024]{5,4,3,2,1,0:T(8,128)(2,1)}, u32[]{:S(2)}, u32[]{:S(2)}) async-start(bf16[16,1,1,2,64,1024]{5,4,3,2,1,0:T(8,128)(2,1)} %copy.175), calls=%async_computation.7 | async-start | bytes 8388608 | tf_op jit(solution)/shard_map/all_to_all | solution.py:31
  453.3 30.9 %all-to-all-start.7 = ((bf16[8,128,1024]{2,1,0:T(8,128)(2,1)}), bf16[8,128,1024]{2,1,0:T(8,128)(2,1)}, u32[]{:S(2)}, u32[]{:S(2)}) async-start(bf16[8,128,1024]{2,1,0:T(8,128)(2,1)} %broadcast_in_dim.73), calls=%async_computation.8 | async-start | bytes 4194304 | tf_op jit(solution)/shard_map/all_to_all | solution.py:38
  457.7 280.7 %all-reduce.9.cloned.1.call-start = ((), (), s32[]{:S(2)}) async-start(), calls=%async_computation.15 | async-start | bytes 12713984 | tf_op jit(solution)/shard_map/psum | solution.py:362
  470.5 13.6 %copy-start.29 = (bf16[128,1024]{1,0:T(8,128)(2,1)S(1)}, bf16[128,1024]{1,0:T(8,128)(2,1)}, u32[]{:S(2)}) copy-start(bf16[128,1024]{1,0:T(8,128)(2,1)} %param.28) | copy-start | bytes 786436
  471.4 15.7 %copy-start.7 = (bf16[2,512,1,2,64]{1,4,3,2,0:T(8,128)(2,1)S(1)}, bf16[2,512,1,2,64]{1,4,3,2,0:T(8,128)(2,1)}, u32[]{:S(2)}) copy-start(bf16[2,512,1,2,64]{1,4,3,2,0:T(8,128)(2,1)} %get-tuple-element.743) | copy-start | bytes 786436
  471.4 15.7 %copy-start.53 = (f32[2,1,2,512]{3,2,1,0:T(2,128)S(1)}, f32[2,1,2,512]{3,2,1,0:T(2,128)}, u32[]{:S(2)}) copy-start(f32[2,1,2,512]{3,2,1,0:T(2,128)} %get-tuple-element.684) | copy-start | bytes 24580
  547.5 6.3 all-to-all-start.8
  556.5 9.3 all-to-all-start.9
  559.9 234.9 %reduce-scatter.5.cloned.1.call-start = ((), (), s32[]{:S(2)}) async-start(), calls=%async_computation.13 | async-start | bytes 2359296 | tf_op jit(solution)/shard_map/reduce_scatter | solution.py:349
  569.5 365.2 %all-reduce.7.cloned.1.call-start = ((), (), s32[]{:S(2)}) async-start(), calls=%async_computation.14 | async-start | bytes 1703936 | tf_op jit(solution)/shard_map/psum | solution.py:367
  572.3 222.4 %copy-start.54 = (f32[1024]{0:T(1024)S(1)}, f32[1024]{0:T(1024)}, u32[]{:S(2)}) copy-start(f32[1024]{0:T(1024)} %param.22) | copy-start | bytes 12292
  572.3 222.4 %copy-start.68 = (f32[128]{0:T(128)S(1)}, f32[128]{0:T(128)}, u32[]{:S(2)}) copy-start(f32[128]{0:T(128)} %copy-done.67) | copy-start | bytes 1540
  572.3 223.7 %copy-start.57 = (bf16[1024]{0:T(1024)(128)(2,1)S(1)}, bf16[1024]{0:T(1024)(128)(2,1)}, u32[]{:S(2)}) copy-start(bf16[1024]{0:T(1024)(128)(2,1)} %get-tuple-element.409) | copy-start | bytes 6148
  572.3 236.8 %copy-start.69 = (bf16[128]{0:T(256)(128)(2,1)S(1)}, bf16[128]{0:T(256)(128)(2,1)}, u32[]{:S(2)}) copy-start(bf16[128]{0:T(256)(128)(2,1)} %get-tuple-element.405) | copy-start | bytes 772
  572.3 236.8 %copy-start.71 = (bf16[64]{0:T(256)(128)(2,1)S(1)}, bf16[64]{0:T(256)(128)(2,1)}, u32[]{:S(2)}) copy-start(bf16[64]{0:T(256)(128)(2,1)} %get-tuple-element.407) | copy-start | bytes 388
  572.3 276.8 %copy-start.10 = (f32[128,1024]{1,0:T(8,128)S(1)}, f32[128,1024]{1,0:T(8,128)}, u32[]{:S(2)}) copy-start(f32[128,1024]{1,0:T(8,128)} %copy-done.9) | copy-start | bytes 1572868
  572.3 276.8 %copy-start.15 = (bf16[128,1024]{1,0:T(8,128)(2,1)S(1)}, bf16[128,1024]{1,0:T(8,128)(2,1)}, u32[]{:S(2)}) copy-start(bf16[128,1024]{1,0:T(8,128)(2,1)} %param.35) | copy-start | bytes 786436
  572.3 276.8 %copy-start.42 = (f32[1024]{0:T(1024)S(1)}, f32[1024]{0:T(1024)}, u32[]{:S(2)}) copy-start(f32[1024]{0:T(1024)} %param.29) | copy-start | bytes 12292
  572.4 276.8 %copy-start.62 = (f32[128]{0:T(128)S(1)}, f32[128]{0:T(128)}, u32[]{:S(2)}) copy-start(f32[128]{0:T(128)} %copy-done.60) | copy-start | bytes 1540
  858.4 82.5 %copy-start.1 = (bf16[2,512,1024]{2,1,0:T(8,128)(2,1)S(1)}, bf16[2,512,1024]{2,1,0:T(8,128)(2,1)}, u32[]{:S(2)}) copy-start(bf16[2,512,1024]{2,1,0:T(8,128)(2,1)} %param.33) | copy-start | bytes 6291460
  (62 other events, 390.4 us)
Sparse Core Ops, SparseCore 0:
  103.0 51.5 reduce-scatter.2
  471.5 266.7 all-reduce.8
  741.4 53.3 reduce-scatter.4
  798.4 136.2 all-reduce.6
where the time goes:
time: 957 us; the launch traced here: 948 us
  waiting for transfers between devices  549 us (57%)
  matrix products  100 us (10%)
  local copies, waits for them, and re-layouts  94.1 us (10%)
  other arithmetic  78.5 us (8%)
  blocking collectives  58.7 us (6%)
  starting transfers between devices  51.8 us (5%)
  between operations  15 us (2%)
    all_to_all x4, waiting for transfers between devices, joined_exchange(): lax.all_to_all(blocks, axis, split_axis=0, concat_axis=0, tiled=True)  172 us
    psum x1, waiting for transfers between devices, shards(): lax.psum(router_part.astype(jnp.bfloat16), 'tensor').astype(jnp.float32)  163 us
    psum x1, waiting for transfers between devices, shards(): lax.psum(grad_qkv.astype(jnp.bfloat16), ('dp', 'ctx')).astype(jnp.float32)  73.7 us
    reduce_scatter x1, waiting for transfers between devices, shards(): lax.psum_scatter(matmul_nt(d_qkv, w_qkv).astype(jnp.bfloat16), 'tensor',...  56.3 us
    all_to_all x4, waiting for transfers between devices, from_everyone(): return lax.all_to_all(copies, axis, split_axis=0, concat_axis=0, tiled=True)  45.9 us
    psum x1, blocking collectives, shards(): lax.psum(norm1_sum.astype(jnp.bfloat16), ('dp', 'ctx')).astype(jnp.float32)  37.8 us
    reduce_scatter x1, waiting for transfers between devices, shards(): lax.psum_scatter(matmul(heads_out, w_out).astype(jnp.bfloat16), 'tensor',...  36.8 us
    all_to_all x4, starting transfers between devices, joined_exchange(): lax.all_to_all(blocks, axis, split_axis=0, concat_axis=0, tiled=True)  28 us
  transfers between devices with their start and end apart: 13, of which 13 were waited for; matrix products, arithmetic and copies ran while one was open for 18% of the time, Pallas kernels for 0%

commit v1 on v0

--- a/solution.py
+++ b/solution.py
@@ -1,6 +1,8 @@
 import jax
 import jax.numpy as jnp
 from jax import lax
+from jax.experimental import pallas as pl
+from jax.experimental.pallas import tpu as pltpu
 from jax.sharding import PartitionSpec as P
 
 HEAD_DIM = 64
@@ -9,6 +11,7 @@
 EPS = 1e-06
 THETA = 10000.0
 MASKED = -1e30
+MESH = pl.DeviceIdType.MESH
 
 
 def split_up(x, dim, count):
@@ -104,6 +107,405 @@
     reshaped = buffer.reshape((lax.axis_size("dp"), lax.axis_size("ctx")) + buffer.shape[1:])
     arrived = joined_exchange(reshaped, ("dp", "ctx"), ("dp", "ctx"), (0, 1), (0, 1))
     return arrived.reshape(buffer.shape)
+
+
+def dot_nt(left, right):
+    return lax.dot_general(
+        left, right, (((1,), (1,)), ((), ())), preferred_element_type=jnp.float32
+    )
+
+
+def dot_tn(left, right):
+    return lax.dot_general(
+        left, right, (((0,), (0,)), ((), ())), preferred_element_type=jnp.float32
+    )
+
+
+def x_offset(a):
+    return a + a // 2 - 2 * (a // 3)
+
+
+def back_place(a):
+    return (2 * a) % 3 + 3 * (a // 3)
+
+
+def across(a, b, flip):
+    dp, ctx = lax.axis_index("dp"), lax.axis_index("ctx")
+    x, y = dp % 4, dp // 4
+    return ((y + b) % 2) * 4 + (x + x_offset(a)) % 4, (ctx + flip) % 2
+
+
+def moe_kernel(
+    rows_ref,
+    gate_ref,
+    dy_ref,
+    w_gate_ref,
+    w_up_ref,
+    w_down_ref,
+    d_rows_ref,
+    d_gate_ref,
+    out_part_ref,
+    grad_gu_ref,
+    grad_down_ref,
+    rows_all,
+    gate_all,
+    dy_all,
+    w_gu,
+    w_dn,
+    acc_gu,
+    acc_dn,
+    out_all,
+    din_all,
+    sib,
+    summed,
+    dg_out,
+    dg_in,
+    places,
+    x_buf,
+    y_buf,
+    d_buf,
+    o_buf,
+    i_buf,
+    gs_buf,
+    dgs_buf,
+    load_sem,
+    ag_send,
+    ag_recv,
+    sib_send,
+    sib_recv,
+    rs_send,
+    rs_recv,
+    dg_send,
+    dg_recv,
+    store_sem,
+):
+    tensor = lax.axis_index("tensor")
+    dp, ctx = lax.axis_index("dp"), lax.axis_index("ctx")
+    me = dp * 2 + ctx
+    kinds = (rows_all, gate_all, dy_all)
+
+    def to(a, b, flip):
+        d, c = across(a, b, flip)
+        return (d, c, tensor)
+
+    loads = []
+    for j in range(2):
+        loads.append(
+            pltpu.make_async_copy(w_gate_ref.at[j], w_gu.at[j, :, pl.ds(0, 512)], load_sem.at[3 * j])
+        )
+        loads.append(
+            pltpu.make_async_copy(
+                w_up_ref.at[j], w_gu.at[j, :, pl.ds(512, 512)], load_sem.at[3 * j + 1]
+            )
+        )
+        loads.append(pltpu.make_async_copy(w_down_ref.at[j], w_dn.at[j], load_sem.at[3 * j + 2]))
+    for load in loads:
+        load.start()
+
+    barrier = pltpu.get_barrier_semaphore()
+    for a in range(4):
+        for b in range(2):
+            for flip in range(2):
+                if (a, b, flip) != (0, 0, 0):
+                    pl.semaphore_signal(
+                        barrier, inc=1, device_id=to(a, b, flip), device_id_type=MESH
+                    )
+    pl.semaphore_wait(barrier, 15)
+
+    def own_push(k, a, b, flip):
+        r = 4 * a + 2 * b + flip
+        back = 4 * back_place(a) + 2 * b + flip
+        return pltpu.make_async_remote_copy(
+            src_ref=kinds[k].at[0],
+            dst_ref=kinds[k].at[back],
+            send_sem=ag_send.at[k, r],
+            recv_sem=ag_recv.at[k, back],
+            device_id=to(a, b, flip),
+            device_id_type=MESH,
+        )
+
+    def relay(k, r):
+        return pltpu.make_async_remote_copy(
+            src_ref=kinds[k].at[r],
+            dst_ref=kinds[k].at[r + 1],
+            send_sem=ag_send.at[k, r + 1],
+            recv_sem=ag_recv.at[k, r + 1],
+            device_id=to(0, 0, 1),
+            device_id_type=MESH,
+        )
+
+    def arrival(k, r):
+        return pltpu.make_async_remote_copy(
+            src_ref=kinds[k].at[r],
+            dst_ref=kinds[k].at[r],
+            send_sem=ag_send.at[k, r],
+            recv_sem=ag_recv.at[k, r],
+            device_id=to(0, 0, 1),
+            device_id_type=MESH,
+        )
+
+    rows_all[0] = rows_ref[...]
+    gate_all[0] = gate_ref[...]
+    dy_all[0] = dy_ref[...]
+    for k in range(3):
+        own_push(k, 0, 0, 1).start()
+    for k in range(3):
+        for a in range(4):
+            for b in range(2):
+                if (a, b) != (0, 0):
+                    own_push(k, a, b, 0).start()
+
+    acc_gu[...] = jnp.zeros_like(acc_gu)
+    acc_dn[...] = jnp.zeros_like(acc_dn)
+
+    def arrive(a, first):
+        for b in range(2):
+            if not (first and b == 0):
+                for k in range(3):
+                    arrival(k, 4 * a + 2 * b).wait_recv()
+                    relay(k, 4 * a + 2 * b).start()
+        for b in range(2):
+            for k in range(3):
+                arrival(k, 4 * a + 2 * b + 1).wait_recv()
+
+    def sib_push(ci, r):
+        return pltpu.make_async_remote_copy(
+            src_ref=din_all.at[r],
+            dst_ref=sib.at[ci],
+            send_sem=sib_send.at[ci],
+            recv_sem=sib_recv.at[ci],
+            device_id=to(0, 0, 1),
+            device_id_type=MESH,
+        )
+
+    def rs_push(a, b):
+        back = 2 * back_place(a) + b
+        return pltpu.make_async_remote_copy(
+            src_ref=din_all.at[4 * a + 2 * b],
+            dst_ref=summed.at[back],
+            send_sem=rs_send.at[2 * a + b],
+            recv_sem=rs_recv.at[back],
+            device_id=to(a, b, 0),
+            device_id_type=MESH,
+        )
+
+    def dg_push(a, b, flip):
+        r = 4 * a + 2 * b + flip
+        back = 4 * back_place(a) + 2 * b + flip
+        return pltpu.make_async_remote_copy(
+            src_ref=dg_out.at[r],
+            dst_ref=dg_in.at[back],
+            send_sem=dg_send.at[r],
+            recv_sem=dg_recv.at[back],
+            device_id=to(a, b, flip),
+            device_id_type=MESH,
+        )
+
+    def post(a):
+        for b in range(2):
+            ci, r = 2 * a + b, 4 * a + 2 * b
+            sib_push(ci, r + 1).wait_recv()
+            total = din_all[r].astype(jnp.float32) + sib[ci].astype(jnp.float32)
+            din_all[r] = total.astype(jnp.bfloat16)
+
+            @pl.when(ci > 0)
+            def _():
+                rs_push(a, b).start()
+
+    expert_row = lax.broadcasted_iota(jnp.int32, (32, 128), 0)
+    slot_row = lax.broadcasted_iota(jnp.int32, (64, 128), 0).astype(jnp.float32)
+    before = (
+        lax.broadcasted_iota(jnp.int32, (128, 128), 0)
+        < lax.broadcasted_iota(jnp.int32, (128, 128), 1)
+    ).astype(jnp.float32)
+    before = before.astype(jnp.bfloat16)
+
+    def gather(a, q):
+        r = 4 * a + q
+        gates = gate_all[r]
+        at = pl.ds(pl.multiple_of(q * 64, 64), 64)
+        rows = [
+            jnp.sum(jnp.where(expert_row == 2 * me + j, gates, 0.0), 0, keepdims=True)
+            for j in range(2)
+        ]
+        both = jnp.concatenate(rows + [jnp.zeros((6, 128), jnp.float32)], 0)
+        named = jnp.where(both > 0.0, 1.0, 0.0).astype(jnp.bfloat16)
+        slots = jnp.dot(named, before, preferred_element_type=jnp.float32)
+        hits = [
+            jnp.where((slot_row == slots[j : j + 1]) & (rows[j] > 0.0), 1.0, 0.0) for j in range(2)
+        ]
+        place = jnp.concatenate(hits, 0).astype(jnp.bfloat16)
+        places[q] = place
+        x = jnp.dot(place, rows_all[r], preferred_element_type=jnp.float32).astype(jnp.bfloat16)
+        y = jnp.dot(place, dy_all[r], preferred_element_type=jnp.float32)
+        for j in range(2):
+            gs = jnp.sum(hits[j] * rows[j], 1, keepdims=True)
+            y_j = y[64 * j : 64 * j + 64]
+            x_buf[j, at, :] = x[64 * j : 64 * j + 64]
+            y_buf[j, at, :] = y_j.astype(jnp.bfloat16)
+            d_buf[j, at, :] = (y_j * gs).astype(jnp.bfloat16)
+            gs_buf[j, at, :] = gs
+
+    def expert(j):
+        x = x_buf[j]
+        gu = jnp.dot(x, w_gu[j], preferred_element_type=jnp.float32)
+        g, u = gu[:, :512], gu[:, 512:]
+        s = jax.nn.sigmoid(g)
+        silu = g * s
+        act = (silu * u).astype(jnp.bfloat16)
+        eout = (
+            jnp.dot(act, w_dn[j], preferred_element_type=jnp.float32)
+            .astype(jnp.bfloat16)
+            .astype(jnp.float32)
+        )
+        dgs_buf[j] = jnp.sum(y_buf[j].astype(jnp.float32) * eout, 1, keepdims=True)
+        o_buf[j] = (eout * gs_buf[j]).astype(jnp.bfloat16)
+        d = d_buf[j]
+        d_act = dot_nt(d, w_dn[j])
+        d_g = (d_act * u * s * (1.0 + g * (1.0 - s))).astype(jnp.bfloat16)
+        d_u = (d_act * silu).astype(jnp.bfloat16)
+        d_gu = jnp.concatenate([d_g, d_u], 1)
+        i_buf[j] = dot_nt(d_gu, w_gu[j]).astype(jnp.bfloat16)
+        acc_gu[j] += dot_tn(x, d_gu)
+        acc_dn[j] += dot_tn(act, d)
+
+    def spread(a, q):
+        r = 4 * a + q
+        b, flip = q // 2, q % 2
+        at = pl.ds(pl.multiple_of(q * 64, 64), 64)
+        place = places[q]
+        d, c = across(a, b, flip)
+        o = jnp.concatenate([o_buf[0, at, :], o_buf[1, at, :]], 0)
+        out_all[d * 2 + c] = dot_tn(place, o).astype(jnp.bfloat16)
+        i = jnp.concatenate([i_buf[0, at, :], i_buf[1, at, :]], 0)
+        din_all[r] = dot_tn(place, i).astype(jnp.bfloat16)
+        hits = place.astype(jnp.float32)
+        back = [
+            jnp.sum(hits[64 * j : 64 * j + 64] * dgs_buf[j, at, :], 0, keepdims=True)
+            for j in range(2)
+        ]
+        dg_out[r] = jnp.concatenate(back + [jnp.zeros((6, 128), jnp.float32)], 0)
+
+        @pl.when(r > 0)
+        def _():
+            dg_push(a, b, flip).start()
+
+    arrive(0, True)
+    for load in loads:
+        load.wait()
+
+    def step(a, carry):
+        lax.fori_loop(0, 4, lambda q, c: (gather(a, q), c)[1], 0)
+        lax.fori_loop(0, 2, lambda j, c: (expert(j), c)[1], 0)
+        lax.fori_loop(0, 4, lambda q, c: (spread(a, q), c)[1], 0)
+        for b in range(2):
+            sib_push(2 * a + b, 4 * a + 2 * b + 1).start()
+
+        @pl.when(a > 0)
+        def _():
+            post(a - 1)
+
+        @pl.when(a < 3)
+        def _():
+            arrive(a + 1, False)
+
+        return carry
+
+    lax.fori_loop(0, 4, step, 0)
+    post(3)
+    for k in range(3):
+        for r in range(1, 16):
+            arrival(k, r).wait_send()
+    stores = []
+    for j in range(2):
+        for h in range(8):
+            rows_all[8 * j + h] = acc_gu[j, 128 * h : 128 * h + 128, :].astype(jnp.bfloat16)
+        for h in range(4):
+            dy_all[4 * j + h] = acc_dn[j, 128 * h : 128 * h + 128, :].astype(jnp.bfloat16)
+    stores.append(pltpu.make_async_copy(rows_all, grad_gu_ref, store_sem.at[0]))
+    stores.append(pltpu.make_async_copy(dy_all.at[pl.ds(0, 8)], grad_down_ref, store_sem.at[1]))
+    stores.append(pltpu.make_async_copy(out_all, out_part_ref, store_sem.at[2]))
+    for store in stores:
+        store.start()
+
+    for r in range(1, 16):
+        a, b, flip = r // 4, (r // 2) % 2, r % 2
+        dg_push(a, b, flip).wait()
+    dg_in[0] = dg_out[0]
+    d_gate = jnp.zeros((32, 128), jnp.float32)
+    for r in range(16):
+        d, c = across(r // 4, (r // 2) % 2, r % 2)
+        got = dg_in[r]
+        for j in range(2):
+            d_gate = jnp.where(expert_row == (d * 2 + c) * 2 + j, got[j : j + 1], d_gate)
+    d_gate_ref[...] = d_gate
+    total = din_all[0].astype(jnp.float32)
+    for ci in range(8):
+        sib_push(ci, 2 * ci + 1).wait_send()
+        if ci > 0:
+            rs_push(ci // 2, ci % 2).wait()
+    for ci in range(1, 8):
+        total = total + summed[ci].astype(jnp.float32)
+    d_rows_ref[...] = total
+    for store in stores:
+        store.wait()
+
+
+def moe(rows, gates, dy, w_gate, w_up, w_down):
+    bf, f32 = jnp.bfloat16, jnp.float32
+    vmem, hbm = pl.BlockSpec(memory_space=pltpu.VMEM), pl.BlockSpec(memory_space=pl.ANY)
+    sem = pltpu.SemaphoreType.DMA
+    return pl.pallas_call(
+        moe_kernel,
+        out_shape=(
+            jax.ShapeDtypeStruct((128, 1024), f32),
+            jax.ShapeDtypeStruct((32, 128), f32),
+            jax.ShapeDtypeStruct((16, 128, 1024), bf),
+            jax.ShapeDtypeStruct((16, 128, 1024), bf),
+            jax.ShapeDtypeStruct((8, 128, 1024), bf),
+        ),
+        in_specs=[vmem] * 3 + [hbm] * 3,
+        out_specs=(vmem, vmem, hbm, hbm, hbm),
+        scratch_shapes=[
+            pltpu.VMEM((16, 128, 1024), bf),
+            pltpu.VMEM((16, 32, 128), f32),
+            pltpu.VMEM((16, 128, 1024), bf),
+            pltpu.VMEM((2, 1024, 1024), bf),
+            pltpu.VMEM((2, 512, 1024), bf),
+            pltpu.VMEM((2, 1024, 1024), f32),
+            pltpu.VMEM((2, 512, 1024), f32),
+            pltpu.VMEM((16, 128, 1024), bf),
+            pltpu.VMEM((16, 128, 1024), bf),
+            pltpu.VMEM((8, 128, 1024), bf),
+            pltpu.VMEM((8, 128, 1024), bf),
+            pltpu.VMEM((16, 8, 128), f32),
+            pltpu.VMEM((16, 8, 128), f32),
+            pltpu.VMEM((4, 128, 128), bf),
+            pltpu.VMEM((2, 256, 1024), bf),
+            pltpu.VMEM((2, 256, 1024), bf),
+            pltpu.VMEM((2, 256, 1024), bf),
+            pltpu.VMEM((2, 256, 1024), bf),
+            pltpu.VMEM((2, 256, 1024), bf),
+            pltpu.VMEM((2, 256, 1), f32),
+            pltpu.VMEM((2, 256, 1), f32),
+            sem((6,)),
+            sem((3, 16)),
+            sem((3, 16)),
+            sem((8,)),
+            sem((8,)),
+            sem((8,)),
+            sem((8,)),
+            sem((16,)),
+            sem((16,)),
+            sem((3,)),
+        ],
+        compiler_params=pltpu.CompilerParams(
+            collective_id=1, has_side_effects=True, vmem_limit_bytes=60 << 20
+        ),
+        cost_estimate=pl.CostEstimate(
+            flops=20_000_000_000, bytes_accessed=30_000_000, transcendentals=2_000_000
+        ),
+    )(rows, gates, dy, w_gate, w_up, w_down)
 
 
 def shards(
@@ -219,38 +621,19 @@
     normed_two = (res_hat * norm2_gain).astype(jnp.bfloat16)
     logits = matmul(normed_two, router)
     expert_ids = jnp.arange(n_experts, dtype=jnp.int32)
-    route_hot = routes[:, :, None] == expert_ids[None, None, :]
-    chosen = jnp.sum(jnp.where(route_hot, logits[:, None, :], 0.0), -1)
-    top_logit = jnp.max(chosen, -1, keepdims=True)
-    gate_exp = jnp.exp(chosen - top_logit)
-    gate_weights = gate_exp / jnp.sum(gate_exp, -1, keepdims=True)
-    flat_ids = routes.reshape(-1)
-    flat_hot = route_hot.reshape(-1, n_experts).astype(jnp.int32)
-    earlier = jnp.cumsum(flat_hot, 0) - flat_hot
-    slot_index = jnp.sum(earlier * flat_hot, 1)
-    targets = flat_ids * capacity + slot_index
-    source_rows = jnp.arange(tok_rows * top_k, dtype=jnp.int32) // top_k
-    send_rows = (
-        jnp.zeros((n_experts * capacity, model_dim), jnp.bfloat16)
-        .at[targets]
-        .set(normed_two[source_rows])
-    )
-    arrived = route_rows(send_rows.reshape(n_groups, exp_dev, capacity, model_dim))
-    gate_h = jnp.einsum("gjcd,jdf->gjcf", arrived, w_gate, preferred_element_type=jnp.float32)
-    up_h = jnp.einsum("gjcd,jdf->gjcf", arrived, w_up, preferred_element_type=jnp.float32)
-    sig_gate = jax.nn.sigmoid(gate_h)
-    silu_gate = gate_h * sig_gate
-    activation = (silu_gate * up_h).astype(jnp.bfloat16)
-    expert_out = jnp.einsum(
-        "gjcf,jfd->gjcd", activation, w_down, preferred_element_type=jnp.float32
-    ).astype(jnp.bfloat16)
-    returned = route_rows(expert_out).reshape(n_experts * capacity, model_dim)
-    picked = returned[targets].reshape(tok_rows, top_k, model_dim).astype(jnp.float32)
-    output = (residual + jnp.sum(gate_weights[:, :, None] * picked, 1)).astype(jnp.bfloat16)
+    named = jnp.any(routes[:, :, None] == expert_ids[None, None, :], 1)
+    top_logit = jnp.max(jnp.where(named, logits, MASKED), -1, keepdims=True)
+    gate_exp = jnp.where(named, jnp.exp(jnp.where(named, logits - top_logit, 0.0)), 0.0)
+    gates = (gate_exp / jnp.sum(gate_exp, -1, keepdims=True)).T
     grad_out = cotangent.astype(jnp.float32)
-    d_gate = jnp.sum(picked * grad_out[:, None, :], -1)
-    d_choice = gate_weights * (d_gate - jnp.sum(gate_weights * d_gate, -1, keepdims=True))
-    d_logits = jnp.sum(jnp.where(route_hot, d_choice[:, :, None], 0.0), 1)
+    d_rows, d_gate, out_part, grad_gu, grad_down = moe(
+        normed_two, gates, cotangent, w_gate, w_up, w_down
+    )
+    mixed = lax.psum_scatter(
+        out_part.reshape(-1, model_dim), ("dp", "ctx"), scatter_dimension=0, tiled=True
+    )
+    output = (residual + mixed.astype(jnp.float32)).astype(jnp.bfloat16)
+    d_logits = (gates * (d_gate - jnp.sum(gates * d_gate, 0, keepdims=True))).T
     router_part = lax.dot_general(
         normed_two.astype(jnp.float32),
         d_logits,
@@ -258,29 +641,10 @@
         precision=lax.Precision.HIGHEST,
     )
     d_normed = jnp.dot(d_logits, router.astype(jnp.float32).T, precision=lax.Precision.HIGHEST)
-    d_picked = (
-        (gate_weights[:, :, None] * grad_out[:, None, :])
-        .astype(jnp.bfloat16)
-        .reshape(-1, model_dim)
-    )
-    d_send = jnp.zeros((n_experts * capacity, model_dim), jnp.bfloat16).at[targets].set(d_picked)
-    d_arrived = route_rows(d_send.reshape(n_groups, exp_dev, capacity, model_dim))
-    d_act = jnp.einsum("gjcd,jfd->gjcf", d_arrived, w_down, preferred_element_type=jnp.float32)
-    grad_down = jnp.einsum(
-        "gjcf,gjcd->jfd", activation, d_arrived, preferred_element_type=jnp.float32
-    )
-    d_gate_h = (d_act * up_h * sig_gate * (1.0 + gate_h * (1.0 - sig_gate))).astype(jnp.bfloat16)
-    d_up_h = (d_act * silu_gate).astype(jnp.bfloat16)
-    grad_gate = jnp.einsum("gjcd,gjcf->jdf", arrived, d_gate_h, preferred_element_type=jnp.float32)
-    grad_up = jnp.einsum("gjcd,gjcf->jdf", arrived, d_up_h, preferred_element_type=jnp.float32)
-    d_inputs = jnp.einsum("gjcf,jdf->gjcd", d_gate_h, w_gate, preferred_element_type=jnp.float32)
-    d_inputs = (
-        d_inputs + jnp.einsum("gjcf,jdf->gjcd", d_up_h, w_up, preferred_element_type=jnp.float32)
-    ).astype(jnp.bfloat16)
-    d_back = route_rows(d_inputs).reshape(n_experts * capacity, model_dim)
-    d_normed = d_normed + jnp.sum(
-        d_back[targets].reshape(tok_rows, top_k, model_dim).astype(jnp.float32), 1
-    )
+    d_normed = d_normed + d_rows
+    grad_gu = grad_gu.reshape(2, 1024, 1024)
+    grad_gate, grad_up = grad_gu[:, :, :512], grad_gu[:, :, 512:]
+    grad_down = grad_down.reshape(2, 512, 1024)
     norm2_part = jnp.sum(d_normed * res_hat, 0)
     d_scaled_two = d_normed * norm2_gain
     d_resid = grad_out + inv_two * (

time: 957 us -> 860 us (0.90)
  Pallas kernels: 0 us -> 108 us
  waiting for transfers between devices: 549 us -> 477 us
  matrix products: 100 us -> 53.2 us
  local copies, waits for them, and re-layouts: 94.1 us -> 48.2 us
  starting transfers between devices: 51.8 us -> 33.3 us
  other arithmetic: 78.5 us -> 65.2 us
    all_to_all x4 -> x0, waiting for transfers between devices: 172 us -> none  [joined_exchange(): lax.all_to_all(blocks, axis, split_axis=0, concat_axis=0, tiled=True)]
    pallas_call x0 -> x1, Pallas kernels: none -> 108 us  [moe(): pl.pallas_call(moe_kernel, out_shape=(jax.ShapeDtypeStruct((128, 1024), f...]
    psum x1, waiting for transfers between devices: 73.7 us -> 130 us  [shards(): lax.psum(grad_qkv.astype(jnp.bfloat16), ('dp', 'ctx')).astype(jnp.float32)]
    dot_general x9 -> x0, matrix products: 38.4 us -> none  [the longest x1 6.65 us: shards(): jnp.einsum('gjcf,gjcd->jfd', activation, d_arrived, preferred_element_typ...]
    all_to_all x4 -> x0, starting transfers between devices: 28 us -> none  [joined_exchange(): lax.all_to_all(blocks, axis, split_axis=0, concat_axis=0, tiled=True)]
    reduce_scatter x0 -> x1, waiting for transfers between devices: none -> 27.7 us  [shards(): lax.psum_scatter(out_part.reshape(-1, model_dim), ('dp', 'ctx'), scatter_...]
    scatter x1 -> x0, local copies, waits for them, and re-layouts: 17.8 us -> none  [shards(): send_rows = jnp.zeros((n_experts * capacity, model_dim), jnp.bfloat16).at...]
    gather x2 -> x0, local copies, waits for them, and re-layouts: 17.5 us -> none  [the longest x1 8.78 us: shards(): d_back[targets].reshape(tok_rows, top_k, model_dim).astype(jnp.float32)]
  transfers between devices with their start and end apart: 13 -> 11, of which waited for: 13 -> 9; matrix products, arithmetic and copies ran while one was open for 18% -> 13% of each run, Pallas kernels for 0% -> 0%
where the time goes in v1:
time: 860 us; the launch traced here: 851 us
  waiting for transfers between devices  477 us (55%)
  Pallas kernels  108 us (13%)
  other arithmetic  65.2 us (8%)
  matrix products  53.2 us (6%)
  blocking collectives  51.2 us (6%)
  local copies, waits for them, and re-layouts  48.2 us (6%)
  starting transfers between devices  33.3 us (4%)
  between operations  14.9 us (2%)
    psum x1, waiting for transfers between devices, shards(): lax.psum(router_part.astype(jnp.bfloat16), 'tensor').astype(jnp.float32)  160 us
    psum x1, waiting for transfers between devices, shards(): lax.psum(grad_qkv.astype(jnp.bfloat16), ('dp', 'ctx')).astype(jnp.float32)  130 us
    pallas_call x1, Pallas kernels, moe(): pl.pallas_call(moe_kernel, out_shape=(jax.ShapeDtypeStruct((128, 1024), f...  108 us
    reduce_scatter x1, waiting for transfers between devices, shards(): lax.psum_scatter(matmul_nt(d_qkv, w_qkv).astype(jnp.bfloat16), 'tensor',...  56.3 us
    reduce_scatter x1, waiting for transfers between devices, shards(): lax.psum_scatter(matmul(heads_out, w_out).astype(jnp.bfloat16), 'tensor',...  51.4 us
    all_to_all x5, waiting for transfers between devices, from_everyone(): return lax.all_to_all(copies, axis, split_axis=0, concat_axis=0, tiled=True)  50.8 us
    psum x1, blocking collectives, shards(): lax.psum(norm1_sum.astype(jnp.bfloat16), ('dp', 'ctx')).astype(jnp.float32)  38.1 us
    reduce_scatter x1, waiting for transfers between devices, shards(): lax.psum_scatter(out_part.reshape(-1, model_dim), ('dp', 'ctx'), scatter_...  27.7 us
  transfers between devices with their start and end apart: 11, of which 9 were waited for; matrix products, arithmetic and copies ran while one was open for 13% of the time, Pallas kernels for 0%

profile of v1, /device:TPU:1, one launch (start us, length us, event | category | flops | bytes accessed | tf_op | source)
XLA Modules:
  0.0 850.7 jit_solution(8779399829275849720)
XLA Ops:
  11.1 6.9 all-to-all-start
  21.0 23.0 %all-to-all-done = bf16[8,128,1024]{2,1,0:T(8,128)(2,1)S(1)} async-done(((bf16[8,128,1024]{2,1,0:T(8,128)(2,1)}), bf16[8,128,1024]{2,1,0:T(8,128)(2,1)S(1)}, u32[]{:S(2)}, u32[]{:S(2)}) %all-to-all-start) | async-done | bytes 2097184 | tf_op jit(solution)/shard_map/all_to_all | solution.py:41
  47.4 4.0 all-to-all-start.1
  52.1 4.5 all-to-all-done.1
  63.2 7.2 all-to-all-start.2
  74.7 19.5 %while.28 = (s32[]{:T(128)}, bf16[2,512,128]{2,1,0:T(8,128)(2,1)}, f32[2,1,2,512]{3,2,1,0:T(2,128)}, s32[2,512]{1,0:T(2,128)S(1)}, s32[2048]{0:T(1024)S(1)}, /*i...) while((s32[]{:T(128)}, bf16[2,512,128]{2,1,0:T(8,128)(2,1)}, ...), condition=%wide.region_7.8_spmd.clone, body=%wide.region_4.7_spmd.clone.sunk | while | flops 565181440 | bytes 30724220 | solution.py:613
  90.2 2.7 fusion.143
  94.3 3.2 convolution_convert_fusion.1
  97.6 51.4 %reduce-scatter.4.cloned.1.call-done = bf16[128,1024]{1,0:T(8,128)(2,1)} async-done(((bf16[1024,1024]{1,0:T(8,128)(2,1)}), bf16[128,1024]{1,0:T(8,128)(2,1)}) %reduce-scatter.4.cloned.1.call-update) | async-done | bytes 262160 | tf_op jit(solution)/shard_map/reduce_scatter | solution.py:615
  152.1 107.7 %shard_map.263 = (f32[128,1024]{1,0:T(8,128)}, f32[32,128]{1,0:T(8,128)}, bf16[16,128,1024]{2,1,0:T(8,128)(2,1)}, bf16[16,128,1024]{2,1,0:T(8,128)(2,1)}, bf16[8,128,1024]{2,1,0:T(8,128)(2,1)}) custom-call(bf16[128,1024]{1,0:T(8,128)(2,1)} %copy-done.13, f32[32,128]{1,0:T(8,128)} %fusion.93.gate_ref, bf16[128,1024]{1,0:T(8,128)(2,1)} %dy_ref.1, ...), custom_call_target="tpu_custom_call" | custom-call | flops 20000000000 | bytes 30000000 | tf_op jit(solution)/shard_map/pallas_call | solution.py:458
  264.7 3.6 all-to-all-start.3
  270.2 4.5 fusion.102
  274.7 18.5 %all-to-all-done.3 = bf16[8,128,1024]{2,1,0:T(8,128)(2,1)S(1)} async-done(((bf16[8,128,1024]{2,1,0:T(8,128)(2,1)}), bf16[8,128,1024]{2,1,0:T(8,128)(2,1)S(1)}, u32[]{:S(2)}, u32[]{:S(2)}) %all-to-all-start.3) | async-done | bytes 2097184 | tf_op jit(solution)/shard_map/all_to_all | solution.py:41
  298.5 45.2 %while.29 = (s32[]{:T(128)}, f32[2048,1,64]{0,2,1:T(8,128)S(1)}, f32[2048,1,64]{0,2,1:T(8,128)}, f32[2,512,128]{1,0,2:T(2,128)}, bf16[2,512,1,2,64]{1,4,3,2,0:T(...) while((s32[]{:T(128)}, f32[2048,1,64]{0,2,1:T(8,128)S(1)}, ...), condition=%wide.region_18.19_spmd.clone, body=%wide.region_16.18_spmd.clone.sunk | while | flops 1377500160 | bytes 78168360 | solution.py:688
  302.7 3.5 fusion.157
  306.2 4.0 fusion.154
  315.4 5.7 dynamic_update_slice.21
  325.3 3.4 fusion.157
  328.8 4.0 fusion.154
  338.0 5.7 dynamic_update_slice.21
  353.3 7.5 all-to-all-start.4
  370.5 4.0 all-to-all-start.5
  376.1 4.8 all-to-all-done.5
  386.1 3.4 convolution_convert_fusion
  392.4 3.2 convolution_convert_fusion.2
  395.7 160.3 %all-reduce.9.cloned.1.call-done = (bf16[1024,32]{0,1:T(8,128)(2,1)}, bf16[2,1024,512]{2,1,0:T(8,128)(2,1)}, bf16[2,1024,512]{2,1,0:T(8,128)(2,1)}, bf16[2,512,1024]{2,1,0:T(8,128)(2,1)}) async-done(((bf16[1024,32]{0,1:T(8,128)(2,1)}, bf16[2,1024,512]{2,1,0:T(8,128)(2,1)}, bf16[2,1024,512]{2,1,0:T(8,128)(2,1)}, bf16[2,512,1024]{2,1,0:T(8,128)(2,1)}), (bf16[1024,32]{0,1:T(8,128)(2,1)}, ...) | async-done | bytes 6357008 | tf_op jit(solution)/shard_map/psum | solution.py:726
  556.0 56.3 %reduce-scatter.8.cloned.1.call-done = bf16[128,1024]{1,0:T(8,128)(2,1)} async-done(((bf16[1024,1024]{1,0:T(8,128)(2,1)}), bf16[128,1024]{1,0:T(8,128)(2,1)}) %reduce-scatter.8.cloned.1.call-update) | async-done | bytes 262160 | tf_op jit(solution)/shard_map/reduce_scatter | solution.py:713
  613.6 13.1 %all-reduce.2 = (bf16[1024]{0:T(1024)(128)(2,1)S(1)}, bf16[1024]{0:T(1024)(128)(2,1)S(1)}) all-reduce(bf16[1024]{0:T(1024)(128)(2,1)S(1)} %get-tuple-element.419, bf16[1024]{0:T(1024)(128)(2,1)S(1)} %copy-done.43), channel_id=1, replica_groups=mesh['dp'=8,'ctx'=2,'tensor'=8] {'tensor'}, use_global_device_ids=true, to_apply=%region_26.27 | all-reduce | flops 2048 | bytes 8192 | tf_op jit(solution)/shard_map/psum | solution.py:727
  626.7 38.1 %all-reduce = (bf16[1024]{0:T(1024)(128)(2,1)S(1)}, bf16[128]{0:T(256)(128)(2,1)S(1)}, bf16[64]{0:T(256)(128)(2,1)S(1)}, bf16[1024]{0:T(1024)(128)(2,1)S(1)}) all-reduce(bf16[1024]{0:T(1024)(128)(2,1)S(1)} %get-tuple-element.470, bf16[128]{0:T(256)(128)(2,1)S(1)} %copy-done.51, ...), channel_id=1, replica_groups=mesh['dp'=8,'ctx'=2,'tensor'=8] {'dp','ctx'}, use_global_device_ids=true, to_apply=%region_27.28 | all-reduce | flops 2240 | bytes 8960 | tf_op jit(solution)/shard_map/psum | solution.py:736
  667.0 27.7 %reduce-scatter.6.cloned.1.call-done = bf16[128,1024]{1,0:T(8,128)(2,1)} async-done(((bf16[2048,1024]{1,0:T(8,128)(2,1)}), bf16[128,1024]{1,0:T(8,128)(2,1)}) %reduce-scatter.6.cloned.1.call-update) | async-done | bytes 262160 | tf_op jit(solution)/shard_map/reduce_scatter | solution.py:632
  696.9 4.2 convert_element_type.179
  706.2 129.5 %all-reduce.7.cloned.1.call-done = (bf16[1024,256]{1,0:T(8,128)(2,1)}, bf16[128,1024]{1,0:T(8,128)(2,1)}, bf16[1024,32]{0,1:T(8,128)(2,1)}) async-done(((bf16[1024,256]{1,0:T(8,128)(2,1)}, bf16[128,1024]{1,0:T(8,128)(2,1)}, bf16[1024,32]{0,1:T(8,128)(2,1)}), (bf16[1024,256]{1,0:T(8,128)(2,1)}, bf16[128,1024]{1,0:T(8,128)(2,1)}, bf16[1024,32]{0,1:T(8,128)(2,1)})) %all-reduce.7.cloned.1.call-update) | async-done | bytes 851984 | tf_op jit(solution)/shard_map/psum | solution.py:731
  (251 shorter events, 119.7 us)
Async XLA Ops:
  7.2 87.1 %copy-start = (bf16[128,1024]{1,0:T(8,128)(2,1)S(1)}, bf16[128,1024]{1,0:T(8,128)(2,1)}, u32[]{:S(2)}) copy-start(bf16[128,1024]{1,0:T(8,128)(2,1)} %param.28) | copy-start | bytes 786436
  11.1 32.9 %all-to-all-start = ((bf16[8,128,1024]{2,1,0:T(8,128)(2,1)}), bf16[8,128,1024]{2,1,0:T(8,128)(2,1)S(1)}, u32[]{:S(2)}, u32[]{:S(2)}) async-start(bf16[8,128,1024]{2,1,0:T(8,128)(2,1)} %broadcast_in_dim.54), calls=%async_computation | async-start | bytes 4194304 | tf_op jit(solution)/shard_map/all_to_all | solution.py:41
  47.4 9.2 %all-to-all-start.1 = ((f32[8,1,2048]{2,1,0:T(1,128)}), f32[8,1,2048]{2,1,0:T(1,128)}, u32[]{:S(2)}, u32[]{:S(2)}) async-start(f32[8,1,2048]{2,1,0:T(1,128)} %broadcast_in_dim.61), calls=%async_computation.1 | async-start | bytes 131072 | tf_op jit(solution)/shard_map/all_to_all | solution.py:41
  63.2 9.6 %all-to-all-start.2 = ((bf16[2,1024,128]{1,2,0:T(8,128)(2,1)}), bf16[2,1024,128]{1,2,0:T(8,128)(2,1)}, u32[]{:S(2)}, u32[]{:S(2)}) async-start(bf16[2,1024,128]{1,2,0:T(8,128)(2,1)} %broadcast_in_dim.62), calls=%async_computation.2 | async-start | bytes 1048576 | tf_op jit(solution)/shard_map/all_to_all | solution.py:41
  70.4 78.6 %reduce-scatter.4.cloned.1.call-start = ((), (), s32[]{:S(2)}) async-start(), calls=%async_computation.9 | async-start | bytes 2359296 | tf_op jit(solution)/shard_map/reduce_scatter | solution.py:615
  94.3 165.5 %copy-start.5 = (bf16[2048,1,64]{0,2,1:T(8,128)(2,1)}, bf16[2048,1,64]{0,2,1:T(8,128)(2,1)S(1)}, u32[]{:S(2)}) copy-start(bf16[2048,1,64]{0,2,1:T(8,128)(2,1)S(1)} %get-tuple-element.745) | copy-start | bytes 786436
  94.3 165.5 %copy-start.7 = (bf16[2,512,1,2,64]{1,4,3,2,0:T(8,128)(2,1)}, bf16[2,512,1,2,64]{1,4,3,2,0:T(8,128)(2,1)S(1)}, u32[]{:S(2)}) copy-start(bf16[2,512,1,2,64]{1,4,3,2,0:T(8,128)(2,1)S(1)} %get-tuple-element.746) | copy-start | bytes 786436
  94.3 54.7 %copy-start.2 = (bf16[128,1024]{1,0:T(8,128)(2,1)S(1)}, bf16[128,1024]{1,0:T(8,128)(2,1)}, u32[]{:S(2)}) copy-start(bf16[128,1024]{1,0:T(8,128)(2,1)} %param.20) | copy-start | bytes 786436
  94.3 55.9 %copy-start.35 = (f32[1024]{0:T(1024)S(1)}, f32[1024]{0:T(1024)}, u32[]{:S(2)}) copy-start(f32[1024]{0:T(1024)} %param.29) | copy-start | bytes 12292
  94.3 56.9 %copy-start.29 = (bf16[1024,32]{0,1:T(8,128)(2,1)S(1)}, bf16[1024,32]{0,1:T(8,128)(2,1)}, u32[]{:S(2)}) copy-start(bf16[1024,32]{0,1:T(8,128)(2,1)} %param.30) | copy-start | bytes 196612
  150.1 112.7 %copy-start.44 = (f32[128]{0:T(128)}, f32[128]{0:T(128)S(1)}, u32[]{:S(2)}) copy-start(f32[128]{0:T(128)S(1)} %add_rsqrt_fusion) | copy-start | bytes 1540
  152.1 107.7 %copy-start.26 = (f32[32,128]{1,0:T(8,128)S(1)}, f32[32,128]{1,0:T(8,128)}, u32[]{:S(2)}) copy-start(f32[32,128]{1,0:T(8,128)} %fusion.93.gate_ref) | copy-start | bytes 49156
  152.1 108.4 %copy-start.9 = (bf16[128,1024]{1,0:T(8,128)(2,1)S(1)}, bf16[128,1024]{1,0:T(8,128)(2,1)}, u32[]{:S(2)}) copy-start(bf16[128,1024]{1,0:T(8,128)(2,1)} %reduce-scatter.4.cloned.1.call-done) | copy-start | bytes 786436
  152.1 110.7 %copy-start.21 = (bf16[128,1024]{1,0:T(8,128)(2,1)S(1)}, bf16[128,1024]{1,0:T(8,128)(2,1)}, u32[]{:S(2)}) copy-start(bf16[128,1024]{1,0:T(8,128)(2,1)} %dy_ref.1) | copy-start | bytes 786436
  264.7 28.5 %all-to-all-start.3 = ((bf16[8,128,1024]{2,1,0:T(8,128)(2,1)}), bf16[8,128,1024]{2,1,0:T(8,128)(2,1)S(1)}, u32[]{:S(2)}, u32[]{:S(2)}) async-start(bf16[8,128,1024]{2,1,0:T(8,128)(2,1)} %broadcast_in_dim.67), calls=%async_computation.5 | async-start | bytes 4194304 | tf_op jit(solution)/shard_map/all_to_all | solution.py:41
  268.3 287.7 %all-reduce.9.cloned.1.call-start = ((), (), s32[]{:S(2)}) async-start(), calls=%async_computation.13 | async-start | bytes 12713984 | tf_op jit(solution)/shard_map/psum | solution.py:726
  353.3 9.5 %all-to-all-start.4 = ((bf16[2,1024,128]{1,2,0:T(8,128)(2,1)}), bf16[2,1024,128]{1,2,0:T(8,128)(2,1)}, u32[]{:S(2)}, u32[]{:S(2)}) async-start(bf16[2,1024,128]{1,2,0:T(8,128)(2,1)} %copy.105), calls=%async_computation.6 | async-start | bytes 1048576 | tf_op jit(solution)/shard_map/all_to_all | solution.py:65
  370.5 10.5 %all-to-all-start.5 = ((f32[8,1,2048]{2,1,0:T(1,128)}), f32[8,1,2048]{2,1,0:T(1,128)}, u32[]{:S(2)}, u32[]{:S(2)}) async-start(f32[8,1,2048]{2,1,0:T(1,128)} %broadcast_in_dim.68), calls=%async_computation.7 | async-start | bytes 131072 | tf_op jit(solution)/shard_map/all_to_all | solution.py:41
  374.5 237.8 %reduce-scatter.8.cloned.1.call-start = ((), (), s32[]{:S(2)}) async-start(), calls=%async_computation.11 | async-start | bytes 2359296 | tf_op jit(solution)/shard_map/reduce_scatter | solution.py:713
  389.6 305.1 %reduce-scatter.6.cloned.1.call-start = ((), (), s32[]{:S(2)}) async-start(), calls=%async_computation.10 | async-start | bytes 4456448 | tf_op jit(solution)/shard_map/reduce_scatter | solution.py:632
  390.1 445.6 %all-reduce.7.cloned.1.call-start = ((), (), s32[]{:S(2)}) async-start(), calls=%async_computation.12 | async-start | bytes 1703936 | tf_op jit(solution)/shard_map/psum | solution.py:731
  392.3 220.0 %copy-start.42 = (f32[1024]{0:T(1024)S(1)}, f32[1024]{0:T(1024)}, u32[]{:S(2)}) copy-start(f32[1024]{0:T(1024)} %param.22) | copy-start | bytes 12292
  392.3 220.0 %copy-start.49 = (f32[128]{0:T(128)S(1)}, f32[128]{0:T(128)}, u32[]{:S(2)}) copy-start(f32[128]{0:T(128)} %copy-done.48) | copy-start | bytes 1540
  392.3 221.2 %copy-start.43 = (bf16[1024]{0:T(1024)(128)(2,1)S(1)}, bf16[1024]{0:T(1024)(128)(2,1)}, u32[]{:S(2)}) copy-start(bf16[1024]{0:T(1024)(128)(2,1)} %get-tuple-element.417) | copy-start | bytes 6148
  392.4 234.3 %copy-start.51 = (bf16[128]{0:T(256)(128)(2,1)S(1)}, bf16[128]{0:T(256)(128)(2,1)}, u32[]{:S(2)}) copy-start(bf16[128]{0:T(256)(128)(2,1)} %get-tuple-element.413) | copy-start | bytes 772
  392.4 234.3 %copy-start.52 = (bf16[64]{0:T(256)(128)(2,1)S(1)}, bf16[64]{0:T(256)(128)(2,1)}, u32[]{:S(2)}) copy-start(bf16[64]{0:T(256)(128)(2,1)} %get-tuple-element.415) | copy-start | bytes 388
  392.4 302.3 %copy-start.10 = (bf16[128,1024]{1,0:T(8,128)(2,1)S(1)}, bf16[128,1024]{1,0:T(8,128)(2,1)}, u32[]{:S(2)}) copy-start(bf16[128,1024]{1,0:T(8,128)(2,1)} %reduce-scatter.4.cloned.1.call-done) | copy-start | bytes 786436
  392.4 302.3 %copy-start.12 = (f32[128,1024]{1,0:T(8,128)S(1)}, f32[128,1024]{1,0:T(8,128)}, u32[]{:S(2)}) copy-start(f32[128,1024]{1,0:T(8,128)} %copy-done.11) | copy-start | bytes 1572868
  392.4 302.3 %copy-start.22 = (bf16[128,1024]{1,0:T(8,128)(2,1)S(1)}, bf16[128,1024]{1,0:T(8,128)(2,1)}, u32[]{:S(2)}) copy-start(bf16[128,1024]{1,0:T(8,128)(2,1)} %dy_ref.1) | copy-start | bytes 786436
  392.4 302.2 %copy-start.36 = (f32[1024]{0:T(1024)S(1)}, f32[1024]{0:T(1024)}, u32[]{:S(2)}) copy-start(f32[1024]{0:T(1024)} %param.29) | copy-start | bytes 12292
  392.4 302.2 %copy-start.45 = (f32[128]{0:T(128)S(1)}, f32[128]{0:T(128)}, u32[]{:S(2)}) copy-start(f32[128]{0:T(128)} %copy-done.44) | copy-start | bytes 1540
  703.7 140.1 %copy-start.1 = (bf16[128,1024]{1,0:T(8,128)(2,1)S(1)}, bf16[128,1024]{1,0:T(8,128)(2,1)}, u32[]{:S(2)}) copy-start(bf16[128,1024]{1,0:T(8,128)(2,1)} %param.28) | copy-start | bytes 786436
  (37 other events, 383.3 us)
Sparse Core Ops, SparseCore 0:
  97.6 51.3 reduce-scatter.3
  274.8 281.0 all-reduce.8
  559.0 53.3 reduce-scatter.7
  616.2 78.3 reduce-scatter.5
  698.5 137.1 all-reduce.6

commit v2 on v1

v2 whole, which is shorter than its diff:
```python
import jax
import jax.numpy as jnp
import numpy as np
from jax import lax
from jax.experimental import pallas as pl
from jax.experimental.pallas import tpu as pltpu
from jax.sharding import PartitionSpec as P

EPS = 1e-06
THETA = 10000.0
MASKED = -1e30
MESH = pl.DeviceIdType.MESH


def rope_constants(length, half_dim):
    inverse = THETA ** (-(np.arange(half_dim, dtype=np.float64) * 2.0 / (2 * half_dim)))
    angles = inverse[:, None] * np.arange(length, dtype=np.float64)[None, :]
    table = np.stack([np.cos(angles), np.sin(angles)]).astype(np.float32)
    return np.ascontiguousarray(table.reshape(2, half_dim, 2, length // 2).transpose(2, 0, 1, 3))


def turn(value, cos_part, sin_part):
    parts = []
    for h in range(value.shape[0] // 64):
        a, b = value[64 * h : 64 * h + 32], value[64 * h + 32 : 64 * h + 64]
        parts += [a * cos_part - b * sin_part, b * cos_part + a * sin_part]
    return jnp.concatenate(parts, 0)


def column(row):
    return jnp.transpose(jnp.broadcast_to(row, (128, 128)))


def copy_to(src, dst, send, recv, device):
    return pltpu.make_async_remote_copy(
        src_ref=src, dst_ref=dst, send_sem=send, recv_sem=recv, device_id=device, device_id_type=MESH
    )


def dot_nt(left, right):
    return lax.dot_general(
        left, right, (((1,), (1,)), ((), ())), preferred_element_type=jnp.float32
    )


def dot_tn(left, right):
    return lax.dot_general(
        left, right, (((0,), (0,)), ((), ())), preferred_element_type=jnp.float32
    )


def x_offset(a):
    return a + a // 2 - 2 * (a // 3)


def back_place(a):
    return (2 * a) % 3 + 3 * (a // 3)


def across(a, b, flip):
    dp, ctx = lax.axis_index("dp"), lax.axis_index("ctx")
    x, y = dp % 4, dp // 4
    return ((y + b) % 2) * 4 + (x + x_offset(a)) % 4, (ctx + flip) % 2


def moe_kernel(
    rows_ref,
    gate_ref,
    dy_ref,
    w_gate_ref,
    w_up_ref,
    w_down_ref,
    w_t_ref,
    d_rows_ref,
    d_gate_ref,
    out_part_ref,
    grad_ref,
    w_all_ref,
    rows_all,
    gate_all,
    dy_all,
    w_gu,
    w_dn,
    acc_gu,
    acc_dn,
    out_all,
    din_all,
    sib,
    summed,
    dg_out,
    dg_in,
    places,
    x_buf,
    y_buf,
    d_buf,
    o_buf,
    i_buf,
    gs_buf,
    dgs_buf,
    load_sem,
    ag_send,
    ag_recv,
    sib_send,
    sib_recv,
    rs_send,
    rs_recv,
    dg_send,
    dg_recv,
    store_sem,
    w_send,
    w_recv,
):
    tensor = lax.axis_index("tensor")
    dp, ctx = lax.axis_index("dp"), lax.axis_index("ctx")
    me = dp * 2 + ctx
    kinds = (rows_all, gate_all)

    def to(a, b, flip):
        d, c = across(a, b, flip)
        return (d, c, tensor)

    def side(i):
        return (dp, ctx, (tensor + i) % 8)

    loads = []
    for j in range(2):
        loads.append(
            pltpu.make_async_copy(w_gate_ref.at[j], w_gu.at[j, :, pl.ds(0, 512)], load_sem.at[3 * j])
        )
        loads.append(
            pltpu.make_async_copy(
                w_up_ref.at[j], w_gu.at[j, :, pl.ds(512, 512)], load_sem.at[3 * j + 1]
            )
        )
        loads.append(pltpu.make_async_copy(w_down_ref.at[j], w_dn.at[j], load_sem.at[3 * j + 2]))
    loads.append(pltpu.make_async_copy(dy_ref, dy_all, load_sem.at[6]))
    for load in loads:
        load.start()

    barrier = pltpu.get_barrier_semaphore()
    for a in range(4):
        for b in range(2):
            for flip in range(2):
                if (a, b, flip) != (0, 0, 0):
                    pl.semaphore_signal(
                        barrier, inc=1, device_id=to(a, b, flip), device_id_type=MESH
                    )
    for i in range(1, 8):
        pl.semaphore_signal(barrier, inc=1, device_id=side(i), device_id_type=MESH)
    pl.semaphore_wait(barrier, 22)

    def own_push(k, a, b, flip):
        r = 4 * a + 2 * b + flip
        back = 4 * back_place(a) + 2 * b + flip
        return pltpu.make_async_remote_copy(
            src_ref=kinds[k].at[0],
            dst_ref=kinds[k].at[back],
            send_sem=ag_send.at[k, r],
            recv_sem=ag_recv.at[k, back],
            device_id=to(a, b, flip),
            device_id_type=MESH,
        )

    def relay(k, r):
        return pltpu.make_async_remote_copy(
            src_ref=kinds[k].at[r],
            dst_ref=kinds[k].at[r + 1],
            send_sem=ag_send.at[k, r + 1],
            recv_sem=ag_recv.at[k, r + 1],
            device_id=to(0, 0, 1),
            device_id_type=MESH,
        )

    def arrival(k, r):
        return pltpu.make_async_remote_copy(
            src_ref=kinds[k].at[r],
            dst_ref=kinds[k].at[r],
            send_sem=ag_send.at[k, r],
            recv_sem=ag_recv.at[k, r],
            device_id=to(0, 0, 1),
            device_id_type=MESH,
        )

    rows_all[0] = rows_ref[...]
    gate_all[0] = gate_ref[...]
    for k in range(2):
        own_push(k, 0, 0, 1).start()
    for k in range(2):
        for a in range(4):
            for b in range(2):
                if (a, b) != (0, 0):
                    own_push(k, a, b, 0).start()

    acc_gu[...] = jnp.zeros_like(acc_gu)
    acc_dn[...] = jnp.zeros_like(acc_dn)

    def arrive(a, first):
        for b in range(2):
            if not (first and b == 0):
                for k in range(2):
                    arrival(k, 4 * a + 2 * b).wait_recv()
                    relay(k, 4 * a + 2 * b).start()
        for b in range(2):
            for k in range(2):
                arrival(k, 4 * a + 2 * b + 1).wait_recv()

    half = pl.ds(pl.multiple_of(ctx * 128, 128), 128)

    def w_push(i):
        return copy_to(
            w_t_ref.at[half],
            w_all_ref.at[tensor, half],
            w_send.at[i],
            w_recv.at[tensor, ctx],
            side(i),
        )

    def w_relay(t):
        place = w_all_ref.at[t, half]
        return copy_to(place, place, w_send.at[8 + t], w_recv.at[t, ctx], to(0, 0, 1))

    def w_arrival(t, c):
        place = w_all_ref.at[t, pl.ds(pl.multiple_of(c * 128, 128), 128)]
        return copy_to(place, place, w_send.at[0], w_recv.at[t, c], to(0, 0, 1))

    for i in (1, 7, 2, 6, 3, 5, 4):
        w_push(i).start()
    w_own = pltpu.make_async_copy(w_t_ref, w_all_ref.at[tensor], load_sem.at[7])
    w_own.start()

    def sib_push(ci, r):
        return pltpu.make_async_remote_copy(
            src_ref=din_all.at[r],
            dst_ref=sib.at[ci],
            send_sem=sib_send.at[ci],
            recv_sem=sib_recv.at[ci],
            device_id=to(0, 0, 1),
            device_id_type=MESH,
        )

    def rs_push(a, b):
        back = 2 * back_place(a) + b
        return pltpu.make_async_remote_copy(
            src_ref=din_all.at[4 * a + 2 * b],
            dst_ref=summed.at[back],
            send_sem=rs_send.at[2 * a + b],
            recv_sem=rs_recv.at[back],
            device_id=to(a, b, 0),
            device_id_type=MESH,
        )

    def dg_push(a, b, flip):
        r = 4 * a + 2 * b + flip
        back = 4 * back_place(a) + 2 * b + flip
        return pltpu.make_async_remote_copy(
            src_ref=dg_out.at[r],
            dst_ref=dg_in.at[back],
            send_sem=dg_send.at[r],
            recv_sem=dg_recv.at[back],
            device_id=to(a, b, flip),
            device_id_type=MESH,
        )

    def post(a):
        for b in range(2):
            ci, r = 2 * a + b, 4 * a + 2 * b
            sib_push(ci, r + 1).wait_recv()
            total = din_all[r].astype(jnp.float32) + sib[ci].astype(jnp.float32)
            din_all[r] = total.astype(jnp.bfloat16)

            @pl.when(ci > 0)
            def _():
                rs_push(a, b).start()

    expert_row = lax.broadcasted_iota(jnp.int32, (32, 128), 0)
    slot_row = lax.broadcasted_iota(jnp.int32, (64, 128), 0).astype(jnp.float32)
    before = (
        lax.broadcasted_iota(jnp.int32, (128, 128), 0)
        < lax.broadcasted_iota(jnp.int32, (128, 128), 1)
    ).astype(jnp.float32)
    before = before.astype(jnp.bfloat16)

    def gather(a, q):
        r = 4 * a + q
        gates = gate_all[r]
        at = pl.ds(pl.multiple_of(q * 64, 64), 64)
        rows = [
            jnp.sum(jnp.where(expert_row == 2 * me + j, gates, 0.0), 0, keepdims=True)
            for j in range(2)
        ]
        both = jnp.concatenate(rows + [jnp.zeros((6, 128), jnp.float32)], 0)
        named = jnp.where(both > 0.0, 1.0, 0.0).astype(jnp.bfloat16)
        slots = jnp.dot(named, before, preferred_element_type=jnp.float32)
        hits = [
            jnp.where((slot_row == slots[j : j + 1]) & (rows[j] > 0.0), 1.0, 0.0) for j in range(2)
        ]
        place = jnp.concatenate(hits, 0).astype(jnp.bfloat16)
        places[q] = place
        x = jnp.dot(place, rows_all[r], preferred_element_type=jnp.float32).astype(jnp.bfloat16)
        y = jnp.dot(place, dy_all[r], preferred_element_type=jnp.float32)
        for j in range(2):
            gs = jnp.sum(hits[j] * rows[j], 1, keepdims=True)
            y_j = y[64 * j : 64 * j + 64]
            x_buf[j, at, :] = x[64 * j : 64 * j + 64]
            y_buf[j, at, :] = y_j.astype(jnp.bfloat16)
            d_buf[j, at, :] = (y_j * gs).astype(jnp.bfloat16)
            gs_buf[j, at, :] = gs

    def expert(j):
        x = x_buf[j]
        gu = jnp.dot(x, w_gu[j], preferred_element_type=jnp.float32)
        g, u = gu[:, :512], gu[:, 512:]
        s = jax.nn.sigmoid(g)
        silu = g * s
        act = (silu * u).astype(jnp.bfloat16)
        eout = (
            jnp.dot(act, w_dn[j], preferred_element_type=jnp.float32)
            .astype(jnp.bfloat16)
            .astype(jnp.float32)
        )
        dgs_buf[j] = jnp.sum(y_buf[j].astype(jnp.float32) * eout, 1, keepdims=True)
        o_buf[j] = (eout * gs_buf[j]).astype(jnp.bfloat16)
        d = d_buf[j]
        d_act = dot_nt(d, w_dn[j])
        d_g = (d_act * u * s * (1.0 + g * (1.0 - s))).astype(jnp.bfloat16)
        d_u = (d_act * silu).astype(jnp.bfloat16)
        d_gu = jnp.concatenate([d_g, d_u], 1)
        i_buf[j] = dot_nt(d_gu, w_gu[j]).astype(jnp.bfloat16)
        acc_gu[j] += dot_tn(x, d_gu)
        acc_dn[j] += dot_tn(act, d)

    def spread(a, q):
        r = 4 * a + q
        b, flip = q // 2, q % 2
        at = pl.ds(pl.multiple_of(q * 64, 64), 64)
        place = places[q]
        d, c = across(a, b, flip)
        o = jnp.concatenate([o_buf[0, at, :], o_buf[1, at, :]], 0)
        out_all[d * 2 + c] = dot_tn(place, o).astype(jnp.bfloat16)
        i = jnp.concatenate([i_buf[0, at, :], i_buf[1, at, :]], 0)
        din_all[r] = dot_tn(place, i).astype(jnp.bfloat16)
        hits = place.astype(jnp.float32)
        back = [
            jnp.sum(hits[64 * j : 64 * j + 64] * dgs_buf[j, at, :], 0, keepdims=True)
            for j in range(2)
        ]
        dg_out[r] = jnp.concatenate(back + [jnp.zeros((6, 128), jnp.float32)], 0)

        @pl.when(r > 0)
        def _():
            dg_push(a, b, flip).start()

    arrive(0, True)
    for load in loads:
        load.wait()

    def step(a, carry):
        lax.fori_loop(0, 4, lambda q, c: (gather(a, q), c)[1], 0)
        lax.fori_loop(0, 2, lambda j, c: (expert(j), c)[1], 0)
        lax.fori_loop(0, 4, lambda q, c: (spread(a, q), c)[1], 0)
        for b in range(2):
            sib_push(2 * a + b, 4 * a + 2 * b + 1).start()

        @pl.when(a > 0)
        def _():
            post(a - 1)

        @pl.when(a < 3)
        def _():
            arrive(a + 1, False)

        return carry

    lax.fori_loop(0, 4, step, 0)
    for i in range(1, 8):
        t = (tensor + i) % 8
        w_arrival(t, ctx).wait_recv()
        w_relay(t).start()
    post(3)
    for k in range(2):
        for r in range(1, 16):
            arrival(k, r).wait_send()
    stores = []
    for j in range(2):
        for h in range(8):
            rows_all[8 * j + h] = acc_gu[j, 128 * h : 128 * h + 128, :].astype(jnp.bfloat16)
        for h in range(4):
            dy_all[4 * j + h] = acc_dn[j, 128 * h : 128 * h + 128, :].astype(jnp.bfloat16)
    stores.append(pltpu.make_async_copy(rows_all, grad_ref.at[pl.ds(0, 16)], store_sem.at[0]))
    stores.append(
        pltpu.make_async_copy(
            dy_all.at[pl.ds(0, 8)], grad_ref.at[pl.ds(16, 8)], store_sem.at[1]
        )
    )
    stores.append(pltpu.make_async_copy(out_all, out_part_ref, store_sem.at[2]))
    for store in stores:
        store.start()

    for r in range(1, 16):
        a, b, flip = r // 4, (r // 2) % 2, r % 2
        dg_push(a, b, flip).wait()
    dg_in[0] = dg_out[0]
    d_gate = jnp.zeros((32, 128), jnp.float32)
    for r in range(16):
        d, c = across(r // 4, (r // 2) % 2, r % 2)
        got = dg_in[r]
        for j in range(2):
            d_gate = jnp.where(expert_row == (d * 2 + c) * 2 + j, got[j : j + 1], d_gate)
    d_gate_ref[...] = d_gate
    total = din_all[0].astype(jnp.float32)
    for ci in range(8):
        sib_push(ci, 2 * ci + 1).wait_send()
        if ci > 0:
            rs_push(ci // 2, ci % 2).wait()
    for ci in range(1, 8):
        total = total + summed[ci].astype(jnp.float32)
    d_rows_ref[...] = total
    for i in range(1, 8):
        t = (tensor + i) % 8
        w_arrival(t, 1 - ctx).wait_recv()
        w_push(i).wait_send()
        w_relay(t).wait_send()
    w_own.wait()
    for store in stores:
        store.wait()


def moe(rows, gates, dy, w_gate, w_up, w_down, w_t):
    bf, f32 = jnp.bfloat16, jnp.float32
    vmem, hbm = pl.BlockSpec(memory_space=pltpu.VMEM), pl.BlockSpec(memory_space=pl.ANY)
    sem = pltpu.SemaphoreType.DMA
    return pl.pallas_call(
        moe_kernel,
        out_shape=(
            jax.ShapeDtypeStruct((128, 1024), f32),
            jax.ShapeDtypeStruct((32, 128), f32),
            jax.ShapeDtypeStruct((16, 128, 1024), bf),
            jax.ShapeDtypeStruct((24, 128, 1024), bf),
            jax.ShapeDtypeStruct((8, 256, 1024), bf),
        ),
        in_specs=[vmem] * 2 + [hbm] * 5,
        out_specs=(vmem, vmem, hbm, hbm, hbm),
        scratch_shapes=[
            pltpu.VMEM((16, 128, 1024), bf),
            pltpu.VMEM((16, 32, 128), f32),
            pltpu.VMEM((16, 128, 1024), bf),
            pltpu.VMEM((2, 1024, 1024), bf),
            pltpu.VMEM((2, 512, 1024), bf),
            pltpu.VMEM((2, 1024, 1024), f32),
            pltpu.VMEM((2, 512, 1024), f32),
            pltpu.VMEM((16, 128, 1024), bf),
            pltpu.VMEM((16, 128, 1024), bf),
            pltpu.VMEM((8, 128, 1024), bf),
            pltpu.VMEM((8, 128, 1024), bf),
            pltpu.VMEM((16, 8, 128), f32),
            pltpu.VMEM((16, 8, 128), f32),
            pltpu.VMEM((4, 128, 128), bf),
            pltpu.VMEM((2, 256, 1024), bf),
            pltpu.VMEM((2, 256, 1024), bf),
            pltpu.VMEM((2, 256, 1024), bf),
            pltpu.VMEM((2, 256, 1024), bf),
            pltpu.VMEM((2, 256, 1024), bf),
            pltpu.VMEM((2, 256, 1), f32),
            pltpu.VMEM((2, 256, 1), f32),
            sem((8,)),
            sem((2, 16)),
            sem((2, 16)),
            sem((8,)),
            sem((8,)),
            sem((8,)),
            sem((8,)),
            sem((16,)),
            sem((16,)),
            sem((3,)),
            sem((16,)),
            sem((8, 2)),
        ],
        compiler_params=pltpu.CompilerParams(
            collective_id=1, has_side_effects=True, vmem_limit_bytes=60 << 20
        ),
        cost_estimate=pl.CostEstimate(
            flops=20_000_000_000, bytes_accessed=30_000_000, transcendentals=2_000_000
        ),
    )(rows, gates, dy, w_gate, w_up, w_down, w_t)


def attention_kernel(
    x_ref,
    dy_ref,
    segment_ref,
    norm1_ref,
    q_gain_ref,
    k_gain_ref,
    norm2_ref,
    router_ref,
    routes_ref,
    w_q_ref,
    w_k_ref,
    w_v_ref,
    w_out_ref,
    table_ref,
    rows2_ref,
    gates_ref,
    resid_ref,
    rows1_ref,
    raw_ref,
    inv_ref,
    q_ref,
    kv_ref,
    lse_ref,
    heads_ref,
    w_out_all_ref,
    dy_all_ref,
    w_t_ref,
    h_all,
    dy_all,
    w_all,
    w_q,
    w_k,
    w_v,
    w_t,
    raw,
    table,
    stat,
    stats,
    q_t,
    kv_own,
    kv_sib,
    k_own,
    k_sib,
    starts,
    heads,
    heads_all,
    load_sem,
    h_send,
    h_recv,
    dy_send,
    dy_recv,
    w_send,
    w_recv,
    s_send,
    s_recv,
    kv_sem,
    o_send,
    o_recv,
    store_sem,
):
    f32, bf = jnp.float32, jnp.bfloat16
    dp, ctx, me = lax.axis_index("dp"), lax.axis_index("ctx"), lax.axis_index("tensor")

    def side(i):
        return (dp, ctx, (me + i) % 8)

    def to(a, b, flip):
        d, c = across(a, b, flip)
        return (d, c, me)

    sibling = (dp, 1 - ctx, me)
    loads = [
        pltpu.make_async_copy(w_q_ref, w_q, load_sem.at[0]),
        pltpu.make_async_copy(w_k_ref, w_k, load_sem.at[1]),
        pltpu.make_async_copy(w_v_ref, w_v, load_sem.at[2]),
        pltpu.make_async_copy(w_out_ref, w_all.at[me], load_sem.at[3]),
        pltpu.make_async_copy(table_ref.at[ctx], table, load_sem.at[4]),
    ]
    for load in loads:
        load.start()
    barrier = pltpu.get_barrier_semaphore()
    for i in range(1, 8):
        pl.semaphore_signal(barrier, inc=1, device_id=side(i), device_id_type=MESH)
    for a in range(4):
        for b in range(2):
            if (a, b) != (0, 0):
                pl.semaphore_signal(barrier, inc=1, device_id=to(a, b, 0), device_id_type=MESH)
    pl.semaphore_signal(barrier, inc=1, device_id=sibling, device_id_type=MESH)
    x = x_ref[...].astype(f32)
    inv_one = lax.rsqrt(jnp.mean(x * x, -1, keepdims=True) + EPS)
    h_all[me] = (x * inv_one * norm1_ref[...]).astype(bf)
    dy_all[0] = dy_ref[...]
    pl.semaphore_wait(barrier, 15)

    def h_push(i):
        return copy_to(h_all.at[me], h_all.at[me], h_send.at[i], h_recv.at[me], side(i))

    def h_arrival(t):
        return copy_to(h_all.at[t], h_all.at[t], h_send.at[0], h_recv.at[t], sibling)

    def dy_push(a, b):
        back = 4 * back_place(a) + 2 * b
        return copy_to(
            dy_all.at[0], dy_all.at[back], dy_send.at[4 * a + 2 * b], dy_recv.at[back], to(a, b, 0)
        )

    def dy_relay(r):
        return copy_to(
            dy_all.at[r], dy_all.at[r + 1], dy_send.at[r + 1], dy_recv.at[r + 1], sibling
        )

    def dy_arrival(r):
        return copy_to(dy_all.at[r], dy_all.at[r], dy_send.at[r], dy_recv.at[r], sibling)

    for i in (1, 7, 2, 6, 3, 5, 4):
        h_push(i).start()
    dy_relay(0).start()
    for a in range(4):
        for b in range(2):
            if (a, b) != (0, 0):
                dy_push(a, b).start()

    for load in loads:
        load.wait()
    w_t[0:128, :] = jnp.transpose(w_q[...])
    w_t[128:192, :] = jnp.transpose(w_k[...])
    w_t[192:256, :] = jnp.transpose(w_v[...])
    seg = segment_ref[...]
    start = jnp.zeros((16, 128), f32)
    for s in range(1, 8):
        below = jnp.where(seg < s, 1.0, 0.0)
        count = jnp.sum(jnp.sum(below, 1, keepdims=True), 0, keepdims=True)
        start = jnp.where(seg == s, count, start)
    start = jnp.where(ctx == 0, start[:8], start[8:])
    for t in range(8):
        starts[0:1, 128 * t : 128 * t + 128] = start[t : t + 1]

    def project(i, carry):
        t = (me + i) % 8

        @pl.when(i > 0)
        def _():
            h_arrival(t).wait_recv()

        value = dot_nt(w_t[...], h_all[t])
        raw[t] = value
        square = value * value
        sums = [
            jnp.sum(square[0:128], 0, keepdims=True),
            jnp.sum(square[128:192], 0, keepdims=True),
            jnp.zeros((6, 128), f32),
        ]
        stat[t] = jnp.concatenate(sums, 0)
        return carry

    lax.fori_loop(0, 8, project, 0)
    stats[me] = stat[...]

    def s_push(i):
        return copy_to(stats.at[me], stats.at[me], s_send.at[i], s_recv.at[me], side(i))

    def s_arrival(t):
        return copy_to(stats.at[t], stats.at[t], s_send.at[0], s_recv.at[t], sibling)

    for i in range(1, 8):
        s_push(i).start()
    store_rows = pltpu.make_async_copy(h_all, rows1_ref, store_sem.at[0])
    store_raw = pltpu.make_async_copy(raw, raw_ref, store_sem.at[1])
    store_wt = pltpu.make_async_copy(w_t, w_t_ref, store_sem.at[8])
    store_rows.start()
    store_raw.start()
    store_wt.start()

    def w_push(i):
        half = w_all.at[me, pl.ds(pl.multiple_of(ctx * 64, 64), 64)]
        return copy_to(half, half, w_send.at[i], w_recv.at[me, ctx], side(i))

    def w_relay(t):
        half = w_all.at[t, pl.ds(pl.multiple_of(ctx * 64, 64), 64)]
        return copy_to(half, half, w_send.at[8 + t], w_recv.at[t, ctx], sibling)

    def w_arrival(t, c):
        half = w_all.at[t, pl.ds(pl.multiple_of(c * 64, 64), 64)]
        return copy_to(half, half, w_send.at[0], w_recv.at[t, c], sibling)

    for i in (1, 7, 2, 6, 3, 5, 4):
        w_push(i).start()
    gain_q = column(q_gain_ref[...])
    gain_k = column(jnp.concatenate([k_gain_ref[...], jnp.zeros((1, 64), f32)], 1))[:64]
    for i in range(1, 8):
        s_arrival((me + i) % 8).wait_recv()

    def finish(t, carry):
        at = pl.ds(pl.multiple_of(t * 128, 128), 128)
        sums = stats[0, t]
        for s in range(1, 8):
            sums = sums + stats[s, t]
        width = jnp.where(lax.broadcasted_iota(jnp.int32, (8, 128), 0) == 0, 1024.0, 512.0)
        inv = lax.rsqrt(sums / width + EPS)
        inv_ref[t] = inv
        value = raw[t]
        cos_part, sin_part = table[0, :, at], table[1, :, at]
        queries = turn(value[0:128] * inv[0:1] * gain_q, cos_part, sin_part).astype(bf)
        keys = turn(value[128:192] * inv[1:2] * gain_k, cos_part, sin_part).astype(bf)
        q_t[:, at] = queries
        kv_own[0:64, at] = keys
        kv_own[64:128, at] = value[192:256].astype(bf)
        k_own[at, :] = jnp.transpose(keys)
        return carry

    lax.fori_loop(0, 8, finish, 0)
    kv_push = copy_to(kv_own, kv_sib, kv_sem.at[0], kv_sem.at[1], sibling)
    kv_push.start()

    key_row = lax.broadcasted_iota(jnp.int32, (256, 256), 0).astype(f32)
    query_lane = lax.broadcasted_iota(jnp.int32, (256, 256), 1).astype(f32)
    base = (ctx * 1024).astype(f32)

    def attend(n, carry):
        i, h = n // 2, n % 2
        at = pl.ds(pl.multiple_of(i * 256, 256), 256)
        q = q_t[pl.ds(pl.multiple_of(h * 64, 64), 64), at] * 0.125
        begin = starts[0:1, at]

        def block(keys, values, first_key, state, causal):
            top, total, acc = state
            s = jnp.dot(keys, q, preferred_element_type=f32)
            ok = key_row >= begin - first_key
            if causal:
                ok = ok & (key_row <= query_lane)
            s = jnp.where(ok, s, MASKED)
            new_top = jnp.maximum(top, jnp.max(s, 0, keepdims=True))
            e = jnp.exp(s - new_top)
            shrink = jnp.exp(top - new_top)
            total = total * shrink + jnp.sum(e, 0, keepdims=True)
            acc = acc * shrink + jnp.dot(values, e.astype(bf), preferred_element_type=f32)
            return new_top, total, acc

        state = (jnp.full((1, 256), MASKED, f32), jnp.zeros((1, 256), f32), jnp.zeros((64, 256), f32))
        state = block(
            k_own[at, :], kv_own[64:128, at], base + (i * 256).astype(f32), state, True
        )

        def own(j, state):
            ks = pl.ds(pl.multiple_of(j * 256, 256), 256)
            return block(k_own[ks, :], kv_own[64:128, ks], base + (j * 256).astype(f32), state, False)

        state = lax.fori_loop(0, i, own, state)

        def other(j, state):
            ks = pl.ds(pl.multiple_of(j * 256, 256), 256)
            return block(k_sib[ks, :], kv_sib[64:128, ks], (j * 256).astype(f32), state, False)

        top, total, acc = lax.fori_loop(0, 4 * ctx, other, state)
        out = (acc / total).astype(bf)
        hs = pl.ds(pl.multiple_of(h * 64, 64), 64)
        heads[2 * i, hs, :] = out[:, :128]
        heads[2 * i + 1, hs, :] = out[:, 128:]
        lse_ref[h, 0:1, at] = top + jnp.log(total)
        return carry

    kv_push.wait()

    def straighten(t, carry):
        at = pl.ds(pl.multiple_of(t * 128, 128), 128)
        k_sib[at, :] = jnp.transpose(kv_sib[0:64, at])
        return carry

    lax.fori_loop(0, 8, straighten, 0)
    lax.fori_loop(0, 8, attend, 0)

    def o_push(i):
        return copy_to(
            heads.at[(me + i) % 8], heads_all.at[me], o_send.at[i], o_recv.at[me], side(i)
        )

    def o_arrival(t):
        return copy_to(heads_all.at[t], heads_all.at[t], o_send.at[0], o_recv.at[t], sibling)

    for i in range(1, 8):
        o_push(i).start()
    heads_all[me] = heads[me]
    stores = [
        pltpu.make_async_copy(q_t, q_ref, store_sem.at[2]),
        pltpu.make_async_copy(kv_own, kv_ref.at[0], store_sem.at[3]),
        pltpu.make_async_copy(kv_sib, kv_ref.at[1], store_sem.at[4]),
        pltpu.make_async_copy(heads, heads_ref, store_sem.at[5]),
    ]
    for store in stores:
        store.start()

    def pass_on(i, carry):
        t = (me + i) % 8
        w_arrival(t, ctx).wait_recv()
        w_relay(t).start()
        return carry

    lax.fori_loop(1, 8, pass_on, 0)

    def pass_dy(c, carry):
        dy_arrival(2 * c).wait_recv()
        dy_relay(2 * c).start()
        return carry

    lax.fori_loop(1, 8, pass_dy, 0)
    for i in range(1, 8):
        t = (me + i) % 8
        w_arrival(t, 1 - ctx).wait_recv()
        o_arrival(t).wait_recv()
    store_w = pltpu.make_async_copy(w_all, w_out_all_ref, store_sem.at[6])
    store_w.start()
    attended = dot_tn(heads_all[...].reshape(1024, 128), w_all[...].reshape(1024, 1024))
    resid = x + attended
    resid_ref[...] = resid
    inv_two = lax.rsqrt(jnp.mean(resid * resid, -1, keepdims=True) + EPS)
    rows2 = (resid * inv_two * norm2_ref[...]).astype(bf)
    rows2_ref[...] = rows2
    logits = jnp.transpose(jnp.dot(rows2, router_ref[...], preferred_element_type=f32))
    expert_row = lax.broadcasted_iota(jnp.int32, (32, 128), 0)
    routes = jnp.transpose(routes_ref[...])
    named = routes[0:1] == expert_row
    for k in range(1, 8):
        named = named | (routes[k : k + 1] == expert_row)
    chosen = jnp.where(named, logits, MASKED)
    weight = jnp.where(named, jnp.exp(chosen - jnp.max(chosen, 0, keepdims=True)), 0.0)
    gates_ref[...] = weight / jnp.sum(weight, 0, keepdims=True)

    for c in range(8):
        dy_arrival(2 * c + 1).wait_recv()
    store_dy = pltpu.make_async_copy(dy_all, dy_all_ref, store_sem.at[7])
    store_dy.start()
    for i in range(1, 8):
        h_push(i).wait_send()
        s_push(i).wait_send()
        w_push(i).wait_send()
        w_relay((me + i) % 8).wait_send()
        o_push(i).wait_send()
        dy_push(i // 2, i % 2).wait_send()
    for c in range(8):
        dy_relay(2 * c).wait_send()
    for store in [store_rows, store_raw, store_wt, store_w, store_dy] + stores:
        store.wait()


def attention(x, dy, segment, norm1, q_gain, k_gain, norm2, router, routes, w_q, w_k, w_v, w_out):
    bf, f32 = jnp.bfloat16, jnp.float32
    vmem, hbm = pl.BlockSpec(memory_space=pltpu.VMEM), pl.BlockSpec(memory_space=pl.ANY)
    sem = pltpu.SemaphoreType.DMA
    shape = jax.ShapeDtypeStruct
    table = jnp.asarray(rope_constants(2048, 32))
    return pl.pallas_call(
        attention_kernel,
        out_shape=(
            shape((128, 1024), bf),
            shape((32, 128), f32),
            shape((128, 1024), f32),
            shape((8, 128, 1024), bf),
            shape((8, 256, 128), f32),
            shape((8, 8, 128), f32),
            shape((128, 1024), bf),
            shape((2, 128, 1024), bf),
            shape((2, 8, 1024), f32),
            shape((8, 128, 128), bf),
            shape((8, 128, 1024), bf),
            shape((16, 128, 1024), bf),
            shape((256, 1024), bf),
        ),
        in_specs=[vmem] * 9 + [hbm] * 5,
        out_specs=(vmem, vmem, vmem, hbm, hbm, vmem, hbm, hbm, vmem, hbm, hbm, hbm, hbm),
        scratch_shapes=[
            pltpu.VMEM((8, 128, 1024), bf),
            pltpu.VMEM((16, 128, 1024), bf),
            pltpu.VMEM((8, 128, 1024), bf),
            pltpu.VMEM((1024, 128), bf),
            pltpu.VMEM((1024, 64), bf),
            pltpu.VMEM((1024, 64), bf),
            pltpu.VMEM((256, 1024), bf),
            pltpu.VMEM((8, 256, 128), f32),
            pltpu.VMEM((2, 32, 1024), f32),
            pltpu.VMEM((8, 8, 128), f32),
            pltpu.VMEM((8, 8, 8, 128), f32),
            pltpu.VMEM((128, 1024), bf),
            pltpu.VMEM((128, 1024), bf),
            pltpu.VMEM((128, 1024), bf),
            pltpu.VMEM((1024, 64), bf),
            pltpu.VMEM((1024, 64), bf),
            pltpu.VMEM((8, 1024), f32),
            pltpu.VMEM((8, 128, 128), bf),
            pltpu.VMEM((8, 128, 128), bf),
            sem((5,)),
            sem((8,)),
            sem((8,)),
            sem((16,)),
            sem((16,)),
            sem((16,)),
            sem((8, 2)),
            sem((8,)),
            sem((8,)),
            sem((2,)),
            sem((8,)),
            sem((8,)),
            sem((9,)),
        ],
        compiler_params=pltpu.CompilerParams(
            collective_id=2, has_side_effects=True, vmem_limit_bytes=56 << 20
        ),
        cost_estimate=pl.CostEstimate(
            flops=5_000_000_000, bytes_accessed=20_000_000, transcendentals=4_000_000
        ),
    )(
        x,
        dy,
        segment.reshape(16, 128),
        norm1.reshape(1, 1024),
        q_gain.reshape(1, 128),
        k_gain.reshape(1, 64),
        norm2.reshape(1, 1024),
        router,
        routes,
        w_q,
        w_k,
        w_v,
        w_out,
        table,
    )


def backward_kernel(
    x_ref,
    dy_ref,
    d_rows_ref,
    d_gate_ref,
    gates_ref,
    rows2_ref,
    resid_ref,
    router_ref,
    norm1_ref,
    norm2_ref,
    q_gain_ref,
    k_gain_ref,
    segment_ref,
    inv_ref,
    lse_ref,
    rows1_ref,
    raw_ref,
    q_ref,
    kv_ref,
    heads_ref,
    w_out_ref,
    w_all_ref,
    table_ref,
    grad_x_ref,
    norm1_out_ref,
    pack_ref,
    rows1,
    raw,
    q_t,
    kv_own,
    kv_sib,
    heads,
    w_out,
    w_all,
    table,
    starts,
    d_resid,
    datt_all,
    dh_send,
    dh_all,
    tiny,
    q_cat,
    q_nat,
    d_cat,
    d_nat,
    lanes,
    k_nat,
    v_nat,
    dq_acc,
    dk_acc,
    dv_acc,
    dkv_out,
    dkv_in,
    terms,
    stat,
    stats,
    dqkv,
    dqkv_all,
    heads2,
    pack,
    pack_sib,
    pack_in,
    result,
    n1,
    n1_chips,
    n1_sib,
    load_sem,
    a_send,
    a_recv,
    dh_send_sem,
    dh_recv,
    t_send,
    t_recv,
    s_send,
    s_recv,
    dkv_sem,
    o_send,
    o_recv,
    p_sem,
    rs_send,
    rs_recv,
    g_send,
    g_recv,
    gs_send,
    gs_recv,
    n_send,
    n_recv,
    m_send,
    m_recv,
    ns_sem,
):
    f32, bf = jnp.float32, jnp.bfloat16
    dp, ctx, me = lax.axis_index("dp"), lax.axis_index("ctx"), lax.axis_index("tensor")
    sibling = (dp, 1 - ctx, me)

    def side(i):
        return (dp, ctx, (me + i) % 8)

    def chip(i):
        return ((dp + i) % 8, ctx, me)

    sources = (rows1_ref, raw_ref, q_ref, kv_ref.at[0], kv_ref.at[1], heads_ref, w_out_ref)
    targets = (rows1, raw, q_t, kv_own, kv_sib, heads, w_out)
    loads = [
        pltpu.make_async_copy(s, t, load_sem.at[n])
        for n, (s, t) in enumerate(zip(sources, targets, strict=True))
    ]
    loads.append(pltpu.make_async_copy(w_all_ref, w_all, load_sem.at[7]))
    loads.append(pltpu.make_async_copy(table_ref.at[ctx], table, load_sem.at[8]))
    for load in loads:
        load.start()
    barrier = pltpu.get_barrier_semaphore()
    for i in range(1, 8):
        pl.semaphore_signal(barrier, inc=1, device_id=side(i), device_id_type=MESH)
        pl.semaphore_signal(barrier, inc=1, device_id=chip(i), device_id_type=MESH)
    pl.semaphore_signal(barrier, inc=1, device_id=sibling, device_id_type=MESH)

    gates, d_gate = gates_ref[...], d_gate_ref[...]
    d_logits = gates * (d_gate - jnp.sum(gates * d_gate, 0, keepdims=True))
    d_normed = d_rows_ref[...] + lax.dot_general(
        jnp.transpose(d_logits),
        router_ref[...].astype(f32),
        (((1,), (1,)), ((), ())),
        preferred_element_type=f32,
        precision=lax.Precision.HIGHEST,
    )
    resid = resid_ref[...]
    inv_two = lax.rsqrt(jnp.mean(resid * resid, -1, keepdims=True) + EPS)
    res_hat = resid * inv_two
    scaled = d_normed * norm2_ref[...]
    d_res = dy_ref[...].astype(f32) + inv_two * (
        scaled - res_hat * jnp.mean(scaled * res_hat, -1, keepdims=True)
    )
    d_resid[...] = d_res
    datt = d_res.astype(bf)
    datt_all[me] = datt
    for n in (6,):
        loads[n].wait()
    d_heads = dot_nt(w_out[...].reshape(1024, 1024), datt).astype(bf)
    dh_send[...] = d_heads.reshape(8, 128, 128)
    dh_all[me] = dh_send[me]
    pl.semaphore_wait(barrier, 15)

    def dh_push(i):
        return copy_to(
            dh_send.at[(me + i) % 8], dh_all.at[me], dh_send_sem.at[i], dh_recv.at[me], side(i)
        )

    def dh_arrival(t):
        return copy_to(dh_all.at[t], dh_all.at[t], dh_send_sem.at[0], dh_recv.at[t], sibling)

    for i in range(1, 8):
        dh_push(i).start()

    norm2_part = jnp.sum(d_normed * res_hat, 0, keepdims=True)
    router_part = jnp.dot(
        d_logits,
        rows2_ref[...].astype(f32),
        preferred_element_type=f32,
        precision=lax.Precision.HIGHEST,
    )
    tiny[me] = jnp.concatenate(
        [router_part, norm2_part, jnp.zeros((15, 1024), f32)], 0
    ).astype(bf)

    def t_push(i):
        return copy_to(tiny.at[me], tiny.at[me], t_send.at[i], t_recv.at[me], side(i))

    def t_arrival(t):
        return copy_to(tiny.at[t], tiny.at[t], t_send.at[0], t_recv.at[t], sibling)

    def a_push(i):
        return copy_to(datt_all.at[me], datt_all.at[me], a_send.at[i], a_recv.at[me], side(i))

    def a_arrival(t):
        return copy_to(datt_all.at[t], datt_all.at[t], a_send.at[0], a_recv.at[t], sibling)

    for i in range(1, 8):
        t_push(i).start()
    for i in (1, 7, 2, 6, 3, 5, 4):
        a_push(i).start()

    for n in (0, 1, 2, 3, 4, 5, 7, 8):
        loads[n].wait()
    seg = segment_ref[...]
    start = jnp.zeros((16, 128), f32)
    for s in range(1, 8):
        below = jnp.where(seg < s, 1.0, 0.0)
        count = jnp.sum(jnp.sum(below, 1, keepdims=True), 0, keepdims=True)
        start = jnp.where(seg == s, count, start)
    start = jnp.where(ctx == 0, start[:8], start[8:])
    for t in range(8):
        starts[0:1, 128 * t : 128 * t + 128] = start[t : t + 1]

    def lay_out(t, carry):
        at = pl.ds(pl.multiple_of(t * 128, 128), 128)
        i, half = t // 2, t % 2
        q = q_t[:, at] * 0.125
        for h in range(2):
            spot = pl.ds(pl.multiple_of(h * 256 + half * 128, 128), 128)
            q_h = q[64 * h : 64 * h + 64]
            q_cat[i, :, spot] = q_h
            q_nat[i, spot, :] = jnp.transpose(q_h)
            lanes[i, 0:1, spot] = lse_ref[h, 0:1, at]
            lanes[i, 2:3, spot] = starts[0:1, at]
        for n, kv in enumerate((kv_own, kv_sib)):
            k_nat[n, at, :] = jnp.transpose(kv[0:64, at])
            v_nat[n, at, :] = jnp.transpose(kv[64:128, at])
        heads2[:, at] = heads[t]
        return carry

    lax.fori_loop(0, 8, lay_out, 0)
    dk_acc[...] = jnp.zeros_like(dk_acc)
    dv_acc[...] = jnp.zeros_like(dv_acc)
    dq_acc[...] = jnp.zeros_like(dq_acc)
    for i in range(1, 8):
        dh_arrival((me + i) % 8).wait_recv()

    def lay_dh(t, carry):
        i, half = t // 2, t % 2
        d, o = dh_all[t], heads[t]
        product = d.astype(f32) * o.astype(f32)
        for h in range(2):
            spot = pl.ds(pl.multiple_of(h * 256 + half * 128, 128), 128)
            d_h = d[64 * h : 64 * h + 64]
            d_cat[i, :, spot] = d_h
            d_nat[i, spot, :] = jnp.transpose(d_h)
            lanes[i, 1:2, spot] = jnp.sum(product[64 * h : 64 * h + 64], 0, keepdims=True)
        return carry

    lax.fori_loop(0, 8, lay_dh, 0)
    key_row = lax.broadcasted_iota(jnp.int32, (256, 512), 0).astype(f32)
    query_lane = (lax.broadcasted_iota(jnp.int32, (256, 512), 1) % 256).astype(f32)
    base = (ctx * 1024).astype(f32)

    def block(n, i, j, first_key, causal):
        ks = pl.ds(pl.multiple_of(j * 256, 256), 256)
        kv = (kv_own, kv_sib)[n]
        s = jnp.dot(k_nat[n, ks, :], q_cat[i], preferred_element_type=f32)
        ok = key_row >= lanes[i, 2:3, :] - first_key
        if causal:
            ok = ok & (key_row <= query_lane)
        p = jnp.exp(jnp.where(ok, s, MASKED) - lanes[i, 0:1, :])
        dp_ = jnp.dot(v_nat[n, ks, :], d_cat[i], preferred_element_type=f32)
        ds = (p * (dp_ - lanes[i, 1:2, :])).astype(bf)
        dv_acc[n, ks, :] += jnp.dot(p.astype(bf), d_nat[i], preferred_element_type=f32)
        dk_acc[n, ks, :] += jnp.dot(ds, q_nat[i], preferred_element_type=f32)
        dq_acc[i] += jnp.dot(kv[0:64, ks], ds, preferred_element_type=f32)

    def cross(n, carry):
        block(1, n // 4, n % 4, ((n % 4) * 256).astype(f32), False)
        return carry

    lax.fori_loop(0, 16 * ctx, cross, 0)
    dkv_push = copy_to(dkv_out, dkv_in, dkv_sem.at[0], dkv_sem.at[1], sibling)

    def upright(t, carry):
        at = pl.ds(pl.multiple_of(t * 128, 128), 128)
        dkv_out[0:64, at] = jnp.transpose(dk_acc[1, at, :]).astype(bf)
        dkv_out[64:128, at] = jnp.transpose(dv_acc[1, at, :]).astype(bf)
        return carry

    lax.fori_loop(0, 8, upright, 0)
    dkv_push.start()

    def within(i, carry):
        def full(j, c):
            block(0, i, j, base + (j * 256).astype(f32), False)
            return c

        lax.fori_loop(0, i, full, 0)
        block(0, i, i, base + (i * 256).astype(f32), True)
        return carry

    lax.fori_loop(0, 4, within, 0)
    gain_q = column(q_gain_ref[...])
    gain_k = column(jnp.concatenate([k_gain_ref[...], jnp.zeros((1, 64), f32)], 1))[:64]
    dkv_push.wait()

    def unturn(t, sums):
        at = pl.ds(pl.multiple_of(t * 128, 128), 128)
        i, half = t // 2, t % 2
        parts = [
            dq_acc[i, :, pl.ds(pl.multiple_of(h * 256 + half * 128, 128), 128)] for h in range(2)
        ]
        cos_part, sin_part = table[0, :, at], -table[1, :, at]
        inv = inv_ref[t]
        d_q = turn(jnp.concatenate(parts, 0) * 0.125, cos_part, sin_part)
        came = dkv_in[:, at].astype(f32)
        d_k = turn(jnp.transpose(dk_acc[0, at, :]) + came[0:64], cos_part, sin_part)
        d_v = jnp.transpose(dv_acc[0, at, :]) + came[64:128]
        q_hat, k_hat = raw[t, 0:128] * inv[0:1], raw[t, 128:192] * inv[1:2]
        q_sum, k_sum = sums[0] + d_q * q_hat, sums[1] + d_k * k_hat
        q_term, k_term = d_q * gain_q, d_k * gain_k
        terms[t, 0:128] = q_term
        terms[t, 128:192] = k_term
        dqkv[t, 192:256] = d_v.astype(bf)
        rows = [
            jnp.sum(q_term * q_hat, 0, keepdims=True),
            jnp.sum(k_term * k_hat, 0, keepdims=True),
            jnp.zeros((6, 128), f32),
        ]
        stat[t] = jnp.concatenate(rows, 0)
        return q_sum, k_sum

    q_sum, k_sum = lax.fori_loop(
        0, 8, unturn, (jnp.zeros((128, 128), f32), jnp.zeros((64, 128), f32))
    )
    stats[me] = stat[...]

    def s_push(i):
        return copy_to(stats.at[me], stats.at[me], s_send.at[i], s_recv.at[me], side(i))

    def s_arrival(t):
        return copy_to(stats.at[t], stats.at[t], s_send.at[0], s_recv.at[t], sibling)

    for i in range(1, 8):
        s_push(i).start()
    for i in range(1, 8):
        a_arrival((me + i) % 8).wait_recv()
    pack[256:384, :] = jnp.dot(
        heads2[...], datt_all[...].reshape(1024, 1024), preferred_element_type=f32
    ).astype(bf)
    for i in range(1, 8):
        t_arrival((me + i) % 8).wait_recv()
    total = tiny[0].astype(f32)
    for t in range(1, 8):
        total = total + tiny[t].astype(f32)
    q_row = jnp.sum(jnp.transpose(q_sum), 0, keepdims=True)
    k_row = jnp.sum(jnp.transpose(k_sum), 0, keepdims=True)
    gain_row = jnp.concatenate([q_row, k_row, jnp.zeros((1, 1024 - 192), f32)], 1)
    extra = jnp.concatenate([total[0:33], gain_row, jnp.zeros((94, 1024), f32)], 0)
    pack[384:512, :] = extra.astype(bf)
    for i in range(1, 8):
        s_arrival((me + i) % 8).wait_recv()

    def finish(t, carry):
        at = pl.ds(pl.multiple_of(t * 128, 128), 128)
        inner = stats[0, t]
        for s in range(1, 8):
            inner = inner + stats[s, t]
        inv = inv_ref[t]
        q_hat, k_hat = raw[t, 0:128] * inv[0:1], raw[t, 128:192] * inv[1:2]
        d_q = inv[0:1] * (terms[t, 0:128] - q_hat * (inner[0:1] / 1024.0))
        d_k = inv[1:2] * (terms[t, 128:192] - k_hat * (inner[1:2] / 512.0))
        dqkv[t, 0:128] = d_q.astype(bf)
        dqkv[t, 128:192] = d_k.astype(bf)
        return carry

    lax.fori_loop(0, 8, finish, 0)

    def o_push(i):
        return copy_to(
            dqkv.at[(me + i) % 8], dqkv_all.at[me], o_send.at[i], o_recv.at[me], side(i)
        )

    def o_arrival(t):
        return copy_to(dqkv_all.at[t], dqkv_all.at[t], o_send.at[0], o_recv.at[t], sibling)

    for i in range(1, 8):
        o_push(i).start()
    dqkv_all[me] = dqkv[me]
    grad_qkv = jnp.zeros((256, 1024), f32)
    for t in range(8):
        grad_qkv = grad_qkv + jnp.dot(dqkv[t], rows1[t], preferred_element_type=f32)
    pack[0:256, :] = grad_qkv.astype(bf)
    mine = pl.ds(pl.multiple_of(ctx * 256, 256), 256)
    theirs = pl.ds(pl.multiple_of((1 - ctx) * 256, 256), 256)
    p_push = copy_to(pack.at[theirs], pack_sib, p_sem.at[0], p_sem.at[1], sibling)
    p_push.start()
    for i in range(1, 8):
        o_arrival((me + i) % 8).wait_recv()
    d_rows1 = dot_tn(dqkv_all[...].reshape(2048, 128), w_all[...].reshape(2048, 1024))
    x = x_ref[...].astype(f32)
    inv_one = lax.rsqrt(jnp.mean(x * x, -1, keepdims=True) + EPS)
    x_hat = x * inv_one
    norm1_part = jnp.sum(d_rows1 * x_hat, 0, keepdims=True)
    n1[me] = jnp.concatenate([norm1_part[:, 128 * t : 128 * t + 128] for t in range(8)], 0)

    def n_push(i):
        return copy_to(n1.at[me], n1.at[me], n_send.at[i], n_recv.at[me], side(i))

    def n_arrival(t):
        return copy_to(n1.at[t], n1.at[t], n_send.at[0], n_recv.at[t], sibling)

    for i in range(1, 8):
        n_push(i).start()
    p_push.wait()
    pack[mine, :] = (pack[mine, :].astype(f32) + pack_sib[...].astype(f32)).astype(bf)

    def rs_push(i):
        to = (dp + i) % 8
        rows = pack.at[pl.ds(pl.multiple_of(ctx * 256 + to * 32, 32), 32)]
        return copy_to(rows, pack_in.at[dp], rs_send.at[i], rs_recv.at[dp], chip(i))

    def rs_arrival(d):
        return copy_to(pack_in.at[d], pack_in.at[d], rs_send.at[0], rs_recv.at[d], sibling)

    for i in range(1, 8):
        rs_push(i).start()
    scaled = d_rows1 * norm1_ref[...]
    grad_x_ref[...] = (
        d_resid[...] + inv_one * (scaled - x_hat * jnp.mean(scaled * x_hat, -1, keepdims=True))
    ).astype(bf)
    for i in range(1, 8):
        n_arrival((me + i) % 8).wait_recv()
    norm1_sum = n1[0]
    for t in range(1, 8):
        norm1_sum = norm1_sum + n1[t]
    n1_chips[dp] = norm1_sum

    def m_push(i):
        return copy_to(n1_chips.at[dp], n1_chips.at[dp], m_send.at[i], m_recv.at[dp], chip(i))

    def m_arrival(d):
        return copy_to(n1_chips.at[d], n1_chips.at[d], m_send.at[0], m_recv.at[d], sibling)

    for i in range(1, 8):
        m_push(i).start()
    pack_in[dp] = pack[pl.ds(pl.multiple_of(ctx * 256 + dp * 32, 32), 32), :]
    for i in range(1, 8):
        rs_arrival((dp + i) % 8).wait_recv()
    owned = pack_in[0].astype(f32)
    for d in range(1, 8):
        owned = owned + pack_in[d].astype(f32)
    result[ctx, dp] = owned.astype(bf)

    def g_push(i):
        return copy_to(
            result.at[ctx, dp], result.at[ctx, dp], g_send.at[i], g_recv.at[dp], chip(i)
        )

    def g_arrival(d):
        return copy_to(result.at[ctx, d], result.at[ctx, d], g_send.at[0], g_recv.at[d], sibling)

    def g_relay(d):
        return copy_to(
            result.at[ctx, d], result.at[ctx, d], gs_send.at[d], gs_recv.at[d], sibling
        )

    def g_sib_arrival(d):
        place = result.at[1 - ctx, d]
        return copy_to(place, place, gs_send.at[d], gs_recv.at[d], sibling)

    for i in range(1, 8):
        g_push(i).start()
    g_relay(dp).start()
    for i in range(1, 8):
        m_arrival((dp + i) % 8).wait_recv()
    norm1_sum = n1_chips[0]
    for d in range(1, 8):
        norm1_sum = norm1_sum + n1_chips[d]
    n1_sib[0] = norm1_sum
    ns_push = copy_to(n1_sib.at[0], n1_sib.at[1], ns_sem.at[0], ns_sem.at[1], sibling)
    ns_push.start()

    def pass_on(i, carry):
        d = (dp + i) % 8
        g_arrival(d).wait_recv()
        g_relay(d).start()
        return carry

    lax.fori_loop(1, 8, pass_on, 0)
    ns_push.wait()
    norm1_out_ref[...] = n1_sib[0] + n1_sib[1]
    for d in range(8):
        g_sib_arrival(d).wait_recv()
        g_relay(d).wait_send()
    pack_ref[...] = result[...].reshape(512, 1024)
    for i in range(1, 8):
        dh_push(i).wait_send()
        t_push(i).wait_send()
        a_push(i).wait_send()
        s_push(i).wait_send()
        o_push(i).wait_send()
        n_push(i).wait_send()
        rs_push(i).wait_send()
        m_push(i).wait_send()
        g_push(i).wait_send()


def backward(small, large):
    bf, f32 = jnp.bfloat16, jnp.float32
    vmem, hbm = pl.BlockSpec(memory_space=pltpu.VMEM), pl.BlockSpec(memory_space=pl.ANY)
    sem = pltpu.SemaphoreType.DMA
    shape = jax.ShapeDtypeStruct
    table = jnp.asarray(rope_constants(2048, 32))
    return pl.pallas_call(
        backward_kernel,
        out_shape=(shape((128, 1024), bf), shape((8, 128), f32), shape((512, 1024), bf)),
        in_specs=[vmem] * 15 + [hbm] * 8,
        out_specs=(vmem, vmem, vmem),
        scratch_shapes=[
            pltpu.VMEM((8, 128, 1024), bf),
            pltpu.VMEM((8, 256, 128), f32),
            pltpu.VMEM((128, 1024), bf),
            pltpu.VMEM((128, 1024), bf),
            pltpu.VMEM((128, 1024), bf),
            pltpu.VMEM((8, 128, 128), bf),
            pltpu.VMEM((8, 128, 1024), bf),
            pltpu.VMEM((8, 256, 1024), bf),
            pltpu.VMEM((2, 32, 1024), f32),
            pltpu.VMEM((8, 1024), f32),
            pltpu.VMEM((128, 1024), f32),
            pltpu.VMEM((8, 128, 1024), bf),
            pltpu.VMEM((8, 128, 128), bf),
            pltpu.VMEM((8, 128, 128), bf),
            pltpu.VMEM((8, 48, 1024), bf),
            pltpu.VMEM((4, 64, 512), bf),
            pltpu.VMEM((4, 512, 64), bf),
            pltpu.VMEM((4, 64, 512), bf),
            pltpu.VMEM((4, 512, 64), bf),
            pltpu.VMEM((4, 8, 512), f32),
            pltpu.VMEM((2, 1024, 64), bf),
            pltpu.VMEM((2, 1024, 64), bf),
            pltpu.VMEM((4, 64, 512), f32),
            pltpu.VMEM((2, 1024, 64), f32),
            pltpu.VMEM((2, 1024, 64), f32),
            pltpu.VMEM((128, 1024), bf),
            pltpu.VMEM((128, 1024), bf),
            pltpu.VMEM((8, 192, 128), f32),
            pltpu.VMEM((8, 8, 128), f32),
            pltpu.VMEM((8, 8, 8, 128), f32),
            pltpu.VMEM((8, 256, 128), bf),
            pltpu.VMEM((8, 256, 128), bf),
            pltpu.VMEM((128, 1024), bf),
            pltpu.VMEM((512, 1024), bf),
            pltpu.VMEM((256, 1024), bf),
            pltpu.VMEM((8, 32, 1024), bf),
            pltpu.VMEM((2, 8, 32, 1024), bf),
            pltpu.VMEM((8, 8, 128), f32),
            pltpu.VMEM((8, 8, 128), f32),
            pltpu.VMEM((2, 8, 128), f32),
            sem((9,)),
        ]
        + [sem((8,))] * 8
        + [sem((2,))]
        + [sem((8,))] * 2
        + [sem((2,))]
        + [sem((8,))] * 10
        + [sem((2,))],
        compiler_params=pltpu.CompilerParams(
            collective_id=3, has_side_effects=True, vmem_limit_bytes=56 << 20
        ),
        cost_estimate=pl.CostEstimate(
            flops=10_000_000_000, bytes_accessed=20_000_000, transcendentals=4_000_000
        ),
    )(*small, *large, table)


def shards(
    hidden_in,
    segment,
    norm1_gain,
    w_query,
    w_key,
    w_value,
    q_gain,
    k_gain,
    w_out,
    norm2_gain,
    router,
    w_gate,
    w_up,
    w_down,
    routes,
    cotangent,
):
    f32, bf = jnp.float32, jnp.bfloat16
    rows2, gates, resid, rows1, raw, inv, q_t, kv, lse, heads, w_out_all, dy_all, w_t = attention(
        hidden_in,
        cotangent,
        segment,
        norm1_gain,
        q_gain,
        k_gain,
        norm2_gain,
        router,
        routes,
        w_query,
        w_key,
        w_value,
        w_out,
    )
    d_rows, d_gate, out_part, grads, w_all = moe(
        rows2, gates, dy_all, w_gate, w_up, w_down, w_t
    )
    mixed = lax.psum_scatter(
        out_part.reshape(-1, 1024), ("dp", "ctx"), scatter_dimension=0, tiled=True
    )
    output = (resid + mixed.astype(f32)).astype(bf)
    grad_x, norm1_sum, pack = backward(
        (
            hidden_in,
            cotangent,
            d_rows,
            d_gate,
            gates,
            rows2,
            resid,
            router,
            norm1_gain.reshape(1, 1024),
            norm2_gain.reshape(1, 1024),
            q_gain.reshape(1, 128),
            k_gain.reshape(1, 64),
            segment.reshape(16, 128),
            inv,
            lse,
        ),
        (rows1, raw, q_t, kv, heads, w_out_all, w_all),
    )
    grads = lax.psum(grads, "tensor").astype(f32).reshape(3072, 1024)
    gate_up = grads[:2048].reshape(2, 1024, 1024)
    return (
        output,
        grad_x,
        norm1_sum.reshape(1024),
        pack[0:128].T.astype(f32),
        pack[128:192].T.astype(f32),
        pack[192:256].T.astype(f32),
        pack[417, :128].astype(f32),
        pack[417, 128:192].astype(f32),
        pack[256:384].astype(f32),
        pack[416].astype(f32),
        pack[384:416].T.astype(f32),
        gate_up[:, :, :512],
        gate_up[:, :, 512:],
        grads[2048:].reshape(2, 512, 1024),
    )


def solution(mesh):
    return jax.shard_map(
        shards,
        mesh=mesh,
        in_specs=(
            P(("dp", "ctx", "tensor"), None),
            P("dp"),
            P(),
            P(None, "tensor"),
            P(None, "tensor"),
            P(None, "tensor"),
            P("tensor"),
            P("tensor"),
            P("tensor", None),
            P(),
            P(),
            P(("dp", "ctx"), None, None),
            P(("dp", "ctx"), None, None),
            P(("dp", "ctx"), None, None),
            P(("dp", "ctx", "tensor"), None),
            P(("dp", "ctx", "tensor"), None),
        ),
        out_specs=(
            P(("dp", "ctx", "tensor"), None),
            P(("dp", "ctx", "tensor"), None),
            P(),
            P(None, "tensor"),
            P(None, "tensor"),
            P(None, "tensor"),
            P("tensor"),
            P("tensor"),
            P("tensor", None),
            P(),
            P(),
            P(("dp", "ctx"), None, None),
            P(("dp", "ctx"), None, None),
            P(("dp", "ctx"), None, None),
        ),
        check_vma=False,
    )
```

time: 860 us -> 550 us (0.64); the launches traced: 851 us -> 549 us
  waiting for transfers between devices: 477 us -> 194 us
  Pallas kernels: 108 us -> 310 us
  other arithmetic: 65.2 us -> 10.6 us
  matrix products: 53.2 us -> 0 us
  blocking collectives: 51.2 us -> 0 us
  starting transfers between devices: 33.3 us -> 0.26 us
  local copies, waits for them, and re-layouts: 48.2 us -> 18.6 us
    pallas_call x0 -> x2, Pallas kernels: none -> 220 us  [the longest x1 126 us: backward(): pl.pallas_call(backward_kernel, out_shape=(shape((128, 1024), bf), shape(...]
    reduce_scatter x3 -> x1, waiting for transfers between devices: 135 us -> 0.01 us  [shards(): lax.psum_scatter(out_part.reshape(-1, 1024), ('dp', 'ctx'), scatter_dimen...]
    psum x2 -> x1, waiting for transfers between devices: 290 us -> 194 us  [shards(): grads = lax.psum(grads, 'tensor').astype(f32).reshape(3072, 1024)]
    dot_general x23 -> x0, matrix products: 53.2 us -> none  [the longest x4 8.21 us: block_scores(): jnp.einsum('qkgd,tkd->kgqt', q_block, keys_now, preferred_element_type=jn...]
    psum x2 -> x0, blocking collectives: 51.2 us -> none  [the longest x1 38.1 us: shards(): lax.psum(norm1_sum.astype(jnp.bfloat16), ('dp', 'ctx')).astype(jnp.float32)]
    all_to_all x6 -> x0, waiting for transfers between devices: 50.8 us -> none  [the longest x5 50.8 us: from_everyone(): return lax.all_to_all(copies, axis, split_axis=0, concat_axis=0, tiled=True)]
    all_to_all x6 -> x0, starting transfers between devices: 33.1 us -> none  [the longest x5 25.6 us: from_everyone(): return lax.all_to_all(copies, axis, split_axis=0, concat_axis=0, tiled=True)]
    pallas_call x1, Pallas kernels: 108 us -> 90.6 us  [moe(): pl.pallas_call(moe_kernel, out_shape=(jax.ShapeDtypeStruct((128, 1024), f...]
  transfers between devices with their start and end apart: 11 -> 2, of which waited for: 9 -> 1; matrix products, arithmetic and copies ran while one was open for 13% -> 4% of each run, Pallas kernels for 0% -> 23%
where the time goes in v2:
time: 550 us; the launch traced here: 549 us
  Pallas kernels  310 us (56%)
  waiting for transfers between devices  194 us (35%)
  local copies, waits for them, and re-layouts  18.6 us (3%)
  between operations  15.6 us (3%)
  other arithmetic  10.6 us (2%)
    psum x1, waiting for transfers between devices, shards(): grads = lax.psum(grads, 'tensor').astype(f32).reshape(3072, 1024)  194 us
    pallas_call x1, Pallas kernels, backward(): pl.pallas_call(backward_kernel, out_shape=(shape((128, 1024), bf), shape(...  126 us
    pallas_call x1, Pallas kernels, attention(): pl.pallas_call(attention_kernel, out_shape=(shape((128, 1024), bf), shape...  93.6 us
    pallas_call x1, Pallas kernels, moe(): pl.pallas_call(moe_kernel, out_shape=(jax.ShapeDtypeStruct((128, 1024), f...  90.6 us
  transfers between devices with their start and end apart: 2, of which 1 were waited for; matrix products, arithmetic and copies ran while one was open for 4% of the time, Pallas kernels for 23%

profile of v2, /device:TPU:1, one launch (start us, length us, event | category | flops | bytes accessed | tf_op | source)
XLA Modules:
  0.0 549.4 jit_solution(10167888689770537314)
XLA Ops:
  8.0 0.0 all-reduce.2.cloned.1.call-start
  8.1 1.4 copy.33.routes_ref
  9.5 1.7 copy.32.router_ref
  11.2 1.7 copy.34.w_k_ref
  12.9 1.7 copy.35.w_v_ref
  14.6 93.6 %shard_map.281 = (bf16[128,1024]{1,0:T(8,128)(2,1)}, f32[32,128]{1,0:T(8,128)}, f32[128,1024]{1,0:T(8,128)}, bf16[8,128,1024]{2,1,0:T(8,128)(2,1)}, f32[8,256,12...) custom-call(bf16[128,1024]{1,0:T(8,128)(2,1)} %x_ref.3, ...), custom_call_target="tpu_custom_call" | custom-call | flops 5000000000 | bytes 20000000 | tf_op jit(solution)/shard_map/pallas_call | solution.py:838
  108.2 90.6 %shard_map.282 = (f32[128,1024]{1,0:T(8,128)}, f32[32,128]{1,0:T(8,128)}, bf16[16,128,1024]{2,1,0:T(8,128)(2,1)}, bf16[24,128,1024]{2,1,0:T(8,128)(2,1)}, bf16[8,256,1024]{2,1,0:T(8,128)(2,1)}) custom-call(bf16[128,1024]{1,0:T(8,128)(2,1)} %get-tuple-element.36.rows_ref.rows2_ref, f32[32,128]{1,0:T(8,128)} %get-tuple-element.37.gate_ref.gates_ref, ...), custom_call_target="tpu_custom_call" | custom-call | flops 20000000000 | bytes 30000000 | tf_op jit(solution)/shard_map/pallas_call | solution.py:432
  198.8 0.0 all-reduce.2.cloned.1.call-update
  198.8 0.2 reduce-scatter.2.cloned.1.call-start
  199.1 0.3 reduce-scatter.2.cloned.1.call-update
  199.4 126.3 %shard_map.283 = (bf16[128,1024]{1,0:T(8,128)(2,1)}, f32[8,128]{1,0:T(8,128)}, bf16[512,1024]{1,0:T(8,128)(2,1)}) custom-call(bf16[128,1024]{1,0:T(8,128)(2,1)} %x_ref.3, bf16[128,1024]{1,0:T(8,128)(2,1)} %dy_ref.3, f32[128,1024]{1,0:T(8,128)} %get-tuple-element.41.d_rows_ref, f32[32,128]{1,0:T(8,128)} %get-tuple-element.42.d_gate_ref, ...), custom_call_target="tpu_custom_call" | custom-call | flops 10000000000 | bytes 20000000 | tf_op jit(solution)/shard_map/pallas_call | solution.py:1403
  325.7 1.9 slice_convert_fusion
  327.7 1.0 copy.37
  328.7 1.2 bitcast_convert_fusion
  329.8 1.2 bitcast_convert_fusion.1
  331.0 1.3 slice_convert_fusion.1
  332.3 1.5 convert_bitcast_fusion.3
  333.8 1.8 convert_bitcast_fusion.1
  335.6 193.6 %all-reduce.2.cloned.1.call-done = bf16[24,128,1024]{2,1,0:T(8,128)(2,1)} async-done(((bf16[24,128,1024]{2,1,0:T(8,128)(2,1)}), bf16[24,128,1024]{2,1,0:T(8,128)(2,1)}) %all-reduce.2.cloned.1.call-update) | async-done | bytes 6291472 | tf_op jit(solution)/shard_map/psum | solution.py:1527
  529.3 4.2 slice.53
  533.5 0.0 copy-done
  533.5 1.0 slice.50
  534.5 0.0 copy-start.1
  534.5 0.0 copy-start.2
  534.5 0.0 copy-start.3
  534.6 4.4 fusion
  539.0 0.0 copy-done.1
  539.0 1.7 add_convert_fusion
  540.7 0.0 copy-done.2
  540.7 0.7 copy.41
  541.4 0.0 copy-done.3
  541.4 0.6 copy.42
  (2 shorter events, 0.0 us)
Async XLA Ops:
  8.0 521.2 %all-reduce.2.cloned.1.call-start = ((), (), s32[]{:S(2)}) async-start(), calls=%async_computation.2 | async-start | bytes 12582912 | tf_op jit(solution)/shard_map/psum | solution.py:1527
  198.8 340.2 %reduce-scatter.2.cloned.1.call-start = ((), (), s32[]{:S(2)}) async-start(), calls=%async_computation.1 | async-start | bytes 4456448 | tf_op jit(solution)/shard_map/reduce_scatter | solution.py:1503
  529.3 4.2 copy-start
  534.5 4.5 copy-start.1
  534.5 6.2 %copy-start.2 = (bf16[128,1024]{1,0:T(8,128)(2,1)S(1)}, bf16[128,1024]{1,0:T(8,128)(2,1)}, u32[]{:S(2)}) copy-start(bf16[128,1024]{1,0:T(8,128)(2,1)} %get-tuple-element.91) | copy-start | bytes 786436
  534.5 6.9 %copy-start.3 = (f32[8,128]{1,0:T(8,128)S(1)}, f32[8,128]{1,0:T(8,128)}, u32[]{:S(2)}) copy-start(f32[8,128]{1,0:T(8,128)} %get-tuple-element.53) | copy-start | bytes 12292
Sparse Core Ops, SparseCore 0:
  198.9 330.2 all-reduce.1
Sparse Core Ops, SparseCore 1:
  203.3 140.6 reduce-scatter.1

commit v3 on v2

--- a/solution.py
+++ b/solution.py
@@ -49,18 +49,17 @@
     )
 
 
-def x_offset(a):
-    return a + a // 2 - 2 * (a // 3)
-
-
-def back_place(a):
-    return (2 * a) % 3 + 3 * (a // 3)
-
-
 def across(a, b, flip):
     dp, ctx = lax.axis_index("dp"), lax.axis_index("ctx")
     x, y = dp % 4, dp // 4
-    return ((y + b) % 2) * 4 + (x + x_offset(a)) % 4, (ctx + flip) % 2
+    odd = a % 2
+    by_x = odd * (1 + 2 * b) + (1 - odd) * a
+    by_y = (1 - odd) * b + odd * (1 - a // 2)
+    return ((y + by_y) % 2) * 4 + (x + by_x) % 4, (ctx + flip) % 2
+
+
+def opposite(a, b):
+    return b + (a % 2) * (1 - 2 * b)
 
 
 def moe_kernel(
@@ -86,7 +85,11 @@
     out_all,
     din_all,
     sib,
-    summed,
+    rs_a,
+    rs_b,
+    rs_c,
+    rs_d,
+    rs_e,
     dg_out,
     dg_in,
     places,
@@ -100,6 +103,8 @@
     load_sem,
     ag_send,
     ag_recv,
+    g_send,
+    g_recv,
     sib_send,
     sib_recv,
     rs_send,
@@ -113,7 +118,6 @@
     tensor = lax.axis_index("tensor")
     dp, ctx = lax.axis_index("dp"), lax.axis_index("ctx")
     me = dp * 2 + ctx
-    kinds = (rows_all, gate_all)
 
     def to(a, b, flip):
         d, c = across(a, b, flip)
@@ -149,60 +153,46 @@
         pl.semaphore_signal(barrier, inc=1, device_id=side(i), device_id_type=MESH)
     pl.semaphore_wait(barrier, 22)
 
-    def own_push(k, a, b, flip):
+    right, left, partner = to(3, 0, 0), to(3, 1, 0), to(0, 1, 0)
+    sibling = to(0, 0, 1)
+    low, high = pl.ds(0, 64), pl.ds(64, 64)
+
+    def hop(n):
+        src, dst, device = (
+            (rows_all.at[0], rows_all.at[14], right),
+            (rows_all.at[0], rows_all.at[12], left),
+            (rows_all.at[0], rows_all.at[2], partner),
+            (rows_all.at[14, low], rows_all.at[8, low], right),
+            (rows_all.at[12, high], rows_all.at[8, high], left),
+            (rows_all.at[2], rows_all.at[6], right),
+            (rows_all.at[2], rows_all.at[4], left),
+            (rows_all.at[8], rows_all.at[10], partner),
+        )[n]
+        return copy_to(src, dst, ag_send.at[n], ag_recv.at[n], device)
+
+    def relay(ci):
+        r = 2 * ci
+        return copy_to(
+            rows_all.at[r], rows_all.at[r + 1], ag_send.at[8 + ci], ag_recv.at[8 + ci], sibling
+        )
+
+    def gate_push(a, b, flip):
         r = 4 * a + 2 * b + flip
-        back = 4 * back_place(a) + 2 * b + flip
-        return pltpu.make_async_remote_copy(
-            src_ref=kinds[k].at[0],
-            dst_ref=kinds[k].at[back],
-            send_sem=ag_send.at[k, r],
-            recv_sem=ag_recv.at[k, back],
-            device_id=to(a, b, flip),
-            device_id_type=MESH,
-        )
-
-    def relay(k, r):
-        return pltpu.make_async_remote_copy(
-            src_ref=kinds[k].at[r],
-            dst_ref=kinds[k].at[r + 1],
-            send_sem=ag_send.at[k, r + 1],
-            recv_sem=ag_recv.at[k, r + 1],
-            device_id=to(0, 0, 1),
-            device_id_type=MESH,
-        )
-
-    def arrival(k, r):
-        return pltpu.make_async_remote_copy(
-            src_ref=kinds[k].at[r],
-            dst_ref=kinds[k].at[r],
-            send_sem=ag_send.at[k, r],
-            recv_sem=ag_recv.at[k, r],
-            device_id=to(0, 0, 1),
-            device_id_type=MESH,
+        back = 4 * a + 2 * opposite(a, b) + flip
+        return copy_to(
+            gate_all.at[0], gate_all.at[back], g_send.at[r], g_recv.at[back], to(a, b, flip)
         )
 
     rows_all[0] = rows_ref[...]
     gate_all[0] = gate_ref[...]
-    for k in range(2):
-        own_push(k, 0, 0, 1).start()
-    for k in range(2):
-        for a in range(4):
-            for b in range(2):
-                if (a, b) != (0, 0):
-                    own_push(k, a, b, 0).start()
+    for n in range(3):
+        hop(n).start()
+    relay(0).start()
+    for r in range(1, 16):
+        gate_push(r // 4, (r // 2) % 2, r % 2).start()
 
     acc_gu[...] = jnp.zeros_like(acc_gu)
     acc_dn[...] = jnp.zeros_like(acc_dn)
-
-    def arrive(a, first):
-        for b in range(2):
-            if not (first and b == 0):
-                for k in range(2):
-                    arrival(k, 4 * a + 2 * b).wait_recv()
-                    relay(k, 4 * a + 2 * b).start()
-        for b in range(2):
-            for k in range(2):
-                arrival(k, 4 * a + 2 * b + 1).wait_recv()
 
     half = pl.ds(pl.multiple_of(ctx * 128, 128), 128)
 
@@ -228,30 +218,46 @@
     w_own = pltpu.make_async_copy(w_t_ref, w_all_ref.at[tensor], load_sem.at[7])
     w_own.start()
 
-    def sib_push(ci, r):
-        return pltpu.make_async_remote_copy(
-            src_ref=din_all.at[r],
-            dst_ref=sib.at[ci],
-            send_sem=sib_send.at[ci],
-            recv_sem=sib_recv.at[ci],
-            device_id=to(0, 0, 1),
-            device_id_type=MESH,
+    def sib_push(ci):
+        return copy_to(
+            din_all.at[2 * ci + 1], sib.at[ci], sib_send.at[ci], sib_recv.at[ci], sibling
         )
 
-    def rs_push(a, b):
-        back = 2 * back_place(a) + b
-        return pltpu.make_async_remote_copy(
-            src_ref=din_all.at[4 * a + 2 * b],
-            dst_ref=summed.at[back],
-            send_sem=rs_send.at[2 * a + b],
-            recv_sem=rs_recv.at[back],
-            device_id=to(a, b, 0),
-            device_id_type=MESH,
-        )
+    def rs_hop(n):
+        src, dst, device = (
+            (din_all.at[4], rs_a.at[0], right),
+            (din_all.at[6], rs_a.at[1], left),
+            (din_all.at[10], rs_b, partner),
+            (din_all.at[2], rs_c, partner),
+            (din_all.at[8, low], rs_d.at[0], right),
+            (din_all.at[8, high], rs_d.at[1], left),
+            (din_all.at[12], rs_e.at[0], right),
+            (din_all.at[14], rs_e.at[1], left),
+        )[n]
+        return copy_to(src, dst, rs_send.at[n], rs_recv.at[n], device)
+
+    def rs_go(*hops):
+        for n in hops:
+            rs_hop(n).start()
+
+    def rs_got(*hops):
+        for n in hops:
+            rs_hop(n).wait_recv()
+
+    def plus(r, rows, *parts):
+        total = din_all[r, rows].astype(jnp.float32)
+        for part in parts:
+            total = total + part.astype(jnp.float32)
+        din_all[r, rows] = total.astype(jnp.bfloat16)
+
+    def post(*cis):
+        for ci in cis:
+            sib_push(ci).wait_recv()
+            plus(2 * ci, slice(None), sib[ci])
 
     def dg_push(a, b, flip):
         r = 4 * a + 2 * b + flip
-        back = 4 * back_place(a) + 2 * b + flip
+        back = 4 * a + 2 * opposite(a, b) + flip
         return pltpu.make_async_remote_copy(
             src_ref=dg_out.at[r],
             dst_ref=dg_in.at[back],
@@ -260,17 +266,6 @@
             device_id=to(a, b, flip),
             device_id_type=MESH,
         )
-
-    def post(a):
-        for b in range(2):
-            ci, r = 2 * a + b, 4 * a + 2 * b
-            sib_push(ci, r + 1).wait_recv()
-            total = din_all[r].astype(jnp.float32) + sib[ci].astype(jnp.float32)
-            din_all[r] = total.astype(jnp.bfloat16)
-
-            @pl.when(ci > 0)
-            def _():
-                rs_push(a, b).start()
 
     expert_row = lax.broadcasted_iota(jnp.int32, (32, 128), 0)
     slot_row = lax.broadcasted_iota(jnp.int32, (64, 128), 0).astype(jnp.float32)
@@ -336,7 +331,7 @@
         place = places[q]
         d, c = across(a, b, flip)
         o = jnp.concatenate([o_buf[0, at, :], o_buf[1, at, :]], 0)
-        out_all[d * 2 + c] = dot_tn(place, o).astype(jnp.bfloat16)
+        out_all[c * 8 + d] = dot_tn(place, o).astype(jnp.bfloat16)
         i = jnp.concatenate([i_buf[0, at, :], i_buf[1, at, :]], 0)
         din_all[r] = dot_tn(place, i).astype(jnp.bfloat16)
         hits = place.astype(jnp.float32)
@@ -350,36 +345,87 @@
         def _():
             dg_push(a, b, flip).start()
 
-    arrive(0, True)
+    for n, ci in ((0, 7), (1, 6)):
+        hop(n).wait_recv()
+        hop(3 + n).start()
+        relay(ci).start()
+    hop(2).wait_recv()
+    hop(5).start()
+    hop(6).start()
+    relay(1).start()
+    relay(0).wait_recv()
+    for r in range(1, 16):
+        gate_push(r // 4, (r // 2) % 2, r % 2).wait_recv()
     for load in loads:
         load.wait()
+    relay(1).wait_recv()
 
     def step(a, carry):
         lax.fori_loop(0, 4, lambda q, c: (gather(a, q), c)[1], 0)
+
+        @pl.when(a == 1)
+        def _():
+            post(0, 1)
+
+        @pl.when(a == 2)
+        def _():
+            post(2, 3)
+            rs_go(0, 1)
+
+        @pl.when(a == 3)
+        def _():
+            post(4, 5)
+            rs_go(2)
+            rs_got(0, 1)
+            plus(2, slice(None), rs_a[0], rs_a[1])
+            rs_go(3)
+
         lax.fori_loop(0, 2, lambda j, c: (expert(j), c)[1], 0)
         lax.fori_loop(0, 4, lambda q, c: (spread(a, q), c)[1], 0)
         for b in range(2):
-            sib_push(2 * a + b, 4 * a + 2 * b + 1).start()
-
-        @pl.when(a > 0)
+            sib_push(2 * a + b).start()
+
+        @pl.when(a == 0)
         def _():
-            post(a - 1)
-
-        @pl.when(a < 3)
+            hop(3).wait_recv()
+            hop(4).wait_recv()
+            hop(7).start()
+            relay(4).start()
+            for n, ci in ((5, 3), (6, 2)):
+                hop(n).wait_recv()
+                relay(ci).start()
+            for ci in (2, 3):
+                relay(ci).wait_recv()
+
+        @pl.when(a == 1)
         def _():
-            arrive(a + 1, False)
+            hop(7).wait_recv()
+            relay(5).start()
+            for ci in (4, 5, 6, 7):
+                relay(ci).wait_recv()
 
         return carry
 
     lax.fori_loop(0, 4, step, 0)
+    rs_got(2)
+    plus(8, slice(None), rs_b[...])
+    rs_go(4, 5)
+    post(6, 7)
+    rs_got(4)
+    plus(12, low, rs_d[0])
+    rs_go(6)
+    rs_got(5)
+    plus(14, high, rs_d[1])
+    rs_go(7)
     for i in range(1, 8):
         t = (tensor + i) % 8
         w_arrival(t, ctx).wait_recv()
         w_relay(t).start()
-    post(3)
-    for k in range(2):
-        for r in range(1, 16):
-            arrival(k, r).wait_send()
+    for n in range(8):
+        hop(n).wait_send()
+        relay(n).wait_send()
+    for r in range(1, 16):
+        gate_push(r // 4, (r // 2) % 2, r % 2).wait_send()
     stores = []
     for j in range(2):
         for h in range(8):
@@ -407,14 +453,13 @@
         for j in range(2):
             d_gate = jnp.where(expert_row == (d * 2 + c) * 2 + j, got[j : j + 1], d_gate)
     d_gate_ref[...] = d_gate
-    total = din_all[0].astype(jnp.float32)
     for ci in range(8):
-        sib_push(ci, 2 * ci + 1).wait_send()
-        if ci > 0:
-            rs_push(ci // 2, ci % 2).wait()
-    for ci in range(1, 8):
-        total = total + summed[ci].astype(jnp.float32)
-    d_rows_ref[...] = total
+        sib_push(ci).wait_send()
+    rs_got(3, 6, 7)
+    total = din_all[0].astype(jnp.float32) + rs_c[...].astype(jnp.float32)
+    d_rows_ref[...] = total + rs_e[0].astype(jnp.float32) + rs_e[1].astype(jnp.float32)
+    for n in range(8):
+        rs_hop(n).wait_send()
     for i in range(1, 8):
         t = (tensor + i) % 8
         w_arrival(t, 1 - ctx).wait_recv()
@@ -451,7 +496,11 @@
             pltpu.VMEM((16, 128, 1024), bf),
             pltpu.VMEM((16, 128, 1024), bf),
             pltpu.VMEM((8, 128, 1024), bf),
-            pltpu.VMEM((8, 128, 1024), bf),
+            pltpu.VMEM((2, 128, 1024), bf),
+            pltpu.VMEM((128, 1024), bf),
+            pltpu.VMEM((128, 1024), bf),
+            pltpu.VMEM((2, 64, 1024), bf),
+            pltpu.VMEM((2, 128, 1024), bf),
             pltpu.VMEM((16, 8, 128), f32),
             pltpu.VMEM((16, 8, 128), f32),
             pltpu.VMEM((4, 128, 128), bf),
@@ -463,8 +512,10 @@
             pltpu.VMEM((2, 256, 1), f32),
             pltpu.VMEM((2, 256, 1), f32),
             sem((8,)),
-            sem((2, 16)),
-            sem((2, 16)),
+            sem((16,)),
+            sem((16,)),
+            sem((16,)),
+            sem((16,)),
             sem((8,)),
             sem((8,)),
             sem((8,)),
@@ -516,8 +567,6 @@
     dy_all,
     w_all,
     w_q,
-    w_k,
-    w_v,
     w_t,
     raw,
     table,
@@ -558,8 +607,8 @@
     sibling = (dp, 1 - ctx, me)
     loads = [
         pltpu.make_async_copy(w_q_ref, w_q, load_sem.at[0]),
-        pltpu.make_async_copy(w_k_ref, w_k, load_sem.at[1]),
-        pltpu.make_async_copy(w_v_ref, w_v, load_sem.at[2]),
+        pltpu.make_async_copy(w_k_ref, w_t.at[pl.ds(128, 64)], load_sem.at[1]),
+        pltpu.make_async_copy(w_v_ref, w_t.at[pl.ds(192, 64)], load_sem.at[2]),
         pltpu.make_async_copy(w_out_ref, w_all.at[me], load_sem.at[3]),
         pltpu.make_async_copy(table_ref.at[ctx], table, load_sem.at[4]),
     ]
@@ -579,39 +628,60 @@
     dy_all[0] = dy_ref[...]
     pl.semaphore_wait(barrier, 15)
 
-    def h_push(i):
-        return copy_to(h_all.at[me], h_all.at[me], h_send.at[i], h_recv.at[me], side(i))
-
-    def h_arrival(t):
-        return copy_to(h_all.at[t], h_all.at[t], h_send.at[0], h_recv.at[t], sibling)
-
-    def dy_push(a, b):
-        back = 4 * back_place(a) + 2 * b
+    z, y = me // 2, me % 2
+    up, down, pair = (
+        (dp, ctx, ((z + 1) % 4) * 2 + y),
+        (dp, ctx, ((z + 3) % 4) * 2 + y),
+        (dp, ctx, z * 2 + 1 - y),
+    )
+    low, high = pl.ds(0, 64), pl.ds(64, 64)
+
+    def block_at(k, flip):
+        return ((z + k) % 4) * 2 + (y + flip) % 2
+
+    def h_hop(n):
+        place, device = (
+            (h_all.at[me], up),
+            (h_all.at[me], down),
+            (h_all.at[me], pair),
+            (h_all.at[block_at(3, 0), low], up),
+            (h_all.at[block_at(1, 0), high], down),
+            (h_all.at[block_at(0, 1)], up),
+            (h_all.at[block_at(0, 1)], down),
+            (h_all.at[block_at(2, 0)], pair),
+        )[n]
+        return copy_to(place, place, h_send.at[n], h_recv.at[n], device)
+
+    right, left, partner = to(3, 0, 0), to(3, 1, 0), to(0, 1, 0)
+
+    def dy_hop(n):
+        src, dst, device = (
+            (dy_all.at[0], dy_all.at[14], right),
+            (dy_all.at[0], dy_all.at[12], left),
+            (dy_all.at[0], dy_all.at[2], partner),
+            (dy_all.at[14, low], dy_all.at[8, low], right),
+            (dy_all.at[12, high], dy_all.at[8, high], left),
+            (dy_all.at[2], dy_all.at[6], right),
+            (dy_all.at[2], dy_all.at[4], left),
+            (dy_all.at[8], dy_all.at[10], partner),
+        )[n]
+        return copy_to(src, dst, dy_send.at[n], dy_recv.at[n], device)
+
+    def dy_relay(ci):
+        r = 2 * ci
         return copy_to(
-            dy_all.at[0], dy_all.at[back], dy_send.at[4 * a + 2 * b], dy_recv.at[back], to(a, b, 0)
+            dy_all.at[r], dy_all.at[r + 1], dy_send.at[8 + ci], dy_recv.at[8 + ci], sibling
         )
 
-    def dy_relay(r):
-        return copy_to(
-            dy_all.at[r], dy_all.at[r + 1], dy_send.at[r + 1], dy_recv.at[r + 1], sibling
-        )
-
-    def dy_arrival(r):
-        return copy_to(dy_all.at[r], dy_all.at[r], dy_send.at[r], dy_recv.at[r], sibling)
-
-    for i in (1, 7, 2, 6, 3, 5, 4):
-        h_push(i).start()
+    for n in range(3):
+        h_hop(n).start()
+    for n in range(3):
+        dy_hop(n).start()
     dy_relay(0).start()
-    for a in range(4):
-        for b in range(2):
-            if (a, b) != (0, 0):
-                dy_push(a, b).start()
 
     for load in loads:
         load.wait()
     w_t[0:128, :] = jnp.transpose(w_q[...])
-    w_t[128:192, :] = jnp.transpose(w_k[...])
-    w_t[192:256, :] = jnp.transpose(w_v[...])
     seg = segment_ref[...]
     start = jnp.zeros((16, 128), f32)
     for s in range(1, 8):
@@ -622,13 +692,7 @@
     for t in range(8):
         starts[0:1, 128 * t : 128 * t + 128] = start[t : t + 1]
 
-    def project(i, carry):
-        t = (me + i) % 8
-
-        @pl.when(i > 0)
-        def _():
-            h_arrival(t).wait_recv()
-
+    def project(t):
         value = dot_nt(w_t[...], h_all[t])
         raw[t] = value
         square = value * value
@@ -638,9 +702,23 @@
             jnp.zeros((6, 128), f32),
         ]
         stat[t] = jnp.concatenate(sums, 0)
-        return carry
-
-    lax.fori_loop(0, 8, project, 0)
+
+    project(me)
+    for n in range(2):
+        h_hop(n).wait_recv()
+        h_hop(3 + n).start()
+    h_hop(2).wait_recv()
+    h_hop(5).start()
+    h_hop(6).start()
+    for k, flip in ((3, 0), (1, 0), (0, 1)):
+        project(block_at(k, flip))
+    h_hop(3).wait_recv()
+    h_hop(4).wait_recv()
+    h_hop(7).start()
+    project(block_at(2, 0))
+    for n, k in ((5, 3), (6, 1), (7, 2)):
+        h_hop(n).wait_recv()
+        project(block_at(k, 1))
     stats[me] = stat[...]
 
     def s_push(i):
@@ -670,6 +748,14 @@
         half = w_all.at[t, pl.ds(pl.multiple_of(c * 64, 64), 64)]
         return copy_to(half, half, w_send.at[0], w_recv.at[t, c], sibling)
 
+    for n, ci in ((0, 7), (1, 6)):
+        dy_hop(n).wait_recv()
+        dy_hop(3 + n).start()
+        dy_relay(ci).start()
+    dy_hop(2).wait_recv()
+    dy_hop(5).start()
+    dy_hop(6).start()
+    dy_relay(1).start()
     for i in (1, 7, 2, 6, 3, 5, 4):
         w_push(i).start()
     gain_q = column(q_gain_ref[...])
@@ -753,6 +839,10 @@
         k_sib[at, :] = jnp.transpose(kv_sib[0:64, at])
         return carry
 
+    dy_hop(3).wait_recv()
+    dy_hop(4).wait_recv()
+    dy_hop(7).start()
+    dy_relay(4).start()
     lax.fori_loop(0, 8, straighten, 0)
     lax.fori_loop(0, 8, attend, 0)
 
@@ -784,12 +874,9 @@
 
     lax.fori_loop(1, 8, pass_on, 0)
 
-    def pass_dy(c, carry):
-        dy_arrival(2 * c).wait_recv()
-        dy_relay(2 * c).start()
-        return carry
-
-    lax.fori_loop(1, 8, pass_dy, 0)
+    for n, ci in ((5, 3), (6, 2), (7, 5)):
+        dy_hop(n).wait_recv()
+        dy_relay(ci).start()
     for i in range(1, 8):
         t = (me + i) % 8
         w_arrival(t, 1 - ctx).wait_recv()
@@ -802,9 +889,9 @@
     inv_two = lax.rsqrt(jnp.mean(resid * resid, -1, keepdims=True) + EPS)
     rows2 = (resid * inv_two * norm2_ref[...]).astype(bf)
     rows2_ref[...] = rows2
-    logits = jnp.transpose(jnp.dot(rows2, router_ref[...], preferred_element_type=f32))
+    logits = dot_nt(router_ref[...], rows2)
     expert_row = lax.broadcasted_iota(jnp.int32, (32, 128), 0)
-    routes = jnp.transpose(routes_ref[...])
+    routes = routes_ref[...]
     named = routes[0:1] == expert_row
     for k in range(1, 8):
         named = named | (routes[k : k + 1] == expert_row)
@@ -812,19 +899,19 @@
     weight = jnp.where(named, jnp.exp(chosen - jnp.max(chosen, 0, keepdims=True)), 0.0)
     gates_ref[...] = weight / jnp.sum(weight, 0, keepdims=True)
 
-    for c in range(8):
-        dy_arrival(2 * c + 1).wait_recv()
+    for ci in range(8):
+        dy_relay(ci).wait_recv()
     store_dy = pltpu.make_async_copy(dy_all, dy_all_ref, store_sem.at[7])
     store_dy.start()
     for i in range(1, 8):
-        h_push(i).wait_send()
         s_push(i).wait_send()
         w_push(i).wait_send()
         w_relay((me + i) % 8).wait_send()
         o_push(i).wait_send()
-        dy_push(i // 2, i % 2).wait_send()
-    for c in range(8):
-        dy_relay(2 * c).wait_send()
+    for n in range(8):
+        h_hop(n).wait_send()
+        dy_hop(n).wait_send()
+        dy_relay(n).wait_send()
     for store in [store_rows, store_raw, store_wt, store_w, store_dy] + stores:
         store.wait()
 
@@ -859,8 +946,6 @@
             pltpu.VMEM((16, 128, 1024), bf),
             pltpu.VMEM((8, 128, 1024), bf),
             pltpu.VMEM((1024, 128), bf),
-            pltpu.VMEM((1024, 64), bf),
-            pltpu.VMEM((1024, 64), bf),
             pltpu.VMEM((256, 1024), bf),
             pltpu.VMEM((8, 256, 128), f32),
             pltpu.VMEM((2, 32, 1024), f32),
@@ -902,11 +987,11 @@
         q_gain.reshape(1, 128),
         k_gain.reshape(1, 64),
         norm2.reshape(1, 1024),
-        router,
-        routes,
+        router.T,
+        routes.T,
         w_q,
-        w_k,
-        w_v,
+        w_k.T,
+        w_v.T,
         w_out,
         table,
     )
@@ -935,10 +1020,14 @@
     heads_ref,
     w_out_ref,
     w_all_ref,
+    grads_ref,
+    out_part_ref,
     table_ref,
     grad_x_ref,
     norm1_out_ref,
     pack_ref,
+    output_ref,
+    reduced_ref,
     rows1,
     raw,
     q_t,
@@ -1003,6 +1092,22 @@
     m_send,
     m_recv,
     ns_sem,
+    grads,
+    reduced,
+    ra1,
+    ra2,
+    ra4,
+    rb1,
+    rb2,
+    rb3,
+    r_send,
+    r_recv,
+    out_own,
+    out_sib,
+    out_in,
+    os_sem,
+    out_send,
+    out_recv,
 ):
     f32, bf = jnp.float32, jnp.bfloat16
     dp, ctx, me = lax.axis_index("dp"), lax.axis_index("ctx"), lax.axis_index("tensor")
@@ -1010,6 +1115,154 @@
 
     def side(i):
         return (dp, ctx, (me + i) % 8)
+
+    z, y = me // 2, me % 2
+    other = 1 - y
+    up, down, across_y = (
+        (dp, ctx, ((z + 1) % 4) * 2 + y),
+        (dp, ctx, ((z + 3) % 4) * 2 + y),
+        (dp, ctx, z * 2 + other),
+    )
+
+    def unit(k, c, first=0):
+        return pl.ds(pl.multiple_of((first + ((z + k) % 4) * 2 + c) * 192, 64), 192)
+
+    def half_unit(k, c, part):
+        return pl.ds(pl.multiple_of((8 + ((z + k) % 4) * 2 + c) * 192 + part * 96, 32), 96)
+
+    def hop(n):
+        if n < 2:
+            src, dst = grads.at[unit(2, n)], ra1.at[n]
+            to = (up, down)[n]
+        elif n < 4:
+            src, dst, to = grads.at[unit(1, n - 2)], ra2.at[0, n - 2], up
+        elif n < 6:
+            src, dst, to = grads.at[unit(3, n - 4)], ra2.at[1, n - 4], down
+        elif n == 6:
+            src, dst, to = grads.at[unit(0, other)], ra4, across_y
+        elif n == 7:
+            src = dst = reduced.at[unit(0, y)]
+            to = across_y
+        elif n < 12:
+            src = dst = reduced.at[unit(0, n % 2)]
+            to = up if n < 10 else down
+        elif n == 12:
+            src = dst = reduced.at[unit(3, 0)]
+            to = up
+        elif n == 13:
+            src = dst = reduced.at[unit(1, 1)]
+            to = down
+        elif n < 18:
+            src, dst, to = grads.at[unit(n - 14, other, 8)], rb1.at[(z + n - 14) % 4], across_y
+        elif n < 20:
+            src, dst, to = grads.at[half_unit(2, y, n - 18)], rb2.at[n - 18], (up, down)[n - 18]
+        elif n == 20:
+            src, dst, to = grads.at[unit(1, y, 8)], rb3.at[0], up
+        elif n == 21:
+            src, dst, to = grads.at[unit(3, y, 8)], rb3.at[1], down
+        elif n < 24:
+            src = dst = reduced.at[unit(0, y, 8)]
+            to = (up, down)[n - 22]
+        elif n == 24:
+            src = dst = reduced.at[half_unit(3, y, 0)]
+            to = up
+        elif n == 25:
+            src = dst = reduced.at[half_unit(1, y, 1)]
+            to = down
+        else:
+            src = dst = reduced.at[unit((0, 3, 1, 2)[n - 26], y, 8)]
+            to = across_y
+        return copy_to(src, dst, r_send.at[n], r_recv.at[n], to)
+
+    def go(*hops):
+        for n in hops:
+            hop(n).start()
+
+    def got(*hops):
+        for n in hops:
+            hop(n).wait_recv()
+
+    def plus(place, *parts):
+        total = grads[place, :].astype(jnp.float32)
+        for part in parts:
+            total = total + part.astype(jnp.float32)
+        grads[place, :] = total.astype(jnp.bfloat16)
+
+    def reduce_0():
+        go(0, 1, 14, 15, 16, 17, 3, 4)
+
+    def reduce_1():
+        got(0)
+        plus(unit(1, 0), ra1[0])
+        go(2)
+        got(1)
+        plus(unit(3, 1), ra1[1])
+        go(5)
+
+    def reduce_2():
+        for k in (2, 1, 3, 0):
+            got(14 + k)
+            plus(unit(k, y, 8), rb1[(z + k) % 4])
+            if k == 2:
+                go(18, 19)
+
+    def reduce_3():
+        got(2, 3, 4, 5)
+        for c in range(2):
+            plus(unit(0, c), ra2[0, c], ra2[1, c])
+        go(6)
+
+    def reduce_4():
+        got(18, 19)
+        plus(half_unit(1, y, 0), rb2[0])
+        plus(half_unit(3, y, 1), rb2[1])
+        go(20, 21)
+
+    def reduce_5():
+        got(6)
+        plus(unit(0, y), ra4[...])
+        reduced[unit(0, y), :] = grads[unit(0, y), :]
+        go(7)
+
+    def reduce_6():
+        got(20, 21)
+        plus(unit(0, y, 8), rb3[0], rb3[1])
+        reduced[unit(0, y, 8), :] = grads[unit(0, y, 8), :]
+        go(22, 23, 26)
+
+    def reduce_7():
+        got(7)
+        go(8, 11, 9, 10)
+
+    def reduce_8():
+        got(22)
+        go(24, 27)
+        got(23)
+        go(25, 28)
+        got(8)
+        go(12)
+        got(11)
+        go(13)
+
+    def reduce_9():
+        got(24, 25)
+        go(29)
+
+    def reduce_10():
+        got(9, 10, 12, 13, 26, 27, 28, 29)
+        for n in range(30):
+            hop(n).wait_send()
+
+    theirs_out = out_part_ref.at[pl.ds(pl.multiple_of((1 - ctx) * 8, 8), 8)]
+    os_push = copy_to(theirs_out, out_sib, os_sem.at[0], os_sem.at[1], sibling)
+
+    def out_push(i):
+        return copy_to(
+            out_own.at[(dp + i) % 8], out_in.at[dp], out_send.at[i], out_recv.at[dp], chip(i)
+        )
+
+    def out_arrival(d):
+        return copy_to(out_in.at[d], out_in.at[d], out_send.at[0], out_recv.at[d], sibling)
 
     def chip(i):
         return ((dp + i) % 8, ctx, me)
@@ -1022,6 +1275,9 @@
     ]
     loads.append(pltpu.make_async_copy(w_all_ref, w_all, load_sem.at[7]))
     loads.append(pltpu.make_async_copy(table_ref.at[ctx], table, load_sem.at[8]))
+    loads.append(pltpu.make_async_copy(grads_ref, grads, load_sem.at[9]))
+    own_blocks = out_part_ref.at[pl.ds(pl.multiple_of(ctx * 8, 8), 8)]
+    loads.append(pltpu.make_async_copy(own_blocks, out_own, load_sem.at[10]))
     for load in loads:
         load.start()
     barrier = pltpu.get_barrier_semaphore()
@@ -1035,7 +1291,7 @@
     d_normed = d_rows_ref[...] + lax.dot_general(
         jnp.transpose(d_logits),
         router_ref[...].astype(f32),
-        (((1,), (1,)), ((), ())),
+        (((1,), (0,)), ((), ())),
         preferred_element_type=f32,
         precision=lax.Precision.HIGHEST,
     )
@@ -1090,12 +1346,15 @@
     def a_arrival(t):
         return copy_to(datt_all.at[t], datt_all.at[t], a_send.at[0], a_recv.at[t], sibling)
 
+    loads[9].wait()
+    reduce_0()
+    os_push.start()
     for i in range(1, 8):
         t_push(i).start()
     for i in (1, 7, 2, 6, 3, 5, 4):
         a_push(i).start()
 
-    for n in (0, 1, 2, 3, 4, 5, 7, 8):
+    for n in (0, 1, 2, 3, 4, 5, 7, 8, 10):
         loads[n].wait()
     seg = segment_ref[...]
     start = jnp.zeros((16, 128), f32)
@@ -1144,6 +1403,7 @@
         return carry
 
     lax.fori_loop(0, 8, lay_dh, 0)
+    reduce_1()
     key_row = lax.broadcasted_iota(jnp.int32, (256, 512), 0).astype(f32)
     query_lane = (lax.broadcasted_iota(jnp.int32, (256, 512), 1) % 256).astype(f32)
     base = (ctx * 1024).astype(f32)
@@ -1177,6 +1437,16 @@
 
     lax.fori_loop(0, 8, upright, 0)
     dkv_push.start()
+    os_push.wait()
+
+    def add_sib(d, carry):
+        out_own[d] = (out_own[d].astype(f32) + out_sib[d].astype(f32)).astype(bf)
+        return carry
+
+    lax.fori_loop(0, 8, add_sib, 0)
+    for i in range(1, 8):
+        out_push(i).start()
+    reduce_3()
 
     def within(i, carry):
         def full(j, c):
@@ -1188,6 +1458,7 @@
         return carry
 
     lax.fori_loop(0, 4, within, 0)
+    reduce_2()
     gain_q = column(q_gain_ref[...])
     gain_k = column(jnp.concatenate([k_gain_ref[...], jnp.zeros((1, 64), f32)], 1))[:64]
     dkv_push.wait()
@@ -1231,11 +1502,14 @@
 
     for i in range(1, 8):
         s_push(i).start()
+    reduce_4()
+    reduce_5()
     for i in range(1, 8):
         a_arrival((me + i) % 8).wait_recv()
     pack[256:384, :] = jnp.dot(
         heads2[...], datt_all[...].reshape(1024, 1024), preferred_element_type=f32
     ).astype(bf)
+    reduce_6()
     for i in range(1, 8):
         t_arrival((me + i) % 8).wait_recv()
     total = tiny[0].astype(f32)
@@ -1274,6 +1548,7 @@
 
     for i in range(1, 8):
         o_push(i).start()
+    reduce_7()
     dqkv_all[me] = dqkv[me]
     grad_qkv = jnp.zeros((256, 1024), f32)
     for t in range(8):
@@ -1300,6 +1575,7 @@
 
     for i in range(1, 8):
         n_push(i).start()
+    reduce_8()
     p_push.wait()
     pack[mine, :] = (pack[mine, :].astype(f32) + pack_sib[...].astype(f32)).astype(bf)
 
@@ -1333,6 +1609,7 @@
     for i in range(1, 8):
         m_push(i).start()
     pack_in[dp] = pack[pl.ds(pl.multiple_of(ctx * 256 + dp * 32, 32), 32), :]
+    reduce_9()
     for i in range(1, 8):
         rs_arrival((dp + i) % 8).wait_recv()
     owned = pack_in[0].astype(f32)
@@ -1381,6 +1658,15 @@
     for d in range(8):
         g_sib_arrival(d).wait_recv()
         g_relay(d).wait_send()
+    for i in range(1, 8):
+        out_arrival((dp + i) % 8).wait_recv()
+    total = resid_ref[...] + out_own[dp].astype(f32)
+    for i in range(1, 8):
+        total = total + out_in[(dp + i) % 8].astype(f32)
+    output_ref[...] = total.astype(bf)
+    reduce_10()
+    store = pltpu.make_async_copy(reduced, reduced_ref, load_sem.at[9])
+    store.start()
     pack_ref[...] = result[...].reshape(512, 1024)
     for i in range(1, 8):
         dh_push(i).wait_send()
@@ -1392,6 +1678,8 @@
         rs_push(i).wait_send()
         m_push(i).wait_send()
         g_push(i).wait_send()
+        out_push(i).wait_send()
+    store.wait()
 
 
 def backward(small, large):
@@ -1402,9 +1690,15 @@
     table = jnp.asarray(rope_constants(2048, 32))
     return pl.pallas_call(
         backward_kernel,
-        out_shape=(shape((128, 1024), bf), shape((8, 128), f32), shape((512, 1024), bf)),
-        in_specs=[vmem] * 15 + [hbm] * 8,
-        out_specs=(vmem, vmem, vmem),
+        out_shape=(
+            shape((128, 1024), bf),
+            shape((8, 128), f32),
+            shape((512, 1024), bf),
+            shape((128, 1024), bf),
+            shape((3072, 1024), bf),
+        ),
+        in_specs=[vmem] * 15 + [hbm] * 10,
+        out_specs=(vmem, vmem, vmem, vmem, hbm),
         scratch_shapes=[
             pltpu.VMEM((8, 128, 1024), bf),
             pltpu.VMEM((8, 256, 128), f32),
@@ -1446,14 +1740,32 @@
             pltpu.VMEM((8, 8, 128), f32),
             pltpu.VMEM((8, 8, 128), f32),
             pltpu.VMEM((2, 8, 128), f32),
-            sem((9,)),
+            sem((11,)),
         ]
         + [sem((8,))] * 8
         + [sem((2,))]
         + [sem((8,))] * 2
         + [sem((2,))]
         + [sem((8,))] * 10
-        + [sem((2,))],
+        + [sem((2,))]
+        + [
+            pltpu.VMEM((3072, 1024), bf),
+            pltpu.VMEM((3072, 1024), bf),
+            pltpu.VMEM((2, 192, 1024), bf),
+            pltpu.VMEM((2, 2, 192, 1024), bf),
+            pltpu.VMEM((192, 1024), bf),
+            pltpu.VMEM((4, 192, 1024), bf),
+            pltpu.VMEM((2, 96, 1024), bf),
+            pltpu.VMEM((2, 192, 1024), bf),
+            sem((30,)),
+            sem((30,)),
+            pltpu.VMEM((8, 128, 1024), bf),
+            pltpu.VMEM((8, 128, 1024), bf),
+            pltpu.VMEM((8, 128, 1024), bf),
+            sem((2,)),
+            sem((8,)),
+            sem((8,)),
+        ],
         compiler_params=pltpu.CompilerParams(
             collective_id=3, has_side_effects=True, vmem_limit_bytes=56 << 20
         ),
@@ -1500,11 +1812,7 @@
     d_rows, d_gate, out_part, grads, w_all = moe(
         rows2, gates, dy_all, w_gate, w_up, w_down, w_t
     )
-    mixed = lax.psum_scatter(
-        out_part.reshape(-1, 1024), ("dp", "ctx"), scatter_dimension=0, tiled=True
-    )
-    output = (resid + mixed.astype(f32)).astype(bf)
-    grad_x, norm1_sum, pack = backward(
+    grad_x, norm1_sum, pack, output, grads = backward(
         (
             hidden_in,
             cotangent,
@@ -1513,7 +1821,7 @@
             gates,
             rows2,
             resid,
-            router,
+            router.T,
             norm1_gain.reshape(1, 1024),
             norm2_gain.reshape(1, 1024),
             q_gain.reshape(1, 128),
@@ -1522,9 +1830,9 @@
             inv,
             lse,
         ),
-        (rows1, raw, q_t, kv, heads, w_out_all, w_all),
+        (rows1, raw, q_t, kv, heads, w_out_all, w_all, grads.reshape(3072, 1024), out_part),
     )
-    grads = lax.psum(grads, "tensor").astype(f32).reshape(3072, 1024)
+    grads = grads.astype(f32)
     gate_up = grads[:2048].reshape(2, 1024, 1024)
     return (
         output,

time: 550 us -> 348 us (0.63)
  waiting for transfers between devices: 194 us -> 0 us
  Pallas kernels: 310 us -> 325 us
  between operations: 15.6 us -> 0.71 us
  local copies, waits for them, and re-layouts: 18.6 us -> 12.7 us
    psum x1 -> x0, waiting for transfers between devices: 194 us -> none  [shards(): grads = lax.psum(grads, 'tensor').astype(f32).reshape(3072, 1024)]
    pallas_call x1, Pallas kernels: 126 us -> 180 us  [backward(): pl.pallas_call(backward_kernel, out_shape=(shape((128, 1024), bf), shape(...]
    pallas_call x1, Pallas kernels: 93.6 us -> 68.2 us  [attention(): pl.pallas_call(attention_kernel, out_shape=(shape((128, 1024), bf), shape...]
    pallas_call x1, Pallas kernels: 90.6 us -> 76.3 us  [moe(): pl.pallas_call(moe_kernel, out_shape=(jax.ShapeDtypeStruct((128, 1024), f...]
    unnamed x15 -> x14, local copies, waits for them, and re-layouts: 8.89 us -> 3.01 us
  transfers between devices with their start and end apart: 2 -> 0, of which waited for: 1 -> 0; matrix products, arithmetic and copies ran while one was open for 4% -> 0% of each run, Pallas kernels for 23% -> 0%
where the time goes in v3:
time: 348 us; the launch traced here: 347 us
  Pallas kernels  325 us (93%)
  local copies, waits for them, and re-layouts  12.7 us (4%)
  other arithmetic  9.07 us (3%)
    pallas_call x1, Pallas kernels, backward(): pl.pallas_call(backward_kernel, out_shape=(shape((128, 1024), bf), shape(...  180 us
    pallas_call x1, Pallas kernels, moe(): pl.pallas_call(moe_kernel, out_shape=(jax.ShapeDtypeStruct((128, 1024), f...  76.3 us
    pallas_call x1, Pallas kernels, attention(): pl.pallas_call(attention_kernel, out_shape=(shape((128, 1024), bf), shape...  68.2 us

profile of v3, /device:TPU:1, one launch (start us, length us, event | category | flops | bytes accessed | tf_op | source)
XLA Modules:
  0.0 347.2 jit_solution(17500177274842948919)
XLA Ops:
  0.6 68.2 %shard_map.281 = (bf16[128,1024]{1,0:T(8,128)(2,1)}, f32[32,128]{1,0:T(8,128)}, f32[128,1024]{1,0:T(8,128)}, bf16[8,128,1024]{2,1,0:T(8,128)(2,1)}, f32[8,256,12...) custom-call(bf16[128,1024]{1,0:T(8,128)(2,1)} %x_ref.3, ...), custom_call_target="tpu_custom_call" | custom-call | flops 5000000000 | bytes 20000000 | tf_op jit(solution)/shard_map/pallas_call | solution.py:925
  68.9 76.3 %shard_map.282 = (f32[128,1024]{1,0:T(8,128)}, f32[32,128]{1,0:T(8,128)}, bf16[16,128,1024]{2,1,0:T(8,128)(2,1)}, bf16[24,128,1024]{2,1,0:T(8,128)(2,1)}, bf16[8,256,1024]{2,1,0:T(8,128)(2,1)}) custom-call(bf16[128,1024]{1,0:T(8,128)(2,1)} %get-tuple-element.37.rows_ref.rows2_ref, f32[32,128]{1,0:T(8,128)} %get-tuple-element.38.gate_ref.gates_ref, ...), custom_call_target="tpu_custom_call" | custom-call | flops 20000000000 | bytes 30000000 | tf_op jit(solution)/shard_map/pallas_call | solution.py:477
  145.1 180.3 %shard_map.283 = (bf16[128,1024]{1,0:T(8,128)(2,1)}, f32[8,128]{1,0:T(8,128)}, bf16[512,1024]{1,0:T(8,128)(2,1)}, bf16[128,1024]{1,0:T(8,128)(2,1)}, bf16[3072,1024]{1,0:T(8,128)(2,1)}) custom-call(bf16[128,1024]{1,0:T(8,128)(2,1)} %x_ref.3, bf16[128,1024]{1,0:T(8,128)(2,1)} %dy_ref.3, f32[128,1024]{1,0:T(8,128)} %get-tuple-element.41.d_rows_ref, ...), custom_call_target="tpu_custom_call" | custom-call | flops 10000000000 | bytes 20000000 | tf_op jit(solution)/shard_map/pallas_call | solution.py:1691
  325.4 1.2 bitcast_convert_fusion
  326.6 1.2 bitcast_convert_fusion.1
  327.8 1.3 slice_convert_fusion.1
  329.1 1.5 convert_bitcast_fusion.3
  330.6 0.0 slice-start
  330.6 2.0 convert_bitcast_fusion.1
  332.6 1.9 slice_convert_fusion
  334.5 1.0 copy.32
  335.5 0.0 slice-start.1
  335.5 4.2 %slice.51 = f32[1024,1024]{1,0:T(8,128)} slice(bf16[3072,1024]{1,0:T(8,128)(2,1)} %get-tuple-element.59), slice={[2048:3072], [0:1024]} | slice | bytes 8388608 | tf_op jit(solution)/shard_map/slice | solution.py:1851
  339.7 0.0 slice-done
  339.7 0.0 slice-done.1
  339.7 1.0 slice.48
  340.8 0.0 copy-start.1
  340.8 0.0 copy-start
  340.8 0.0 copy-start.2
  340.8 4.4 %fusion = (f32[2,1024,512]{2,1,0:T(8,128)}, f32[2,1024,512]{2,1,0:T(8,128)}) fusion(f32[2,1024,1024]{2,1,0:T(8,128)S(1)} %bitcast.28), kind=kLoop, calls=%fused_computation.8 | loop fusion | bytes 16777216 | tf_op jit(solution)/shard_map/slice | solution.py:1850
  345.2 0.0 copy-done.1
  345.2 0.7 copy.36
  345.9 0.0 copy-done
  345.9 0.7 copy.37
  346.6 0.0 copy-done.2
  346.6 0.6 copy.38
  (1 shorter events, 0.0 us)
Async XLA Ops:
  330.6 9.1 %slice-start = ((s8[6291456]{0:T(1024)(128)(4,1)}), s8[2097152]{0:T(1024)(128)(4,1)S(1)}, s32[]{:S(2)}) async-start(s8[6291456]{0:T(1024)(128)(4,1)} %bitcast.29), calls=%async_computation | async-start | bytes 4194304
  335.5 4.2 %slice-start.1 = ((s8[6291456]{0:T(1024)(128)(4,1)}), s8[4194304]{0:T(1024)(128)(4,1)S(1)}, s32[]{:S(2)}) async-start(s8[6291456]{0:T(1024)(128)(4,1)} %bitcast.29), calls=%async_computation.1 | async-start | bytes 8388608
  340.8 4.5 %copy-start.1 = (bf16[128,1024]{1,0:T(8,128)(2,1)S(1)}, bf16[128,1024]{1,0:T(8,128)(2,1)}, u32[]{:S(2)}) copy-start(bf16[128,1024]{1,0:T(8,128)(2,1)} %get-tuple-element.94) | copy-start | bytes 786436
  340.8 5.1 %copy-start = (bf16[128,1024]{1,0:T(8,128)(2,1)S(1)}, bf16[128,1024]{1,0:T(8,128)(2,1)}, u32[]{:S(2)}) copy-start(bf16[128,1024]{1,0:T(8,128)(2,1)} %get-tuple-element.95) | copy-start | bytes 786436
  340.8 5.8 %copy-start.2 = (f32[8,128]{1,0:T(8,128)S(1)}, f32[8,128]{1,0:T(8,128)}, u32[]{:S(2)}) copy-start(f32[8,128]{1,0:T(8,128)} %get-tuple-element.57) | copy-start | bytes 12292

commit v4 on v3

--- a/solution.py
+++ b/solution.py
@@ -60,6 +60,26 @@
 
 def opposite(a, b):
     return b + (a % 2) * (1 - 2 * b)
+
+
+def first_half(z, y, k, c):
+    return pl.ds(pl.multiple_of(240 * (((z + k) % 4) * 2 + c), 16), 240)
+
+
+def second_half(z, y, k, c):
+    return pl.ds(pl.multiple_of(1920 + 144 * (((z + k) % 4) * 2 + c), 16), 144)
+
+
+def piece(z, y, k, c, part):
+    start = 1920 + 144 * (((z + k) % 4) * 2 + c) + 80 * part
+    return pl.ds(pl.multiple_of(start, 16), (80, 64)[part])
+
+
+def add_rows(ref, place, *parts):
+    total = ref[place, :].astype(jnp.float32)
+    for part in parts:
+        total = total + part.astype(jnp.float32)
+    ref[place, :] = total.astype(jnp.bfloat16)
 
 
 def moe_kernel(
@@ -78,10 +98,8 @@
     rows_all,
     gate_all,
     dy_all,
-    w_gu,
-    w_dn,
-    acc_gu,
-    acc_dn,
+    w_full,
+    acc,
     out_all,
     din_all,
     sib,
@@ -114,6 +132,11 @@
     store_sem,
     w_send,
     w_recv,
+    ra_0,
+    ra_1,
+    rb,
+    r_send,
+    r_recv,
 ):
     tensor = lax.axis_index("tensor")
     dp, ctx = lax.axis_index("dp"), lax.axis_index("ctx")
@@ -129,14 +152,14 @@
     loads = []
     for j in range(2):
         loads.append(
-            pltpu.make_async_copy(w_gate_ref.at[j], w_gu.at[j, :, pl.ds(0, 512)], load_sem.at[3 * j])
+            pltpu.make_async_copy(w_gate_ref.at[j], w_full.at[pl.ds(1024 * j, 1024), pl.ds(0, 512)], load_sem.at[3 * j])
         )
         loads.append(
             pltpu.make_async_copy(
-                w_up_ref.at[j], w_gu.at[j, :, pl.ds(512, 512)], load_sem.at[3 * j + 1]
+                w_up_ref.at[j], w_full.at[pl.ds(1024 * j, 1024), pl.ds(512, 512)], load_sem.at[3 * j + 1]
             )
         )
-        loads.append(pltpu.make_async_copy(w_down_ref.at[j], w_dn.at[j], load_sem.at[3 * j + 2]))
+        loads.append(pltpu.make_async_copy(w_down_ref.at[j], w_full.at[pl.ds(2048 + 512 * j, 512)], load_sem.at[3 * j + 2]))
     loads.append(pltpu.make_async_copy(dy_ref, dy_all, load_sem.at[6]))
     for load in loads:
         load.start()
@@ -191,8 +214,7 @@
     for r in range(1, 16):
         gate_push(r // 4, (r // 2) % 2, r % 2).start()
 
-    acc_gu[...] = jnp.zeros_like(acc_gu)
-    acc_dn[...] = jnp.zeros_like(acc_dn)
+    acc[...] = jnp.zeros_like(acc)
 
     half = pl.ds(pl.multiple_of(ctx * 128, 128), 128)
 
@@ -302,27 +324,29 @@
             gs_buf[j, at, :] = gs
 
     def expert(j):
+        of_gu = pl.ds(pl.multiple_of(j * 1024, 1024), 1024)
+        of_dn = pl.ds(pl.multiple_of(2048 + j * 512, 512), 512)
         x = x_buf[j]
-        gu = jnp.dot(x, w_gu[j], preferred_element_type=jnp.float32)
+        gu = jnp.dot(x, w_full[of_gu, :], preferred_element_type=jnp.float32)
         g, u = gu[:, :512], gu[:, 512:]
         s = jax.nn.sigmoid(g)
         silu = g * s
         act = (silu * u).astype(jnp.bfloat16)
         eout = (
-            jnp.dot(act, w_dn[j], preferred_element_type=jnp.float32)
+            jnp.dot(act, w_full[of_dn, :], preferred_element_type=jnp.float32)
             .astype(jnp.bfloat16)
             .astype(jnp.float32)
         )
         dgs_buf[j] = jnp.sum(y_buf[j].astype(jnp.float32) * eout, 1, keepdims=True)
         o_buf[j] = (eout * gs_buf[j]).astype(jnp.bfloat16)
         d = d_buf[j]
-        d_act = dot_nt(d, w_dn[j])
+        d_act = dot_nt(d, w_full[of_dn, :])
         d_g = (d_act * u * s * (1.0 + g * (1.0 - s))).astype(jnp.bfloat16)
         d_u = (d_act * silu).astype(jnp.bfloat16)
         d_gu = jnp.concatenate([d_g, d_u], 1)
-        i_buf[j] = dot_nt(d_gu, w_gu[j]).astype(jnp.bfloat16)
-        acc_gu[j] += dot_tn(x, d_gu)
-        acc_dn[j] += dot_tn(act, d)
+        i_buf[j] = dot_nt(d_gu, w_full[of_gu, :]).astype(jnp.bfloat16)
+        acc[of_gu, :] += dot_tn(x, d_gu)
+        acc[of_dn, :] += dot_tn(act, d)
 
     def spread(a, q):
         r = 4 * a + q
@@ -410,6 +434,34 @@
     rs_got(2)
     plus(8, slice(None), rs_b[...])
     rs_go(4, 5)
+
+    def round_rows(n, carry):
+        place = pl.ds(pl.multiple_of(n * 128, 128), 128)
+        w_full[place, :] = acc[place, :].astype(jnp.bfloat16)
+        return carry
+
+    lax.fori_loop(0, 24, round_rows, 0)
+    z, y = tensor // 2, tensor % 2
+    up, down, pair = (
+        (dp, ctx, ((z + 1) % 4) * 2 + y),
+        (dp, ctx, ((z + 3) % 4) * 2 + y),
+        (dp, ctx, z * 2 + 1 - y),
+    )
+
+    def grad_hop(n):
+        place, dst, device = (
+            (first_half(z, y, 2, 0), ra_0.at[0], up),
+            (first_half(z, y, 2, 1), ra_0.at[1], down),
+            (first_half(z, y, 1, 1), ra_1.at[0], up),
+            (first_half(z, y, 3, 0), ra_1.at[1], down),
+            (second_half(z, y, 2, 1 - y), rb.at[0], pair),
+            (second_half(z, y, 1, 1 - y), rb.at[1], pair),
+            (second_half(z, y, 3, 1 - y), rb.at[2], pair),
+        )[n]
+        return copy_to(w_full.at[place], dst, r_send.at[n], r_recv.at[n], device)
+
+    for n in (0, 1, 4, 2, 3, 5, 6):
+        grad_hop(n).start()
     post(6, 7)
     rs_got(4)
     plus(12, low, rs_d[0])
@@ -426,21 +478,8 @@
         relay(n).wait_send()
     for r in range(1, 16):
         gate_push(r // 4, (r // 2) % 2, r % 2).wait_send()
-    stores = []
-    for j in range(2):
-        for h in range(8):
-            rows_all[8 * j + h] = acc_gu[j, 128 * h : 128 * h + 128, :].astype(jnp.bfloat16)
-        for h in range(4):
-            dy_all[4 * j + h] = acc_dn[j, 128 * h : 128 * h + 128, :].astype(jnp.bfloat16)
-    stores.append(pltpu.make_async_copy(rows_all, grad_ref.at[pl.ds(0, 16)], store_sem.at[0]))
-    stores.append(
-        pltpu.make_async_copy(
-            dy_all.at[pl.ds(0, 8)], grad_ref.at[pl.ds(16, 8)], store_sem.at[1]
-        )
-    )
-    stores.append(pltpu.make_async_copy(out_all, out_part_ref, store_sem.at[2]))
-    for store in stores:
-        store.start()
+    store_out = pltpu.make_async_copy(out_all, out_part_ref, store_sem.at[0])
+    store_out.start()
 
     for r in range(1, 16):
         a, b, flip = r // 4, (r // 2) % 2, r % 2
@@ -466,8 +505,26 @@
         w_push(i).wait_send()
         w_relay(t).wait_send()
     w_own.wait()
-    for store in stores:
-        store.wait()
+    grad_hop(0).wait_recv()
+    add_rows(w_full, first_half(z, y, 1, 0), ra_0[0])
+    grad_hop(1).wait_recv()
+    add_rows(w_full, first_half(z, y, 3, 1), ra_0[1])
+    grad_hop(4).wait_recv()
+    add_rows(w_full, second_half(z, y, 2, y), rb[0])
+    grad_hop(2).wait_recv()
+    add_rows(w_full, first_half(z, y, 0, 1), ra_1[0])
+    grad_hop(3).wait_recv()
+    add_rows(w_full, first_half(z, y, 0, 0), ra_1[1])
+    grad_hop(5).wait_recv()
+    add_rows(w_full, second_half(z, y, 1, y), rb[1])
+    grad_hop(6).wait_recv()
+    add_rows(w_full, second_half(z, y, 3, y), rb[2])
+    store_grad = pltpu.make_async_copy(w_full, grad_ref, store_sem.at[1])
+    store_grad.start()
+    for n in range(7):
+        grad_hop(n).wait_send()
+    store_out.wait()
+    store_grad.wait()
 
 
 def moe(rows, gates, dy, w_gate, w_up, w_down, w_t):
@@ -480,19 +537,17 @@
             jax.ShapeDtypeStruct((128, 1024), f32),
             jax.ShapeDtypeStruct((32, 128), f32),
             jax.ShapeDtypeStruct((16, 128, 1024), bf),
-            jax.ShapeDtypeStruct((24, 128, 1024), bf),
+            jax.ShapeDtypeStruct((3072, 1024), bf),
             jax.ShapeDtypeStruct((8, 256, 1024), bf),
         ),
-        in_specs=[vmem] * 2 + [hbm] * 5,
+        in_specs=[vmem] * 2 + [hbm] * 4 + [vmem],
         out_specs=(vmem, vmem, hbm, hbm, hbm),
         scratch_shapes=[
             pltpu.VMEM((16, 128, 1024), bf),
             pltpu.VMEM((16, 32, 128), f32),
             pltpu.VMEM((16, 128, 1024), bf),
-            pltpu.VMEM((2, 1024, 1024), bf),
-            pltpu.VMEM((2, 512, 1024), bf),
-            pltpu.VMEM((2, 1024, 1024), f32),
-            pltpu.VMEM((2, 512, 1024), f32),
+            pltpu.VMEM((3072, 1024), bf),
+            pltpu.VMEM((3072, 1024), f32),
             pltpu.VMEM((16, 128, 1024), bf),
             pltpu.VMEM((16, 128, 1024), bf),
             pltpu.VMEM((8, 128, 1024), bf),
@@ -522,9 +577,14 @@
             sem((8,)),
             sem((16,)),
             sem((16,)),
-            sem((3,)),
+            sem((2,)),
             sem((16,)),
             sem((8, 2)),
+            pltpu.VMEM((2, 240, 1024), bf),
+            pltpu.VMEM((2, 240, 1024), bf),
+            pltpu.VMEM((3, 144, 1024), bf),
+            sem((7,)),
+            sem((7,)),
         ],
         compiler_params=pltpu.CompilerParams(
             collective_id=1, has_side_effects=True, vmem_limit_bytes=60 << 20
@@ -563,6 +623,7 @@
     w_out_all_ref,
     dy_all_ref,
     w_t_ref,
+    heads_all_ref,
     h_all,
     dy_all,
     w_all,
@@ -696,12 +757,8 @@
         value = dot_nt(w_t[...], h_all[t])
         raw[t] = value
         square = value * value
-        sums = [
-            jnp.sum(square[0:128], 0, keepdims=True),
-            jnp.sum(square[128:192], 0, keepdims=True),
-            jnp.zeros((6, 128), f32),
-        ]
-        stat[t] = jnp.concatenate(sums, 0)
+        stat[0, pl.ds(t, 1), :] = jnp.sum(square[0:128], 0, keepdims=True)
+        stat[1, pl.ds(t, 1), :] = jnp.sum(square[128:192], 0, keepdims=True)
 
     project(me)
     for n in range(2):
@@ -765,11 +822,13 @@
 
     def finish(t, carry):
         at = pl.ds(pl.multiple_of(t * 128, 128), 128)
-        sums = stats[0, t]
-        for s in range(1, 8):
-            sums = sums + stats[s, t]
-        width = jnp.where(lax.broadcasted_iota(jnp.int32, (8, 128), 0) == 0, 1024.0, 512.0)
-        inv = lax.rsqrt(sums / width + EPS)
+        rows = []
+        for n, width in enumerate((1024.0, 512.0)):
+            total = stats[0, n, pl.ds(t, 1), :]
+            for s in range(1, 8):
+                total = total + stats[s, n, pl.ds(t, 1), :]
+            rows.append(lax.rsqrt(total / width + EPS))
+        inv = jnp.concatenate(rows + [jnp.zeros((6, 128), f32)], 0)
         inv_ref[t] = inv
         value = raw[t]
         cos_part, sin_part = table[0, :, at], table[1, :, at]
@@ -883,6 +942,8 @@
         o_arrival(t).wait_recv()
     store_w = pltpu.make_async_copy(w_all, w_out_all_ref, store_sem.at[6])
     store_w.start()
+    store_heads = pltpu.make_async_copy(heads_all, heads_all_ref, store_sem.at[9])
+    store_heads.start()
     attended = dot_tn(heads_all[...].reshape(1024, 128), w_all[...].reshape(1024, 1024))
     resid = x + attended
     resid_ref[...] = resid
@@ -912,7 +973,7 @@
         h_hop(n).wait_send()
         dy_hop(n).wait_send()
         dy_relay(n).wait_send()
-    for store in [store_rows, store_raw, store_wt, store_w, store_dy] + stores:
+    for store in [store_rows, store_raw, store_wt, store_w, store_dy, store_heads] + stores:
         store.wait()
 
 
@@ -938,9 +999,10 @@
             shape((8, 128, 1024), bf),
             shape((16, 128, 1024), bf),
             shape((256, 1024), bf),
+            shape((8, 128, 128), bf),
         ),
         in_specs=[vmem] * 9 + [hbm] * 5,
-        out_specs=(vmem, vmem, vmem, hbm, hbm, vmem, hbm, hbm, vmem, hbm, hbm, hbm, hbm),
+        out_specs=(vmem, vmem, vmem, hbm, hbm, vmem, hbm, hbm, vmem, hbm, hbm, hbm, hbm, hbm),
         scratch_shapes=[
             pltpu.VMEM((8, 128, 1024), bf),
             pltpu.VMEM((16, 128, 1024), bf),
@@ -949,8 +1011,8 @@
             pltpu.VMEM((256, 1024), bf),
             pltpu.VMEM((8, 256, 128), f32),
             pltpu.VMEM((2, 32, 1024), f32),
-            pltpu.VMEM((8, 8, 128), f32),
-            pltpu.VMEM((8, 8, 8, 128), f32),
+            pltpu.VMEM((2, 8, 128), f32),
+            pltpu.VMEM((8, 2, 8, 128), f32),
             pltpu.VMEM((128, 1024), bf),
             pltpu.VMEM((128, 1024), bf),
             pltpu.VMEM((128, 1024), bf),
@@ -971,7 +1033,7 @@
             sem((2,)),
             sem((8,)),
             sem((8,)),
-            sem((9,)),
+            sem((10,)),
         ],
         compiler_params=pltpu.CompilerParams(
             collective_id=2, has_side_effects=True, vmem_limit_bytes=56 << 20
@@ -1018,6 +1080,7 @@
     q_ref,
     kv_ref,
     heads_ref,
+    heads_all_ref,
     w_out_ref,
     w_all_ref,
     grads_ref,
@@ -1039,7 +1102,9 @@
     table,
     starts,
     d_resid,
-    datt_all,
+    heads_all,
+    wo_part,
+    wo_in,
     dh_send,
     dh_all,
     tiny,
@@ -1060,7 +1125,6 @@
     stats,
     dqkv,
     dqkv_all,
-    heads2,
     pack,
     pack_sib,
     pack_in,
@@ -1094,7 +1158,6 @@
     ns_sem,
     grads,
     reduced,
-    ra1,
     ra2,
     ra4,
     rb1,
@@ -1104,7 +1167,9 @@
     r_recv,
     out_own,
     out_sib,
-    out_in,
+    out_a,
+    out_b,
+    out_c,
     os_sem,
     out_send,
     out_recv,
@@ -1116,157 +1181,237 @@
     def side(i):
         return (dp, ctx, (me + i) % 8)
 
+    def chip(i):
+        return ((dp + i) % 8, ctx, me)
+
     z, y = me // 2, me % 2
     other = 1 - y
-    up, down, across_y = (
+    up, down, pair = (
         (dp, ctx, ((z + 1) % 4) * 2 + y),
         (dp, ctx, ((z + 3) % 4) * 2 + y),
         (dp, ctx, z * 2 + other),
     )
 
-    def unit(k, c, first=0):
-        return pl.ds(pl.multiple_of((first + ((z + k) % 4) * 2 + c) * 192, 64), 192)
-
-    def half_unit(k, c, part):
-        return pl.ds(pl.multiple_of((8 + ((z + k) % 4) * 2 + c) * 192 + part * 96, 32), 96)
-
-    def hop(n):
+    def a_rows(k, c, s=0):
+        start = 240 * (((z + k) % 4) * 2 + c) + 128 * s
+        return pl.ds(pl.multiple_of(start, 16), (128, 112)[s])
+
+    def of_part(s):
+        return pl.ds(128 * s, (128, 112)[s])
+
+    def b_rows(k, c):
+        return second_half(z, y, k, c)
+
+    def hop(n, s=0):
         if n < 2:
-            src, dst = grads.at[unit(2, n)], ra1.at[n]
+            src, dst = grads.at[a_rows((1, 3)[n], n, s)], ra2.at[n, of_part(s)]
             to = (up, down)[n]
+        elif n == 2:
+            src, dst, to = grads.at[b_rows(0, other)], rb1, pair
+        elif n < 5:
+            part = n - 3
+            src, to = grads.at[piece(z, y, 2, y, part)], (up, down)[part]
+            dst = (rb2.at[pl.ds(0, 80)], rb2.at[pl.ds(80, 64)])[part]
+        elif n == 5:
+            src, dst, to = grads.at[a_rows(0, other, s)], ra4.at[of_part(s)], pair
+        elif n == 6:
+            src, dst, to = grads.at[b_rows(1, y)], rb3.at[0], up
+        elif n == 7:
+            src, dst, to = grads.at[b_rows(3, y)], rb3.at[1], down
+        else:
+            place, to = (
+                (a_rows(0, y, s), pair),
+                (a_rows(0, y, s), up),
+                (a_rows(0, y, s), down),
+                (a_rows(0, other, s), up),
+                (a_rows(0, other, s), down),
+                (a_rows(3, 0, s), up),
+                (a_rows(1, 1, s), down),
+                (b_rows(0, y), up),
+                (b_rows(0, y), down),
+                (piece(z, y, 3, y, 0), up),
+                (piece(z, y, 1, y, 1), down),
+                (b_rows(0, y), pair),
+                (b_rows(3, y), pair),
+                (b_rows(1, y), pair),
+                (b_rows(2, y), pair),
+            )[n - 8]
+            src = dst = reduced.at[place]
+        return copy_to(src, dst, r_send.at[n + 23 * s], r_recv.at[n + 23 * s], to)
+
+    def go(*hops, s=0):
+        for n in hops:
+            hop(n, s).start()
+
+    def got(*hops, s=0):
+        for n in hops:
+            hop(n, s).wait_recv()
+
+    def reduce_0():
+        go(0, 1, 3, 4, 2)
+
+    def reduce_1(s):
+        got(0, 1, s=s)
+        for c in range(2):
+            add_rows(grads, a_rows(0, c, s), ra2[c, of_part(s)])
+        go(5, s=s)
+
+    def reduce_2():
+        got(3, 4)
+        add_rows(grads, piece(z, y, 1, y, 0), rb2[0:80])
+        add_rows(grads, piece(z, y, 3, y, 1), rb2[80:144])
+        go(6, 7)
+        got(2)
+        add_rows(grads, b_rows(0, y), rb1[...])
+
+    def reduce_3(s):
+        got(5, s=s)
+        add_rows(grads, a_rows(0, y, s), ra4[of_part(s)])
+        reduced[a_rows(0, y, s), :] = grads[a_rows(0, y, s), :]
+        go(8, 9, 10, s=s)
+
+    def reduce_4():
+        got(6, 7)
+        add_rows(grads, b_rows(0, y), rb3[0], rb3[1])
+        reduced[b_rows(0, y), :] = grads[b_rows(0, y), :]
+        go(15, 16, 19)
+
+    def reduce_5(s):
+        got(8, s=s)
+        go(11, 12, s=s)
+
+    def reduce_6():
+        got(15)
+        go(17, 20)
+        got(16)
+        go(18, 21)
+
+    def reduce_7(s):
+        @pl.when(y == 0)
+        def _():
+            got(9, 12, s=s)
+
+        @pl.when(y == 1)
+        def _():
+            got(11, 10, s=s)
+
+        go(13, 14, s=s)
+
+    def reduce_8():
+        got(17, 18)
+        go(22)
+
+    def reduce_9():
+        for s in range(2):
+
+            @pl.when(y == 0)
+            def _():
+                got(10, 11, s=s)
+
+            @pl.when(y == 1)
+            def _():
+                got(9, 12, s=s)
+
+            got(13, 14, s=s)
+        got(19, 20, 21, 22)
+        for n in range(23):
+            hop(n).wait_send()
+        for n in (0, 1, 5, 8, 9, 10, 11, 12, 13, 14):
+            hop(n, 1).wait_send()
+
+    def x_side(i):
+        return ((dp // 4) * 4 + (dp + i) % 4, ctx, me)
+
+    right, left, partner = x_side(1), x_side(3), ((dp + 4) % 8, ctx, me)
+    theirs_out = out_part_ref.at[pl.ds(pl.multiple_of((1 - ctx) * 8, 8), 8)]
+    os_push = copy_to(
+        theirs_out, out_sib.at[:, :, pl.ds(0, 1024)], os_sem.at[0], os_sem.at[1], sibling
+    )
+    wo_push = copy_to(
+        wo_part.at[1 - ctx],
+        out_sib.at[:, :, pl.ds(1024, 512)],
+        os_sem.at[2],
+        os_sem.at[3],
+        sibling,
+    )
+
+    def out_at(i, b):
+        return (dp // 4 + b) % 2 * 4 + (dp + i) % 4
+
+    def out_hop(n):
+        b = n % 2
+        if n < 2:
+            src, dst, to = out_own.at[out_at(2, b), pl.ds(0, 64)], out_a.at[0, b], right
         elif n < 4:
-            src, dst, to = grads.at[unit(1, n - 2)], ra2.at[0, n - 2], up
+            src, dst, to = out_own.at[out_at(2, b), pl.ds(64, 64)], out_a.at[1, b], left
         elif n < 6:
-            src, dst, to = grads.at[unit(3, n - 4)], ra2.at[1, n - 4], down
-        elif n == 6:
-            src, dst, to = grads.at[unit(0, other)], ra4, across_y
-        elif n == 7:
-            src = dst = reduced.at[unit(0, y)]
-            to = across_y
-        elif n < 12:
-            src = dst = reduced.at[unit(0, n % 2)]
-            to = up if n < 10 else down
-        elif n == 12:
-            src = dst = reduced.at[unit(3, 0)]
-            to = up
-        elif n == 13:
-            src = dst = reduced.at[unit(1, 1)]
-            to = down
-        elif n < 18:
-            src, dst, to = grads.at[unit(n - 14, other, 8)], rb1.at[(z + n - 14) % 4], across_y
-        elif n < 20:
-            src, dst, to = grads.at[half_unit(2, y, n - 18)], rb2.at[n - 18], (up, down)[n - 18]
-        elif n == 20:
-            src, dst, to = grads.at[unit(1, y, 8)], rb3.at[0], up
-        elif n == 21:
-            src, dst, to = grads.at[unit(3, y, 8)], rb3.at[1], down
-        elif n < 24:
-            src = dst = reduced.at[unit(0, y, 8)]
-            to = (up, down)[n - 22]
-        elif n == 24:
-            src = dst = reduced.at[half_unit(3, y, 0)]
-            to = up
-        elif n == 25:
-            src = dst = reduced.at[half_unit(1, y, 1)]
-            to = down
+            src, dst, to = out_own.at[out_at(1, b)], out_b.at[0, b], right
+        elif n < 8:
+            src, dst, to = out_own.at[out_at(3, b)], out_b.at[1, b], left
         else:
-            src = dst = reduced.at[unit((0, 3, 1, 2)[n - 26], y, 8)]
-            to = across_y
-        return copy_to(src, dst, r_send.at[n], r_recv.at[n], to)
-
-    def go(*hops):
-        for n in hops:
-            hop(n).start()
-
-    def got(*hops):
-        for n in hops:
-            hop(n).wait_recv()
-
-    def plus(place, *parts):
-        total = grads[place, :].astype(jnp.float32)
+            src, dst, to = out_own.at[out_at(0, 1)], out_c, partner
+        return copy_to(src, dst, out_send.at[n], out_recv.at[n], to)
+
+    def out_0():
+        os_push.wait()
+        wo_push.wait()
+
+        def add_sib(d, carry):
+            left_part = out_own[d, :, 0:1024].astype(f32)
+            right_part = wo_part[ctx, d].astype(f32)
+            total = jnp.concatenate([left_part, right_part], 1) + out_sib[d].astype(f32)
+            out_own[d] = total.astype(bf)
+            return carry
+
+        lax.fori_loop(0, 8, add_sib, 0)
+        for n in range(4):
+            out_hop(n).start()
+
+    def out_add(at, rows, *parts):
+        total = out_own[at, rows].astype(f32)
         for part in parts:
-            total = total + part.astype(jnp.float32)
-        grads[place, :] = total.astype(jnp.bfloat16)
-
-    def reduce_0():
-        go(0, 1, 14, 15, 16, 17, 3, 4)
-
-    def reduce_1():
-        got(0)
-        plus(unit(1, 0), ra1[0])
-        go(2)
-        got(1)
-        plus(unit(3, 1), ra1[1])
-        go(5)
-
-    def reduce_2():
-        for k in (2, 1, 3, 0):
-            got(14 + k)
-            plus(unit(k, y, 8), rb1[(z + k) % 4])
-            if k == 2:
-                go(18, 19)
-
-    def reduce_3():
-        got(2, 3, 4, 5)
-        for c in range(2):
-            plus(unit(0, c), ra2[0, c], ra2[1, c])
-        go(6)
-
-    def reduce_4():
-        got(18, 19)
-        plus(half_unit(1, y, 0), rb2[0])
-        plus(half_unit(3, y, 1), rb2[1])
-        go(20, 21)
-
-    def reduce_5():
-        got(6)
-        plus(unit(0, y), ra4[...])
-        reduced[unit(0, y), :] = grads[unit(0, y), :]
-        go(7)
-
-    def reduce_6():
-        got(20, 21)
-        plus(unit(0, y, 8), rb3[0], rb3[1])
-        reduced[unit(0, y, 8), :] = grads[unit(0, y, 8), :]
-        go(22, 23, 26)
-
-    def reduce_7():
-        got(7)
-        go(8, 11, 9, 10)
-
-    def reduce_8():
-        got(22)
-        go(24, 27)
-        got(23)
-        go(25, 28)
-        got(8)
-        go(12)
-        got(11)
-        go(13)
-
-    def reduce_9():
-        got(24, 25)
-        go(29)
-
-    def reduce_10():
-        got(9, 10, 12, 13, 26, 27, 28, 29)
-        for n in range(30):
-            hop(n).wait_send()
-
-    theirs_out = out_part_ref.at[pl.ds(pl.multiple_of((1 - ctx) * 8, 8), 8)]
-    os_push = copy_to(theirs_out, out_sib, os_sem.at[0], os_sem.at[1], sibling)
-
-    def out_push(i):
-        return copy_to(
-            out_own.at[(dp + i) % 8], out_in.at[dp], out_send.at[i], out_recv.at[dp], chip(i)
-        )
-
-    def out_arrival(d):
-        return copy_to(out_in.at[d], out_in.at[d], out_send.at[0], out_recv.at[d], sibling)
-
-    def chip(i):
-        return ((dp + i) % 8, ctx, me)
-
+            total = total + part.astype(f32)
+        out_own[at, rows] = total.astype(bf)
+
+    def out_1():
+        for b in range(2):
+            out_hop(b).wait_recv()
+            out_add(out_at(1, b), pl.ds(0, 64), out_a[0, b])
+            out_hop(4 + b).start()
+            out_hop(2 + b).wait_recv()
+            out_add(out_at(3, b), pl.ds(64, 64), out_a[1, b])
+            out_hop(6 + b).start()
+
+    def out_2():
+        for b in (1, 0):
+            out_hop(4 + b).wait_recv()
+            out_hop(6 + b).wait_recv()
+            out_add(out_at(0, b), slice(None), out_b[0, b], out_b[1, b])
+            if b == 1:
+                out_hop(8).start()
+
+    def out_3():
+        out_hop(8).wait_recv()
+        total = out_own[dp].astype(f32) + out_c[...].astype(f32)
+        output_ref[...] = (resid_ref[...] + total[:, 0:1024]).astype(bf)
+        wo_sum = total[:, 1024:1536].astype(bf)
+        for t in range(8):
+            wo_part[0, 0, 16 * t : 16 * t + 16, :] = wo_sum[16 * t : 16 * t + 16]
+        for i in range(1, 8):
+            wo_hop(i).start()
+        wo_in[me] = wo_part[0, 0, pl.ds(pl.multiple_of(me * 16, 16), 16), :]
+        for n in range(9):
+            out_hop(n).wait_send()
+
+    def wo_hop(i):
+        rows = pl.ds(pl.multiple_of((me + i) % 8 * 16, 16), 16)
+        return copy_to(wo_part.at[0, 0, rows], wo_in.at[me], a_send.at[i], a_recv.at[me], side(i))
+
+    def wo_arrival(t):
+        return copy_to(wo_in.at[t], wo_in.at[t], a_send.at[0], a_recv.at[t], sibling)
+
+    early = pltpu.make_async_copy(grads_ref, grads, load_sem.at[9])
+    early.start()
     sources = (rows1_ref, raw_ref, q_ref, kv_ref.at[0], kv_ref.at[1], heads_ref, w_out_ref)
     targets = (rows1, raw, q_t, kv_own, kv_sib, heads, w_out)
     loads = [
@@ -1275,11 +1420,13 @@
     ]
     loads.append(pltpu.make_async_copy(w_all_ref, w_all, load_sem.at[7]))
     loads.append(pltpu.make_async_copy(table_ref.at[ctx], table, load_sem.at[8]))
-    loads.append(pltpu.make_async_copy(grads_ref, grads, load_sem.at[9]))
+    loads.append(early)
+    loads.append(pltpu.make_async_copy(heads_all_ref, heads_all, load_sem.at[11]))
     own_blocks = out_part_ref.at[pl.ds(pl.multiple_of(ctx * 8, 8), 8)]
-    loads.append(pltpu.make_async_copy(own_blocks, out_own, load_sem.at[10]))
-    for load in loads:
-        load.start()
+    loads.append(pltpu.make_async_copy(own_blocks, out_own.at[:, :, pl.ds(0, 1024)], load_sem.at[10]))
+    for n, load in enumerate(loads):
+        if n != 9:
+            load.start()
     barrier = pltpu.get_barrier_semaphore()
     for i in range(1, 8):
         pl.semaphore_signal(barrier, inc=1, device_id=side(i), device_id_type=MESH)
@@ -1304,7 +1451,6 @@
     )
     d_resid[...] = d_res
     datt = d_res.astype(bf)
-    datt_all[me] = datt
     for n in (6,):
         loads[n].wait()
     d_heads = dot_nt(w_out[...].reshape(1024, 1024), datt).astype(bf)
@@ -1330,31 +1476,31 @@
         preferred_element_type=f32,
         precision=lax.Precision.HIGHEST,
     )
-    tiny[me] = jnp.concatenate(
-        [router_part, norm2_part, jnp.zeros((15, 1024), f32)], 0
-    ).astype(bf)
-
-    def t_push(i):
-        return copy_to(tiny.at[me], tiny.at[me], t_send.at[i], t_recv.at[me], side(i))
-
-    def t_arrival(t):
-        return copy_to(tiny.at[t], tiny.at[t], t_send.at[0], t_recv.at[t], sibling)
-
-    def a_push(i):
-        return copy_to(datt_all.at[me], datt_all.at[me], a_send.at[i], a_recv.at[me], side(i))
-
-    def a_arrival(t):
-        return copy_to(datt_all.at[t], datt_all.at[t], a_send.at[0], a_recv.at[t], sibling)
+    def pack_rows(place, value):
+        for c in range(2):
+            pack[c, place, :] = value[:, 512 * c : 512 * c + 512].astype(bf)
+
+    pack_rows(pl.ds(256, 32), router_part)
+    pack_rows(pl.ds(288, 16), jnp.concatenate([norm2_part, jnp.zeros((15, 1024), f32)], 0))
+    pack_rows(pl.ds(320, 64), jnp.zeros((64, 1024), f32))
 
     loads[9].wait()
     reduce_0()
     os_push.start()
-    for i in range(1, 8):
-        t_push(i).start()
-    for i in (1, 7, 2, 6, 3, 5, 4):
-        a_push(i).start()
-
-    for n in (0, 1, 2, 3, 4, 5, 7, 8, 10):
+    loads[10].wait()
+
+    def wo_rows(t, carry):
+        value = jnp.dot(heads_all[t], datt, preferred_element_type=f32).astype(bf)
+        rows = pl.ds(pl.multiple_of(t * 16, 16), 16)
+        for d in range(8):
+            for c in range(2):
+                wo_part[c, d, rows, :] = value[16 * d : 16 * d + 16, 512 * c : 512 * c + 512]
+        return carry
+
+    lax.fori_loop(0, 8, wo_rows, 0)
+    wo_push.start()
+    go(0, 1, s=1)
+    for n in (0, 1, 2, 3, 4, 5, 7, 8, 11):
         loads[n].wait()
     seg = segment_ref[...]
     start = jnp.zeros((16, 128), f32)
@@ -1380,7 +1526,6 @@
         for n, kv in enumerate((kv_own, kv_sib)):
             k_nat[n, at, :] = jnp.transpose(kv[0:64, at])
             v_nat[n, at, :] = jnp.transpose(kv[64:128, at])
-        heads2[:, at] = heads[t]
         return carry
 
     lax.fori_loop(0, 8, lay_out, 0)
@@ -1403,7 +1548,6 @@
         return carry
 
     lax.fori_loop(0, 8, lay_dh, 0)
-    reduce_1()
     key_row = lax.broadcasted_iota(jnp.int32, (256, 512), 0).astype(f32)
     query_lane = (lax.broadcasted_iota(jnp.int32, (256, 512), 1) % 256).astype(f32)
     base = (ctx * 1024).astype(f32)
@@ -1422,11 +1566,30 @@
         dk_acc[n, ks, :] += jnp.dot(ds, q_nat[i], preferred_element_type=f32)
         dq_acc[i] += jnp.dot(kv[0:64, ks], ds, preferred_element_type=f32)
 
-    def cross(n, carry):
-        block(1, n // 4, n % 4, ((n % 4) * 256).astype(f32), False)
-        return carry
-
-    lax.fori_loop(0, 16 * ctx, cross, 0)
+    def hook_0():
+        reduce_1(0)
+        reduce_2()
+
+    def hook_1():
+        out_0()
+        reduce_1(1)
+
+    def hook_2():
+        reduce_3(0)
+        reduce_4()
+
+    def hook_3():
+        reduce_3(1)
+        out_1()
+
+    for i in range(4):
+
+        def cross(j, carry, i=i):
+            block(1, i, j, (j * 256).astype(f32), False)
+            return carry
+
+        lax.fori_loop(0, 4 * ctx, cross, 0)
+        (hook_0, hook_1, hook_2, hook_3)[i]()
     dkv_push = copy_to(dkv_out, dkv_in, dkv_sem.at[0], dkv_sem.at[1], sibling)
 
     def upright(t, carry):
@@ -1437,28 +1600,21 @@
 
     lax.fori_loop(0, 8, upright, 0)
     dkv_push.start()
-    os_push.wait()
-
-    def add_sib(d, carry):
-        out_own[d] = (out_own[d].astype(f32) + out_sib[d].astype(f32)).astype(bf)
-        return carry
-
-    lax.fori_loop(0, 8, add_sib, 0)
-    for i in range(1, 8):
-        out_push(i).start()
-    reduce_3()
-
-    def within(i, carry):
+
+    def within(i):
         def full(j, c):
             block(0, i, j, base + (j * 256).astype(f32), False)
             return c
 
         lax.fori_loop(0, i, full, 0)
-        block(0, i, i, base + (i * 256).astype(f32), True)
-        return carry
-
-    lax.fori_loop(0, 4, within, 0)
-    reduce_2()
+        block(0, i, i, base + 256.0 * i, True)
+
+    within(0)
+    within(1)
+    within(2)
+    within(3)
+    reduce_5(0)
+    reduce_6()
     gain_q = column(q_gain_ref[...])
     gain_k = column(jnp.concatenate([k_gain_ref[...], jnp.zeros((1, 64), f32)], 1))[:64]
     dkv_push.wait()
@@ -1481,12 +1637,8 @@
         terms[t, 0:128] = q_term
         terms[t, 128:192] = k_term
         dqkv[t, 192:256] = d_v.astype(bf)
-        rows = [
-            jnp.sum(q_term * q_hat, 0, keepdims=True),
-            jnp.sum(k_term * k_hat, 0, keepdims=True),
-            jnp.zeros((6, 128), f32),
-        ]
-        stat[t] = jnp.concatenate(rows, 0)
+        stat[0, pl.ds(t, 1), :] = jnp.sum(q_term * q_hat, 0, keepdims=True)
+        stat[1, pl.ds(t, 1), :] = jnp.sum(k_term * k_hat, 0, keepdims=True)
         return q_sum, k_sum
 
     q_sum, k_sum = lax.fori_loop(
@@ -1502,36 +1654,27 @@
 
     for i in range(1, 8):
         s_push(i).start()
-    reduce_4()
-    reduce_5()
-    for i in range(1, 8):
-        a_arrival((me + i) % 8).wait_recv()
-    pack[256:384, :] = jnp.dot(
-        heads2[...], datt_all[...].reshape(1024, 1024), preferred_element_type=f32
-    ).astype(bf)
-    reduce_6()
-    for i in range(1, 8):
-        t_arrival((me + i) % 8).wait_recv()
-    total = tiny[0].astype(f32)
-    for t in range(1, 8):
-        total = total + tiny[t].astype(f32)
+    out_2()
     q_row = jnp.sum(jnp.transpose(q_sum), 0, keepdims=True)
     k_row = jnp.sum(jnp.transpose(k_sum), 0, keepdims=True)
     gain_row = jnp.concatenate([q_row, k_row, jnp.zeros((1, 1024 - 192), f32)], 1)
-    extra = jnp.concatenate([total[0:33], gain_row, jnp.zeros((94, 1024), f32)], 0)
-    pack[384:512, :] = extra.astype(bf)
+    pack_rows(pl.ds(304, 16), jnp.concatenate([gain_row, jnp.zeros((15, 1024), f32)], 0))
+    reduce_5(1)
     for i in range(1, 8):
         s_arrival((me + i) % 8).wait_recv()
 
     def finish(t, carry):
         at = pl.ds(pl.multiple_of(t * 128, 128), 128)
-        inner = stats[0, t]
-        for s in range(1, 8):
-            inner = inner + stats[s, t]
+        inner = []
+        for n in range(2):
+            part = stats[0, n, pl.ds(t, 1), :]
+            for s in range(1, 8):
+                part = part + stats[s, n, pl.ds(t, 1), :]
+            inner.append(part)
         inv = inv_ref[t]
         q_hat, k_hat = raw[t, 0:128] * inv[0:1], raw[t, 128:192] * inv[1:2]
-        d_q = inv[0:1] * (terms[t, 0:128] - q_hat * (inner[0:1] / 1024.0))
-        d_k = inv[1:2] * (terms[t, 128:192] - k_hat * (inner[1:2] / 512.0))
+        d_q = inv[0:1] * (terms[t, 0:128] - q_hat * (inner[0] / 1024.0))
+        d_k = inv[1:2] * (terms[t, 128:192] - k_hat * (inner[1] / 512.0))
         dqkv[t, 0:128] = d_q.astype(bf)
         dqkv[t, 128:192] = d_k.astype(bf)
         return carry
@@ -1548,16 +1691,14 @@
 
     for i in range(1, 8):
         o_push(i).start()
-    reduce_7()
     dqkv_all[me] = dqkv[me]
     grad_qkv = jnp.zeros((256, 1024), f32)
     for t in range(8):
         grad_qkv = grad_qkv + jnp.dot(dqkv[t], rows1[t], preferred_element_type=f32)
-    pack[0:256, :] = grad_qkv.astype(bf)
-    mine = pl.ds(pl.multiple_of(ctx * 256, 256), 256)
-    theirs = pl.ds(pl.multiple_of((1 - ctx) * 256, 256), 256)
-    p_push = copy_to(pack.at[theirs], pack_sib, p_sem.at[0], p_sem.at[1], sibling)
+    pack_rows(pl.ds(0, 256), grad_qkv)
+    p_push = copy_to(pack.at[1 - ctx], pack_sib, p_sem.at[0], p_sem.at[1], sibling)
     p_push.start()
+    reduce_7(0)
     for i in range(1, 8):
         o_arrival((me + i) % 8).wait_recv()
     d_rows1 = dot_tn(dqkv_all[...].reshape(2048, 128), w_all[...].reshape(2048, 1024))
@@ -1575,13 +1716,13 @@
 
     for i in range(1, 8):
         n_push(i).start()
-    reduce_8()
     p_push.wait()
-    pack[mine, :] = (pack[mine, :].astype(f32) + pack_sib[...].astype(f32)).astype(bf)
+    pack[ctx] = (pack[ctx].astype(f32) + pack_sib[...].astype(f32)).astype(bf)
+    out_3()
 
     def rs_push(i):
         to = (dp + i) % 8
-        rows = pack.at[pl.ds(pl.multiple_of(ctx * 256 + to * 32, 32), 32)]
+        rows = pack.at[ctx, pl.ds(pl.multiple_of(to * 48, 16), 48)]
         return copy_to(rows, pack_in.at[dp], rs_send.at[i], rs_recv.at[dp], chip(i))
 
     def rs_arrival(d):
@@ -1593,6 +1734,8 @@
     grad_x_ref[...] = (
         d_resid[...] + inv_one * (scaled - x_hat * jnp.mean(scaled * x_hat, -1, keepdims=True))
     ).astype(bf)
+    reduce_8()
+    reduce_7(1)
     for i in range(1, 8):
         n_arrival((me + i) % 8).wait_recv()
     norm1_sum = n1[0]
@@ -1608,14 +1751,44 @@
 
     for i in range(1, 8):
         m_push(i).start()
-    pack_in[dp] = pack[pl.ds(pl.multiple_of(ctx * 256 + dp * 32, 32), 32), :]
-    reduce_9()
+    pack_in[dp] = pack[ctx, pl.ds(pl.multiple_of(dp * 48, 16), 48), :]
     for i in range(1, 8):
         rs_arrival((dp + i) % 8).wait_recv()
     owned = pack_in[0].astype(f32)
     for d in range(1, 8):
         owned = owned + pack_in[d].astype(f32)
-    result[ctx, dp] = owned.astype(bf)
+    top = pl.ds(0, 48)
+    result[ctx, dp, top] = owned.astype(bf)
+    wide = (dp == 5) | (dp == 6)
+
+    def t_push(i):
+        return copy_to(result.at[ctx, dp, top], tiny.at[me], t_send.at[i], t_recv.at[me], side(i))
+
+    def t_arrival(t):
+        return copy_to(tiny.at[t], tiny.at[t], t_send.at[0], t_recv.at[t], sibling)
+
+    @pl.when(wide)
+    def _():
+        for i in range(1, 8):
+            t_push(i).start()
+        tiny[me] = result[ctx, dp, top]
+        for i in range(1, 8):
+            t_arrival((me + i) % 8).wait_recv()
+            t_push(i).wait_send()
+        total = tiny[0].astype(f32)
+        for t in range(1, 8):
+            total = total + tiny[t].astype(f32)
+        row = lax.broadcasted_iota(jnp.int32, (48, 512), 0)
+        shared = ((dp == 5) & (row >= 16)) | ((dp == 6) & (row < 16))
+        result[ctx, dp, top] = jnp.where(shared, total, owned).astype(bf)
+
+    for i in range(1, 8):
+        wo_arrival((me + i) % 8).wait_recv()
+    total = wo_in[0].astype(f32)
+    for t in range(1, 8):
+        total = total + wo_in[t].astype(f32)
+    result[ctx, dp, pl.ds(48, 16)] = total.astype(bf)
+
 
     def g_push(i):
         return copy_to(
@@ -1658,27 +1831,20 @@
     for d in range(8):
         g_sib_arrival(d).wait_recv()
         g_relay(d).wait_send()
-    for i in range(1, 8):
-        out_arrival((dp + i) % 8).wait_recv()
-    total = resid_ref[...] + out_own[dp].astype(f32)
-    for i in range(1, 8):
-        total = total + out_in[(dp + i) % 8].astype(f32)
-    output_ref[...] = total.astype(bf)
-    reduce_10()
+    reduce_9()
     store = pltpu.make_async_copy(reduced, reduced_ref, load_sem.at[9])
     store.start()
-    pack_ref[...] = result[...].reshape(512, 1024)
+    pack_ref[...] = result[...]
     for i in range(1, 8):
         dh_push(i).wait_send()
-        t_push(i).wait_send()
-        a_push(i).wait_send()
         s_push(i).wait_send()
         o_push(i).wait_send()
         n_push(i).wait_send()
         rs_push(i).wait_send()
         m_push(i).wait_send()
         g_push(i).wait_send()
-        out_push(i).wait_send()
+    for i in range(1, 8):
+        wo_hop(i).wait_send()
     store.wait()
 
 
@@ -1693,11 +1859,11 @@
         out_shape=(
             shape((128, 1024), bf),
             shape((8, 128), f32),
-            shape((512, 1024), bf),
+            shape((2, 8, 64, 512), bf),
             shape((128, 1024), bf),
             shape((3072, 1024), bf),
         ),
-        in_specs=[vmem] * 15 + [hbm] * 10,
+        in_specs=[vmem] * 15 + [hbm] * 11,
         out_specs=(vmem, vmem, vmem, vmem, hbm),
         scratch_shapes=[
             pltpu.VMEM((8, 128, 1024), bf),
@@ -1711,10 +1877,12 @@
             pltpu.VMEM((2, 32, 1024), f32),
             pltpu.VMEM((8, 1024), f32),
             pltpu.VMEM((128, 1024), f32),
-            pltpu.VMEM((8, 128, 1024), bf),
+            pltpu.VMEM((8, 128, 128), bf),
+            pltpu.VMEM((2, 8, 128, 512), bf),
+            pltpu.VMEM((8, 16, 512), bf),
             pltpu.VMEM((8, 128, 128), bf),
             pltpu.VMEM((8, 128, 128), bf),
-            pltpu.VMEM((8, 48, 1024), bf),
+            pltpu.VMEM((8, 48, 512), bf),
             pltpu.VMEM((4, 64, 512), bf),
             pltpu.VMEM((4, 512, 64), bf),
             pltpu.VMEM((4, 64, 512), bf),
@@ -1728,19 +1896,18 @@
             pltpu.VMEM((128, 1024), bf),
             pltpu.VMEM((128, 1024), bf),
             pltpu.VMEM((8, 192, 128), f32),
-            pltpu.VMEM((8, 8, 128), f32),
-            pltpu.VMEM((8, 8, 8, 128), f32),
+            pltpu.VMEM((2, 8, 128), f32),
+            pltpu.VMEM((8, 2, 8, 128), f32),
             pltpu.VMEM((8, 256, 128), bf),
             pltpu.VMEM((8, 256, 128), bf),
-            pltpu.VMEM((128, 1024), bf),
-            pltpu.VMEM((512, 1024), bf),
-            pltpu.VMEM((256, 1024), bf),
-            pltpu.VMEM((8, 32, 1024), bf),
-            pltpu.VMEM((2, 8, 32, 1024), bf),
+            pltpu.VMEM((2, 384, 512), bf),
+            pltpu.VMEM((384, 512), bf),
+            pltpu.VMEM((8, 48, 512), bf),
+            pltpu.VMEM((2, 8, 64, 512), bf),
             pltpu.VMEM((8, 8, 128), f32),
             pltpu.VMEM((8, 8, 128), f32),
             pltpu.VMEM((2, 8, 128), f32),
-            sem((11,)),
+            sem((12,)),
         ]
         + [sem((8,))] * 8
         + [sem((2,))]
@@ -1751,20 +1918,21 @@
         + [
             pltpu.VMEM((3072, 1024), bf),
             pltpu.VMEM((3072, 1024), bf),
-            pltpu.VMEM((2, 192, 1024), bf),
-            pltpu.VMEM((2, 2, 192, 1024), bf),
-            pltpu.VMEM((192, 1024), bf),
-            pltpu.VMEM((4, 192, 1024), bf),
-            pltpu.VMEM((2, 96, 1024), bf),
-            pltpu.VMEM((2, 192, 1024), bf),
-            sem((30,)),
-            sem((30,)),
-            pltpu.VMEM((8, 128, 1024), bf),
-            pltpu.VMEM((8, 128, 1024), bf),
-            pltpu.VMEM((8, 128, 1024), bf),
-            sem((2,)),
-            sem((8,)),
-            sem((8,)),
+            pltpu.VMEM((2, 240, 1024), bf),
+            pltpu.VMEM((240, 1024), bf),
+            pltpu.VMEM((144, 1024), bf),
+            pltpu.VMEM((144, 1024), bf),
+            pltpu.VMEM((2, 144, 1024), bf),
+            sem((46,)),
+            sem((46,)),
+            pltpu.VMEM((8, 128, 1536), bf),
+            pltpu.VMEM((8, 128, 1536), bf),
+            pltpu.VMEM((2, 2, 64, 1536), bf),
+            pltpu.VMEM((2, 2, 128, 1536), bf),
+            pltpu.VMEM((128, 1536), bf),
+            sem((4,)),
+            sem((9,)),
+            sem((9,)),
         ],
         compiler_params=pltpu.CompilerParams(
             collective_id=3, has_side_effects=True, vmem_limit_bytes=56 << 20
@@ -1773,6 +1941,118 @@
             flops=10_000_000_000, bytes_accessed=20_000_000, transcendentals=4_000_000
         ),
     )(*small, *large, table)
+
+
+def finish_kernel(
+    reduced_ref,
+    out_ref,
+    grad_x_ref,
+    pack_ref,
+    norm1_ref,
+    gate_ref,
+    up_ref,
+    down_ref,
+    out_copy_ref,
+    grad_x_copy_ref,
+    w_q_ref,
+    w_k_ref,
+    w_v_ref,
+    q_gain_ref,
+    k_gain_ref,
+    w_out_ref,
+    norm2_ref,
+    router_ref,
+    norm1_copy_ref,
+    rounded,
+    wide,
+    load_sem,
+    store_sem,
+):
+    f32 = jnp.float32
+    loads = [
+        pltpu.make_async_copy(reduced_ref.at[pl.ds(256 * n, 256)], rounded.at[n], load_sem.at[n])
+        for n in range(12)
+    ]
+    passed = [
+        pltpu.make_async_copy(out_ref, out_copy_ref, load_sem.at[12]),
+        pltpu.make_async_copy(grad_x_ref, grad_x_copy_ref, load_sem.at[13]),
+    ]
+    for copy in loads + passed:
+        copy.start()
+    def rows(start, count):
+        parts = []
+        for c in range(2):
+            pieces = []
+            for d in range(start // 48, (start + count - 1) // 48 + 1):
+                first, last = max(start, 48 * d) - 48 * d, min(start + count, 48 * d + 48) - 48 * d
+                pieces.append(pack_ref[c, d, first:last, :])
+            parts.append(jnp.concatenate(pieces, 0))
+        return jnp.concatenate(parts, 1).astype(f32)
+
+    w_q_ref[...] = jnp.transpose(rows(0, 128))
+    w_k_ref[...] = rows(128, 64)
+    w_v_ref[...] = rows(192, 64)
+    router_ref[...] = rows(256, 32)
+    norm2_ref[...] = rows(288, 16)[0:1]
+    gains = rows(304, 16)
+    q_gain_ref[...] = gains[0:1, 0:128]
+    k_gain_ref[...] = gains[0:1, 128:192]
+    for d in range(8):
+        for c in range(2):
+            w_out_ref[16 * d : 16 * d + 16, 512 * c : 512 * c + 512] = pack_ref[c, d, 48:64, :].astype(f32)
+    norm1_copy_ref[...] = norm1_ref[...]
+    stores = []
+    for n in range(12):
+        loads[n].wait()
+        wide[n] = rounded[n].astype(f32)
+        if n < 8:
+            rows = pl.ds(256 * (n % 4), 256)
+            for m, ref in enumerate((gate_ref, up_ref)):
+                src = wide.at[n, :, pl.ds(512 * m, 512)]
+                stores.append(pltpu.make_async_copy(src, ref.at[n // 4, rows], store_sem.at[2 * n + m]))
+        else:
+            rows = pl.ds(256 * (n % 2), 256)
+            stores.append(
+                pltpu.make_async_copy(wide.at[n], down_ref.at[n // 2 - 4, rows], store_sem.at[n + 8])
+            )
+        for store in stores[-2:] if n < 8 else stores[-1:]:
+            store.start()
+    for copy in stores + passed:
+        copy.wait()
+
+
+def finish(reduced, out, grad_x, pack, norm1):
+    bf, f32 = jnp.bfloat16, jnp.float32
+    vmem, hbm = pl.BlockSpec(memory_space=pltpu.VMEM), pl.BlockSpec(memory_space=pl.ANY)
+    shape = jax.ShapeDtypeStruct
+    return pl.pallas_call(
+        finish_kernel,
+        out_shape=(
+            shape((2, 1024, 512), f32),
+            shape((2, 1024, 512), f32),
+            shape((2, 512, 1024), f32),
+            shape((128, 1024), bf),
+            shape((128, 1024), bf),
+            shape((1024, 128), f32),
+            shape((64, 1024), f32),
+            shape((64, 1024), f32),
+            shape((1, 128), f32),
+            shape((1, 64), f32),
+            shape((128, 1024), f32),
+            shape((1, 1024), f32),
+            shape((32, 1024), f32),
+            shape((8, 128), f32),
+        ),
+        in_specs=[hbm] + [vmem] * 4,
+        out_specs=(hbm,) * 5 + (vmem,) * 9,
+        scratch_shapes=[
+            pltpu.VMEM((12, 256, 1024), bf),
+            pltpu.VMEM((12, 256, 1024), f32),
+            pltpu.SemaphoreType.DMA((14,)),
+            pltpu.SemaphoreType.DMA((20,)),
+        ],
+        compiler_params=pltpu.CompilerParams(vmem_limit_bytes=62 << 20),
+    )(reduced, out, grad_x, pack, norm1)
 
 
 def shards(
@@ -1794,7 +2074,7 @@
     cotangent,
 ):
     f32, bf = jnp.float32, jnp.bfloat16
-    rows2, gates, resid, rows1, raw, inv, q_t, kv, lse, heads, w_out_all, dy_all, w_t = attention(
+    rows2, gates, resid, rows1, raw, inv, q_t, kv, lse, heads, w_out_all, dy_all, w_t, heads_all = attention(
         hidden_in,
         cotangent,
         segment,
@@ -1830,25 +2110,39 @@
             inv,
             lse,
         ),
-        (rows1, raw, q_t, kv, heads, w_out_all, w_all, grads.reshape(3072, 1024), out_part),
+        (rows1, raw, q_t, kv, heads, heads_all, w_out_all, w_all, grads, out_part),
     )
-    grads = grads.astype(f32)
-    gate_up = grads[:2048].reshape(2, 1024, 1024)
+    (
+        gate,
+        up,
+        down,
+        output,
+        grad_x,
+        w_q,
+        w_k,
+        w_v,
+        q_g,
+        k_g,
+        w_o,
+        norm2_sum,
+        grad_router,
+        norm1_sum,
+    ) = finish(grads, output, grad_x, pack, norm1_sum)
     return (
         output,
         grad_x,
         norm1_sum.reshape(1024),
-        pack[0:128].T.astype(f32),
-        pack[128:192].T.astype(f32),
-        pack[192:256].T.astype(f32),
-        pack[417, :128].astype(f32),
-        pack[417, 128:192].astype(f32),
-        pack[256:384].astype(f32),
-        pack[416].astype(f32),
-        pack[384:416].T.astype(f32),
-        gate_up[:, :, :512],
-        gate_up[:, :, 512:],
-        grads[2048:].reshape(2, 512, 1024),
+        w_q,
+        w_k.T,
+        w_v.T,
+        q_g.reshape(128),
+        k_g.reshape(64),
+        w_o,
+        norm2_sum.reshape(1024),
+        grad_router.T,
+        gate,
+        up,
+        down,
     )
 
 

time: 348 us -> 285 us (0.82)
  Pallas kernels: 325 us -> 284 us
  local copies, waits for them, and re-layouts: 12.7 us -> 0 us
  other arithmetic: 9.07 us -> 0 us
    pallas_call x1, Pallas kernels: 180 us -> 115 us  [backward(): pl.pallas_call(backward_kernel, out_shape=(shape((128, 1024), bf), shape(...]
    pallas_call x1, Pallas kernels: 76.3 us -> 93.5 us  [moe(): pl.pallas_call(moe_kernel, out_shape=(jax.ShapeDtypeStruct((128, 1024), f...]
    slice x3 -> x0, local copies, waits for them, and re-layouts: 9.67 us -> none  [the longest x1 4.42 us: shards(): gate_up[:, :, 512:]]
    convert_element_type x6 -> x0, other arithmetic: 9.07 us -> none  [the longest x1 1.95 us: shards(): pack[192:256].T.astype(f32)]
    pallas_call x0 -> x1, Pallas kernels: none -> 9.05 us  [finish(): pl.pallas_call(finish_kernel, out_shape=(shape((2, 1024, 512), f32), shap...]
where the time goes in v4:
time: 285 us
  Pallas kernels  284 us (100%)
    pallas_call x1, Pallas kernels, backward(): pl.pallas_call(backward_kernel, out_shape=(shape((128, 1024), bf), shape(...  115 us
    pallas_call x1, Pallas kernels, moe(): pl.pallas_call(moe_kernel, out_shape=(jax.ShapeDtypeStruct((128, 1024), f...  93.5 us
    pallas_call x1, Pallas kernels, attention(): pl.pallas_call(attention_kernel, out_shape=(shape((128, 1024), bf), shape...  66.5 us
    pallas_call x1, Pallas kernels, finish(): pl.pallas_call(finish_kernel, out_shape=(shape((2, 1024, 512), f32), shap...  9.05 us

profile of v4, /device:TPU:1, one launch (start us, length us, event | category | flops | bytes accessed | tf_op | source)
XLA Modules:
  0.0 284.9 jit_solution(16994593819509361718)
XLA Ops:
  0.6 66.5 %shard_map.281 = (bf16[128,1024]{1,0:T(8,128)(2,1)}, f32[32,128]{1,0:T(8,128)}, f32[128,1024]{1,0:T(8,128)}, bf16[8,128,1024]{2,1,0:T(8,128)(2,1)}, f32[8,256,12...) custom-call(bf16[128,1024]{1,0:T(8,128)(2,1)} %x_ref.3, ...), custom_call_target="tpu_custom_call" | custom-call | flops 5000000000 | bytes 20000000 | tf_op jit(solution)/shard_map/pallas_call | solution.py:986
  67.2 93.5 %shard_map.282 = (f32[128,1024]{1,0:T(8,128)}, f32[32,128]{1,0:T(8,128)}, bf16[16,128,1024]{2,1,0:T(8,128)(2,1)}, bf16[3072,1024]{1,0:T(8,128)(2,1)}, bf16[8,256,1024]{2,1,0:T(8,128)(2,1)}) custom-call(bf16[128,1024]{1,0:T(8,128)(2,1)} %get-tuple-element.52.rows_ref.rows2_ref, f32[32,128]{1,0:T(8,128)} %get-tuple-element.53.gate_ref.gates_ref, ...), custom_call_target="tpu_custom_call" | custom-call | flops 20000000000 | bytes 30000000 | tf_op jit(solution)/shard_map/pallas_call | solution.py:534
  160.7 114.9 %shard_map.283 = (bf16[128,1024]{1,0:T(8,128)(2,1)}, f32[8,128]{1,0:T(8,128)}, bf16[2,8,64,512]{3,2,1,0:T(8,128)(2,1)}, bf16[128,1024]{1,0:T(8,128)(2,1)}, bf16[3072,1024]{1,0:T(8,128)(2,1)}) custom-call(bf16[128,1024]{1,0:T(8,128)(2,1)} %x_ref.3, bf16[128,1024]{1,0:T(8,128)(2,1)} %dy_ref.3, f32[128,1024]{1,0:T(8,128)} %get-tuple-element.56.d_rows_ref, ...), custom_call_target="tpu_custom_call" | custom-call | flops 10000000000 | bytes 20000000 | tf_op jit(solution)/shard_map/pallas_call | solution.py:1857
  275.7 9.1 %shard_map.284 = (f32[2,1024,512]{2,1,0:T(8,128)}, f32[2,1024,512]{2,1,0:T(8,128)}, f32[2,512,1024]{2,1,0:T(8,128)}, bf16[128,1024]{1,0:T(8,128)(2,1)}, bf16[128...) custom-call(bf16[3072,1024]{1,0:T(8,128)(2,1)} %get-tuple-element.71, ...), custom_call_target="tpu_custom_call" | custom-call | tf_op jit(solution)/shard_map/pallas_call | solution.py:2028

commit v5 on v4

--- a/solution.py
+++ b/solution.py
@@ -52,27 +52,27 @@
 def across(a, b, flip):
     dp, ctx = lax.axis_index("dp"), lax.axis_index("ctx")
     x, y = dp % 4, dp // 4
-    odd = a % 2
-    by_x = odd * (1 + 2 * b) + (1 - odd) * a
-    by_y = (1 - odd) * b + odd * (1 - a // 2)
+    mid = ((a + 1) // 2) % 2
+    by_x = mid * (1 + 2 * b) + (1 - mid) * 2 * (a // 3)
+    by_y = mid * (a // 2) + (1 - mid) * b
     return ((y + by_y) % 2) * 4 + (x + by_x) % 4, (ctx + flip) % 2
 
 
 def opposite(a, b):
-    return b + (a % 2) * (1 - 2 * b)
+    return b + (((a + 1) // 2) % 2) * (1 - 2 * b)
 
 
 def first_half(z, y, k, c):
-    return pl.ds(pl.multiple_of(240 * (((z + k) % 4) * 2 + c), 16), 240)
+    return pl.ds(pl.multiple_of(304 * (((z + k) % 4) * 2 + c), 16), 304)
 
 
 def second_half(z, y, k, c):
-    return pl.ds(pl.multiple_of(1920 + 144 * (((z + k) % 4) * 2 + c), 16), 144)
+    return pl.ds(pl.multiple_of(2432 + 80 * (((z + k) % 4) * 2 + c), 16), 80)
 
 
 def piece(z, y, k, c, part):
-    start = 1920 + 144 * (((z + k) % 4) * 2 + c) + 80 * part
-    return pl.ds(pl.multiple_of(start, 16), (80, 64)[part])
+    start = 2432 + 80 * (((z + k) % 4) * 2 + c) + 48 * part
+    return pl.ds(pl.multiple_of(start, 16), (48, 32)[part])
 
 
 def add_rows(ref, place, *parts):
@@ -137,6 +137,7 @@
     rb,
     r_send,
     r_recv,
+    keep_sem,
 ):
     tensor = lax.axis_index("tensor")
     dp, ctx = lax.axis_index("dp"), lax.axis_index("ctx")
@@ -176,20 +177,20 @@
         pl.semaphore_signal(barrier, inc=1, device_id=side(i), device_id_type=MESH)
     pl.semaphore_wait(barrier, 22)
 
-    right, left, partner = to(3, 0, 0), to(3, 1, 0), to(0, 1, 0)
+    right, left, partner = to(1, 0, 0), to(1, 1, 0), to(0, 1, 0)
     sibling = to(0, 0, 1)
     low, high = pl.ds(0, 64), pl.ds(64, 64)
 
     def hop(n):
         src, dst, device = (
-            (rows_all.at[0], rows_all.at[14], right),
-            (rows_all.at[0], rows_all.at[12], left),
+            (rows_all.at[0], rows_all.at[6], right),
+            (rows_all.at[0], rows_all.at[4], left),
             (rows_all.at[0], rows_all.at[2], partner),
-            (rows_all.at[14, low], rows_all.at[8, low], right),
-            (rows_all.at[12, high], rows_all.at[8, high], left),
-            (rows_all.at[2], rows_all.at[6], right),
-            (rows_all.at[2], rows_all.at[4], left),
-            (rows_all.at[8], rows_all.at[10], partner),
+            (rows_all.at[6, low], rows_all.at[12, low], right),
+            (rows_all.at[4, high], rows_all.at[12, high], left),
+            (rows_all.at[2], rows_all.at[10], right),
+            (rows_all.at[2], rows_all.at[8], left),
+            (rows_all.at[12], rows_all.at[14], partner),
         )[n]
         return copy_to(src, dst, ag_send.at[n], ag_recv.at[n], device)
 
@@ -247,14 +248,14 @@
 
     def rs_hop(n):
         src, dst, device = (
-            (din_all.at[4], rs_a.at[0], right),
-            (din_all.at[6], rs_a.at[1], left),
-            (din_all.at[10], rs_b, partner),
+            (din_all.at[8], rs_a.at[0], right),
+            (din_all.at[10], rs_a.at[1], left),
+            (din_all.at[14], rs_b, partner),
             (din_all.at[2], rs_c, partner),
-            (din_all.at[8, low], rs_d.at[0], right),
-            (din_all.at[8, high], rs_d.at[1], left),
-            (din_all.at[12], rs_e.at[0], right),
-            (din_all.at[14], rs_e.at[1], left),
+            (din_all.at[12, low], rs_d.at[0], right),
+            (din_all.at[12, high], rs_d.at[1], left),
+            (din_all.at[4], rs_e.at[0], right),
+            (din_all.at[6], rs_e.at[1], left),
         )[n]
         return copy_to(src, dst, rs_send.at[n], rs_recv.at[n], device)
 
@@ -369,7 +370,7 @@
         def _():
             dg_push(a, b, flip).start()
 
-    for n, ci in ((0, 7), (1, 6)):
+    for n, ci in ((0, 3), (1, 2)):
         hop(n).wait_recv()
         hop(3 + n).start()
         relay(ci).start()
@@ -394,15 +395,11 @@
         @pl.when(a == 2)
         def _():
             post(2, 3)
-            rs_go(0, 1)
 
         @pl.when(a == 3)
         def _():
             post(4, 5)
-            rs_go(2)
-            rs_got(0, 1)
-            plus(2, slice(None), rs_a[0], rs_a[1])
-            rs_go(3)
+            rs_go(0, 1)
 
         lax.fori_loop(0, 2, lambda j, c: (expert(j), c)[1], 0)
         lax.fori_loop(0, 4, lambda q, c: (spread(a, q), c)[1], 0)
@@ -414,26 +411,33 @@
             hop(3).wait_recv()
             hop(4).wait_recv()
             hop(7).start()
-            relay(4).start()
-            for n, ci in ((5, 3), (6, 2)):
+            relay(6).start()
+            for ci in (2, 3):
+                relay(ci).wait_recv()
+
+        @pl.when(a == 1)
+        def _():
+            for n, ci in ((5, 5), (6, 4)):
                 hop(n).wait_recv()
                 relay(ci).start()
-            for ci in (2, 3):
+            for ci in (4, 5):
                 relay(ci).wait_recv()
 
-        @pl.when(a == 1)
+        @pl.when(a == 2)
         def _():
             hop(7).wait_recv()
-            relay(5).start()
-            for ci in (4, 5, 6, 7):
+            relay(7).start()
+            for ci in (6, 7):
                 relay(ci).wait_recv()
 
         return carry
 
     lax.fori_loop(0, 4, step, 0)
-    rs_got(2)
-    plus(8, slice(None), rs_b[...])
-    rs_go(4, 5)
+    post(7, 6)
+    rs_go(2)
+    rs_got(0, 1)
+    plus(2, slice(None), rs_a[0], rs_a[1])
+    rs_go(3)
 
     def round_rows(n, carry):
         place = pl.ds(pl.multiple_of(n * 128, 128), 128)
@@ -460,14 +464,36 @@
         )[n]
         return copy_to(w_full.at[place], dst, r_send.at[n], r_recv.at[n], device)
 
-    for n in (0, 1, 4, 2, 3, 5, 6):
+    for n in range(4):
         grad_hop(n).start()
-    post(6, 7)
+
+    def keep(n, place):
+        return pltpu.make_async_copy(w_full.at[place], grad_ref.at[place], keep_sem.at[n])
+
+    first_places = [first_half(z, y, k, c) for k, c in ((1, 1), (3, 0), (2, 0), (2, 1))]
+    first_places += [second_half(z, y, k, 1 - y) for k in range(4)] + [second_half(z, y, 0, y)]
+    last_places = [
+        first_half(z, y, 1, 0),
+        first_half(z, y, 3, 1),
+        second_half(z, y, 2, y),
+        first_half(z, y, 0, 1),
+        first_half(z, y, 0, 0),
+        second_half(z, y, 1, y),
+        second_half(z, y, 3, y),
+    ]
+    for n, place in enumerate(first_places):
+        keep(n, place).start()
+    rs_got(2)
+    plus(12, slice(None), rs_b[...])
+    rs_go(4, 5)
+    grad_hop(4).start()
+    grad_hop(5).start()
+    grad_hop(6).start()
     rs_got(4)
-    plus(12, low, rs_d[0])
+    plus(4, low, rs_d[0])
     rs_go(6)
     rs_got(5)
-    plus(14, high, rs_d[1])
+    plus(6, high, rs_d[1])
     rs_go(7)
     for i in range(1, 8):
         t = (tensor + i) % 8
@@ -505,26 +531,17 @@
         w_push(i).wait_send()
         w_relay(t).wait_send()
     w_own.wait()
-    grad_hop(0).wait_recv()
-    add_rows(w_full, first_half(z, y, 1, 0), ra_0[0])
-    grad_hop(1).wait_recv()
-    add_rows(w_full, first_half(z, y, 3, 1), ra_0[1])
-    grad_hop(4).wait_recv()
-    add_rows(w_full, second_half(z, y, 2, y), rb[0])
-    grad_hop(2).wait_recv()
-    add_rows(w_full, first_half(z, y, 0, 1), ra_1[0])
-    grad_hop(3).wait_recv()
-    add_rows(w_full, first_half(z, y, 0, 0), ra_1[1])
-    grad_hop(5).wait_recv()
-    add_rows(w_full, second_half(z, y, 1, y), rb[1])
-    grad_hop(6).wait_recv()
-    add_rows(w_full, second_half(z, y, 3, y), rb[2])
-    store_grad = pltpu.make_async_copy(w_full, grad_ref, store_sem.at[1])
-    store_grad.start()
+    for n, (arrived, got) in enumerate(
+        ((0, ra_0.at[0]), (1, ra_0.at[1]), (4, rb.at[0]), (2, ra_1.at[0]), (3, ra_1.at[1]), (5, rb.at[1]), (6, rb.at[2]))
+    ):
+        grad_hop(arrived).wait_recv()
+        add_rows(w_full, last_places[n], got[...])
+        keep(9 + n, last_places[n]).start()
     for n in range(7):
         grad_hop(n).wait_send()
     store_out.wait()
-    store_grad.wait()
+    for n, place in enumerate(first_places + last_places):
+        keep(n, place).wait()
 
 
 def moe(rows, gates, dy, w_gate, w_up, w_down, w_t):
@@ -580,11 +597,12 @@
             sem((2,)),
             sem((16,)),
             sem((8, 2)),
-            pltpu.VMEM((2, 240, 1024), bf),
-            pltpu.VMEM((2, 240, 1024), bf),
-            pltpu.VMEM((3, 144, 1024), bf),
+            pltpu.VMEM((2, 304, 1024), bf),
+            pltpu.VMEM((2, 304, 1024), bf),
+            pltpu.VMEM((3, 80, 1024), bf),
             sem((7,)),
             sem((7,)),
+            sem((16,)),
         ],
         compiler_params=pltpu.CompilerParams(
             collective_id=1, has_side_effects=True, vmem_limit_bytes=60 << 20
@@ -713,18 +731,18 @@
         )[n]
         return copy_to(place, place, h_send.at[n], h_recv.at[n], device)
 
-    right, left, partner = to(3, 0, 0), to(3, 1, 0), to(0, 1, 0)
+    right, left, partner = to(1, 0, 0), to(1, 1, 0), to(0, 1, 0)
 
     def dy_hop(n):
         src, dst, device = (
-            (dy_all.at[0], dy_all.at[14], right),
-            (dy_all.at[0], dy_all.at[12], left),
+            (dy_all.at[0], dy_all.at[6], right),
+            (dy_all.at[0], dy_all.at[4], left),
             (dy_all.at[0], dy_all.at[2], partner),
-            (dy_all.at[14, low], dy_all.at[8, low], right),
-            (dy_all.at[12, high], dy_all.at[8, high], left),
-            (dy_all.at[2], dy_all.at[6], right),
-            (dy_all.at[2], dy_all.at[4], left),
-            (dy_all.at[8], dy_all.at[10], partner),
+            (dy_all.at[6, low], dy_all.at[12, low], right),
+            (dy_all.at[4, high], dy_all.at[12, high], left),
+            (dy_all.at[2], dy_all.at[10], right),
+            (dy_all.at[2], dy_all.at[8], left),
+            (dy_all.at[12], dy_all.at[14], partner),
         )[n]
         return copy_to(src, dst, dy_send.at[n], dy_recv.at[n], device)
 
@@ -805,7 +823,7 @@
         half = w_all.at[t, pl.ds(pl.multiple_of(c * 64, 64), 64)]
         return copy_to(half, half, w_send.at[0], w_recv.at[t, c], sibling)
 
-    for n, ci in ((0, 7), (1, 6)):
+    for n, ci in ((0, 3), (1, 2)):
         dy_hop(n).wait_recv()
         dy_hop(3 + n).start()
         dy_relay(ci).start()
@@ -844,15 +862,14 @@
     kv_push = copy_to(kv_own, kv_sib, kv_sem.at[0], kv_sem.at[1], sibling)
     kv_push.start()
 
-    key_row = lax.broadcasted_iota(jnp.int32, (256, 256), 0).astype(f32)
-    query_lane = lax.broadcasted_iota(jnp.int32, (256, 256), 1).astype(f32)
+    key_row = lax.broadcasted_iota(jnp.int32, (256, 512), 0).astype(f32)
+    query_lane = (lax.broadcasted_iota(jnp.int32, (256, 512), 1) % 256).astype(f32)
     base = (ctx * 1024).astype(f32)
 
-    def attend(n, carry):
-        i, h = n // 2, n % 2
+    def attend(i, carry):
         at = pl.ds(pl.multiple_of(i * 256, 256), 256)
-        q = q_t[pl.ds(pl.multiple_of(h * 64, 64), 64), at] * 0.125
-        begin = starts[0:1, at]
+        q = jnp.concatenate([q_t[0:64, at], q_t[64:128, at]], 1) * 0.125
+        begin = jnp.concatenate([starts[0:1, at]] * 2, 1)
 
         def block(keys, values, first_key, state, causal):
             top, total, acc = state
@@ -868,7 +885,7 @@
             acc = acc * shrink + jnp.dot(values, e.astype(bf), preferred_element_type=f32)
             return new_top, total, acc
 
-        state = (jnp.full((1, 256), MASKED, f32), jnp.zeros((1, 256), f32), jnp.zeros((64, 256), f32))
+        state = (jnp.full((1, 512), MASKED, f32), jnp.zeros((1, 512), f32), jnp.zeros((64, 512), f32))
         state = block(
             k_own[at, :], kv_own[64:128, at], base + (i * 256).astype(f32), state, True
         )
@@ -885,10 +902,13 @@
 
         top, total, acc = lax.fori_loop(0, 4 * ctx, other, state)
         out = (acc / total).astype(bf)
-        hs = pl.ds(pl.multiple_of(h * 64, 64), 64)
-        heads[2 * i, hs, :] = out[:, :128]
-        heads[2 * i + 1, hs, :] = out[:, 128:]
-        lse_ref[h, 0:1, at] = top + jnp.log(total)
+        lse = top + jnp.log(total)
+        for h in range(2):
+            for n in range(2):
+                heads[2 * i + n, 64 * h : 64 * h + 64, :] = out[
+                    :, 256 * h + 128 * n : 256 * h + 128 * n + 128
+                ]
+            lse_ref[h, 0:1, at] = lse[:, 256 * h : 256 * h + 256]
         return carry
 
     kv_push.wait()
@@ -901,9 +921,9 @@
     dy_hop(3).wait_recv()
     dy_hop(4).wait_recv()
     dy_hop(7).start()
-    dy_relay(4).start()
+    dy_relay(6).start()
     lax.fori_loop(0, 8, straighten, 0)
-    lax.fori_loop(0, 8, attend, 0)
+    lax.fori_loop(0, 4, attend, 0)
 
     def o_push(i):
         return copy_to(
@@ -933,7 +953,7 @@
 
     lax.fori_loop(1, 8, pass_on, 0)
 
-    for n, ci in ((5, 3), (6, 2), (7, 5)):
+    for n, ci in ((5, 5), (6, 4), (7, 7)):
         dy_hop(n).wait_recv()
         dy_relay(ci).start()
     for i in range(1, 8):
@@ -1173,6 +1193,7 @@
     os_sem,
     out_send,
     out_recv,
+    keep_sem,
 ):
     f32, bf = jnp.float32, jnp.bfloat16
     dp, ctx, me = lax.axis_index("dp"), lax.axis_index("ctx"), lax.axis_index("tensor")
@@ -1193,11 +1214,11 @@
     )
 
     def a_rows(k, c, s=0):
-        start = 240 * (((z + k) % 4) * 2 + c) + 128 * s
-        return pl.ds(pl.multiple_of(start, 16), (128, 112)[s])
+        start = 304 * (((z + k) % 4) * 2 + c) + 160 * s
+        return pl.ds(pl.multiple_of(start, 16), (160, 144)[s])
 
     def of_part(s):
-        return pl.ds(128 * s, (128, 112)[s])
+        return pl.ds(160 * s, (160, 144)[s])
 
     def b_rows(k, c):
         return second_half(z, y, k, c)
@@ -1211,7 +1232,7 @@
         elif n < 5:
             part = n - 3
             src, to = grads.at[piece(z, y, 2, y, part)], (up, down)[part]
-            dst = (rb2.at[pl.ds(0, 80)], rb2.at[pl.ds(80, 64)])[part]
+            dst = (rb2.at[pl.ds(0, 48)], rb2.at[pl.ds(48, 32)])[part]
         elif n == 5:
             src, dst, to = grads.at[a_rows(0, other, s)], ra4.at[of_part(s)], pair
         elif n == 6:
@@ -1258,11 +1279,9 @@
 
     def reduce_2():
         got(3, 4)
-        add_rows(grads, piece(z, y, 1, y, 0), rb2[0:80])
-        add_rows(grads, piece(z, y, 3, y, 1), rb2[80:144])
+        add_rows(grads, piece(z, y, 1, y, 0), rb2[0:48])
+        add_rows(grads, piece(z, y, 3, y, 1), rb2[48:80])
         go(6, 7)
-        got(2)
-        add_rows(grads, b_rows(0, y), rb1[...])
 
     def reduce_3(s):
         got(5, s=s)
@@ -1271,8 +1290,8 @@
         go(8, 9, 10, s=s)
 
     def reduce_4():
-        got(6, 7)
-        add_rows(grads, b_rows(0, y), rb3[0], rb3[1])
+        got(6, 7, 2)
+        add_rows(grads, b_rows(0, y), rb1[...], rb3[0], rb3[1])
         reduced[b_rows(0, y), :] = grads[b_rows(0, y), :]
         go(15, 16, 19)
 
@@ -1301,7 +1320,19 @@
         got(17, 18)
         go(22)
 
+    def keep(n, place):
+        return pltpu.make_async_copy(reduced.at[place], reduced_ref.at[place], keep_sem.at[n])
+
+    keep_places = (
+        [a_rows(0, c, s) for c in range(2) for s in range(2)]
+        + [a_rows(k, c, s) for k in (1, 3) for c in range(2) for s in range(2)]
+        + [a_rows(2, c, s) for c in range(2) for s in range(2)]
+        + [pl.ds(2432, 640)]
+    )
+
     def reduce_9():
+        for n in range(4):
+            keep(n, keep_places[n]).start()
         for s in range(2):
 
             @pl.when(y == 0)
@@ -1312,8 +1343,14 @@
             def _():
                 got(9, 12, s=s)
 
+        for n in range(4, 12):
+            keep(n, keep_places[n]).start()
+        got(19, 20, 21, 22)
+        keep(16, keep_places[16]).start()
+        for s in range(2):
             got(13, 14, s=s)
-        got(19, 20, 21, 22)
+        for n in range(12, 16):
+            keep(n, keep_places[n]).start()
         for n in range(23):
             hop(n).wait_send()
         for n in (0, 1, 5, 8, 9, 10, 11, 12, 13, 14):
@@ -1433,6 +1470,9 @@
         pl.semaphore_signal(barrier, inc=1, device_id=chip(i), device_id_type=MESH)
     pl.semaphore_signal(barrier, inc=1, device_id=sibling, device_id_type=MESH)
 
+    pl.semaphore_wait(barrier, 15)
+    early.wait()
+    reduce_0()
     gates, d_gate = gates_ref[...], d_gate_ref[...]
     d_logits = gates * (d_gate - jnp.sum(gates * d_gate, 0, keepdims=True))
     d_normed = d_rows_ref[...] + lax.dot_general(
@@ -1456,7 +1496,6 @@
     d_heads = dot_nt(w_out[...].reshape(1024, 1024), datt).astype(bf)
     dh_send[...] = d_heads.reshape(8, 128, 128)
     dh_all[me] = dh_send[me]
-    pl.semaphore_wait(barrier, 15)
 
     def dh_push(i):
         return copy_to(
@@ -1484,8 +1523,6 @@
     pack_rows(pl.ds(288, 16), jnp.concatenate([norm2_part, jnp.zeros((15, 1024), f32)], 0))
     pack_rows(pl.ds(320, 64), jnp.zeros((64, 1024), f32))
 
-    loads[9].wait()
-    reduce_0()
     os_push.start()
     loads[10].wait()
 
@@ -1548,6 +1585,7 @@
         return carry
 
     lax.fori_loop(0, 8, lay_dh, 0)
+    reduce_1(0)
     key_row = lax.broadcasted_iota(jnp.int32, (256, 512), 0).astype(f32)
     query_lane = (lax.broadcasted_iota(jnp.int32, (256, 512), 1) % 256).astype(f32)
     base = (ctx * 1024).astype(f32)
@@ -1567,15 +1605,14 @@
         dq_acc[i] += jnp.dot(kv[0:64, ks], ds, preferred_element_type=f32)
 
     def hook_0():
-        reduce_1(0)
         reduce_2()
+        reduce_1(1)
 
     def hook_1():
         out_0()
-        reduce_1(1)
+        reduce_3(0)
 
     def hook_2():
-        reduce_3(0)
         reduce_4()
 
     def hook_3():
@@ -1832,8 +1869,6 @@
         g_sib_arrival(d).wait_recv()
         g_relay(d).wait_send()
     reduce_9()
-    store = pltpu.make_async_copy(reduced, reduced_ref, load_sem.at[9])
-    store.start()
     pack_ref[...] = result[...]
     for i in range(1, 8):
         dh_push(i).wait_send()
@@ -1845,7 +1880,8 @@
         g_push(i).wait_send()
     for i in range(1, 8):
         wo_hop(i).wait_send()
-    store.wait()
+    for n, place in enumerate(keep_places):
+        keep(n, place).wait()
 
 
 def backward(small, large):
@@ -1918,11 +1954,11 @@
         + [
             pltpu.VMEM((3072, 1024), bf),
             pltpu.VMEM((3072, 1024), bf),
-            pltpu.VMEM((2, 240, 1024), bf),
-            pltpu.VMEM((240, 1024), bf),
-            pltpu.VMEM((144, 1024), bf),
-            pltpu.VMEM((144, 1024), bf),
-            pltpu.VMEM((2, 144, 1024), bf),
+            pltpu.VMEM((2, 304, 1024), bf),
+            pltpu.VMEM((304, 1024), bf),
+            pltpu.VMEM((80, 1024), bf),
+            pltpu.VMEM((80, 1024), bf),
+            pltpu.VMEM((2, 80, 1024), bf),
             sem((46,)),
             sem((46,)),
             pltpu.VMEM((8, 128, 1536), bf),
@@ -1933,6 +1969,7 @@
             sem((4,)),
             sem((9,)),
             sem((9,)),
+            sem((17,)),
         ],
         compiler_params=pltpu.CompilerParams(
             collective_id=3, has_side_effects=True, vmem_limit_bytes=56 << 20

time: 285 us -> 267 us (0.937)
  Pallas kernels: 284 us -> 266 us
    pallas_call x1, Pallas kernels: 115 us -> 106 us  [backward(): pl.pallas_call(backward_kernel, out_shape=(shape((128, 1024), bf), shape(...]
    pallas_call x1, Pallas kernels: 66.5 us -> 58 us  [attention(): pl.pallas_call(attention_kernel, out_shape=(shape((128, 1024), bf), shape...]
where the time goes in v5:
time: 267 us
  Pallas kernels  266 us (100%)
    pallas_call x1, Pallas kernels, backward(): pl.pallas_call(backward_kernel, out_shape=(shape((128, 1024), bf), shape(...  106 us
    pallas_call x1, Pallas kernels, moe(): pl.pallas_call(moe_kernel, out_shape=(jax.ShapeDtypeStruct((128, 1024), f...  92.8 us
    pallas_call x1, Pallas kernels, attention(): pl.pallas_call(attention_kernel, out_shape=(shape((128, 1024), bf), shape...  58 us
    pallas_call x1, Pallas kernels, finish(): pl.pallas_call(finish_kernel, out_shape=(shape((2, 1024, 512), f32), shap...  9.05 us

profile of v5, /device:TPU:1, one launch (start us, length us, event | category | flops | bytes accessed | tf_op | source)
XLA Modules:
  0.0 266.7 jit_solution(17808339037212183160)
XLA Ops:
  0.6 58.0 %shard_map.281 = (bf16[128,1024]{1,0:T(8,128)(2,1)}, f32[32,128]{1,0:T(8,128)}, f32[128,1024]{1,0:T(8,128)}, bf16[8,128,1024]{2,1,0:T(8,128)(2,1)}, f32[8,256,12...) custom-call(bf16[128,1024]{1,0:T(8,128)(2,1)} %x_ref.3, ...), custom_call_target="tpu_custom_call" | custom-call | flops 5000000000 | bytes 20000000 | tf_op jit(solution)/shard_map/pallas_call | solution.py:1006
  58.6 92.8 %shard_map.282 = (f32[128,1024]{1,0:T(8,128)}, f32[32,128]{1,0:T(8,128)}, bf16[16,128,1024]{2,1,0:T(8,128)(2,1)}, bf16[3072,1024]{1,0:T(8,128)(2,1)}, bf16[8,256,1024]{2,1,0:T(8,128)(2,1)}) custom-call(bf16[128,1024]{1,0:T(8,128)(2,1)} %get-tuple-element.52.rows_ref.rows2_ref, f32[32,128]{1,0:T(8,128)} %get-tuple-element.53.gate_ref.gates_ref, ...), custom_call_target="tpu_custom_call" | custom-call | flops 20000000000 | bytes 30000000 | tf_op jit(solution)/shard_map/pallas_call | solution.py:551
  151.4 106.1 %shard_map.283 = (bf16[128,1024]{1,0:T(8,128)(2,1)}, f32[8,128]{1,0:T(8,128)}, bf16[2,8,64,512]{3,2,1,0:T(8,128)(2,1)}, bf16[128,1024]{1,0:T(8,128)(2,1)}, bf16[3072,1024]{1,0:T(8,128)(2,1)}) custom-call(bf16[128,1024]{1,0:T(8,128)(2,1)} %x_ref.3, bf16[128,1024]{1,0:T(8,128)(2,1)} %dy_ref.3, f32[128,1024]{1,0:T(8,128)} %get-tuple-element.56.d_rows_ref, ...), custom_call_target="tpu_custom_call" | custom-call | flops 10000000000 | bytes 20000000 | tf_op jit(solution)/shard_map/pallas_call | solution.py:1893
  257.5 9.1 %shard_map.284 = (f32[2,1024,512]{2,1,0:T(8,128)}, f32[2,1024,512]{2,1,0:T(8,128)}, f32[2,512,1024]{2,1,0:T(8,128)}, bf16[128,1024]{1,0:T(8,128)(2,1)}, bf16[128...) custom-call(bf16[3072,1024]{1,0:T(8,128)(2,1)} %get-tuple-element.71, ...), custom_call_target="tpu_custom_call" | custom-call | tf_op jit(solution)/shard_map/pallas_call | solution.py:2065

commit v6 on v5

--- a/solution.py
+++ b/solution.py
@@ -433,18 +433,9 @@
         return carry
 
     lax.fori_loop(0, 4, step, 0)
-    post(7, 6)
-    rs_go(2)
-    rs_got(0, 1)
-    plus(2, slice(None), rs_a[0], rs_a[1])
-    rs_go(3)
-
-    def round_rows(n, carry):
-        place = pl.ds(pl.multiple_of(n * 128, 128), 128)
+    def round_rows(place):
         w_full[place, :] = acc[place, :].astype(jnp.bfloat16)
-        return carry
-
-    lax.fori_loop(0, 24, round_rows, 0)
+
     z, y = tensor // 2, tensor % 2
     up, down, pair = (
         (dp, ctx, ((z + 1) % 4) * 2 + y),
@@ -464,8 +455,22 @@
         )[n]
         return copy_to(w_full.at[place], dst, r_send.at[n], r_recv.at[n], device)
 
-    for n in range(4):
+    for n in range(2):
+        round_rows(first_half(z, y, 2, n))
         grad_hop(n).start()
+    post(7, 6)
+    rs_go(2)
+    for n, k in ((2, 1), (3, 3)):
+        round_rows(first_half(z, y, k, 3 - n))
+        grad_hop(n).start()
+    rs_got(0, 1)
+    plus(2, slice(None), rs_a[0], rs_a[1])
+    rs_go(3)
+    for k, c in ((1, 0), (3, 1), (0, 0), (0, 1)):
+        round_rows(first_half(z, y, k, c))
+    for k in range(4):
+        for c in range(2):
+            round_rows(second_half(z, y, k, c))
 
     def keep(n, place):
         return pltpu.make_async_copy(w_full.at[place], grad_ref.at[place], keep_sem.at[n])

time: 267 us -> 264 us (0.989)
  Pallas kernels: 266 us -> 263 us
    pallas_call x1, Pallas kernels: 92.8 us -> 90.1 us  [moe(): pl.pallas_call(moe_kernel, out_shape=(jax.ShapeDtypeStruct((128, 1024), f...]
where the time goes in v6:
time: 264 us
  Pallas kernels  263 us (100%)
    pallas_call x1, Pallas kernels, backward(): pl.pallas_call(backward_kernel, out_shape=(shape((128, 1024), bf), shape(...  106 us
    pallas_call x1, Pallas kernels, moe(): pl.pallas_call(moe_kernel, out_shape=(jax.ShapeDtypeStruct((128, 1024), f...  90.1 us
    pallas_call x1, Pallas kernels, attention(): pl.pallas_call(attention_kernel, out_shape=(shape((128, 1024), bf), shape...  58 us
    pallas_call x1, Pallas kernels, finish(): pl.pallas_call(finish_kernel, out_shape=(shape((2, 1024, 512), f32), shap...  9.05 us

profile of v6, /device:TPU:1, one launch (start us, length us, event | category | flops | bytes accessed | tf_op | source)
XLA Modules:
  0.0 263.9 jit_solution(3347025265086903436)
XLA Ops:
  0.6 58.0 %shard_map.281 = (bf16[128,1024]{1,0:T(8,128)(2,1)}, f32[32,128]{1,0:T(8,128)}, f32[128,1024]{1,0:T(8,128)}, bf16[8,128,1024]{2,1,0:T(8,128)(2,1)}, f32[8,256,12...) custom-call(bf16[128,1024]{1,0:T(8,128)(2,1)} %x_ref.3, ...), custom_call_target="tpu_custom_call" | custom-call | flops 5000000000 | bytes 20000000 | tf_op jit(solution)/shard_map/pallas_call | solution.py:1011
  58.6 90.1 %shard_map.282 = (f32[128,1024]{1,0:T(8,128)}, f32[32,128]{1,0:T(8,128)}, bf16[16,128,1024]{2,1,0:T(8,128)(2,1)}, bf16[3072,1024]{1,0:T(8,128)(2,1)}, bf16[8,256,1024]{2,1,0:T(8,128)(2,1)}) custom-call(bf16[128,1024]{1,0:T(8,128)(2,1)} %get-tuple-element.52.rows_ref.rows2_ref, f32[32,128]{1,0:T(8,128)} %get-tuple-element.53.gate_ref.gates_ref, ...), custom_call_target="tpu_custom_call" | custom-call | flops 20000000000 | bytes 30000000 | tf_op jit(solution)/shard_map/pallas_call | solution.py:556
  148.7 106.0 %shard_map.283 = (bf16[128,1024]{1,0:T(8,128)(2,1)}, f32[8,128]{1,0:T(8,128)}, bf16[2,8,64,512]{3,2,1,0:T(8,128)(2,1)}, bf16[128,1024]{1,0:T(8,128)(2,1)}, bf16[3072,1024]{1,0:T(8,128)(2,1)}) custom-call(bf16[128,1024]{1,0:T(8,128)(2,1)} %x_ref.3, bf16[128,1024]{1,0:T(8,128)(2,1)} %dy_ref.3, f32[128,1024]{1,0:T(8,128)} %get-tuple-element.56.d_rows_ref, ...), custom_call_target="tpu_custom_call" | custom-call | flops 10000000000 | bytes 20000000 | tf_op jit(solution)/shard_map/pallas_call | solution.py:1898
  254.7 9.1 %shard_map.284 = (f32[2,1024,512]{2,1,0:T(8,128)}, f32[2,1024,512]{2,1,0:T(8,128)}, f32[2,512,1024]{2,1,0:T(8,128)}, bf16[128,1024]{1,0:T(8,128)(2,1)}, bf16[128...) custom-call(bf16[3072,1024]{1,0:T(8,128)(2,1)} %get-tuple-element.71, ...), custom_call_target="tpu_custom_call" | custom-call | tf_op jit(solution)/shard_map/pallas_call | solution.py:2070

commit v7 on v6

--- a/solution.py
+++ b/solution.py
@@ -236,8 +236,6 @@
         place = w_all_ref.at[t, pl.ds(pl.multiple_of(c * 128, 128), 128)]
         return copy_to(place, place, w_send.at[0], w_recv.at[t, c], to(0, 0, 1))
 
-    for i in (1, 7, 2, 6, 3, 5, 4):
-        w_push(i).start()
     w_own = pltpu.make_async_copy(w_t_ref, w_all_ref.at[tensor], load_sem.at[7])
     w_own.start()
 
@@ -384,6 +382,8 @@
     for load in loads:
         load.wait()
     relay(1).wait_recv()
+    for i in (1, 7, 2, 6, 3, 5, 4):
+        w_push(i).start()
 
     def step(a, carry):
         lax.fori_loop(0, 4, lambda q, c: (gather(a, q), c)[1], 0)

time: 264 us -> 267 us (1.011)
    pallas_call x1, Pallas kernels: 90.1 us -> 93.2 us  [moe(): pl.pallas_call(moe_kernel, out_shape=(jax.ShapeDtypeStruct((128, 1024), f...]
where the time goes in v7:
time: 267 us; the launch traced here: 266 us
  Pallas kernels  265 us (99%)
    pallas_call x1, Pallas kernels, backward(): pl.pallas_call(backward_kernel, out_shape=(shape((128, 1024), bf), shape(...  105 us
    pallas_call x1, Pallas kernels, moe(): pl.pallas_call(moe_kernel, out_shape=(jax.ShapeDtypeStruct((128, 1024), f...  93.2 us
    pallas_call x1, Pallas kernels, attention(): pl.pallas_call(attention_kernel, out_shape=(shape((128, 1024), bf), shape...  58 us
    pallas_call x1, Pallas kernels, finish(): pl.pallas_call(finish_kernel, out_shape=(shape((2, 1024, 512), f32), shap...  9.05 us

profile of v7, /device:TPU:1, one launch (start us, length us, event | category | flops | bytes accessed | tf_op | source)
XLA Modules:
  0.0 266.3 jit_solution(7211650188812499472)
XLA Ops:
  0.6 58.0 %shard_map.281 = (bf16[128,1024]{1,0:T(8,128)(2,1)}, f32[32,128]{1,0:T(8,128)}, f32[128,1024]{1,0:T(8,128)}, bf16[8,128,1024]{2,1,0:T(8,128)(2,1)}, f32[8,256,12...) custom-call(bf16[128,1024]{1,0:T(8,128)(2,1)} %x_ref.3, ...), custom_call_target="tpu_custom_call" | custom-call | flops 5000000000 | bytes 20000000 | tf_op jit(solution)/shard_map/pallas_call | solution.py:1011
  58.6 93.2 %shard_map.282 = (f32[128,1024]{1,0:T(8,128)}, f32[32,128]{1,0:T(8,128)}, bf16[16,128,1024]{2,1,0:T(8,128)(2,1)}, bf16[3072,1024]{1,0:T(8,128)(2,1)}, bf16[8,256,1024]{2,1,0:T(8,128)(2,1)}) custom-call(bf16[128,1024]{1,0:T(8,128)(2,1)} %get-tuple-element.52.rows_ref.rows2_ref, f32[32,128]{1,0:T(8,128)} %get-tuple-element.53.gate_ref.gates_ref, ...), custom_call_target="tpu_custom_call" | custom-call | flops 20000000000 | bytes 30000000 | tf_op jit(solution)/shard_map/pallas_call | solution.py:556
  151.9 105.2 %shard_map.283 = (bf16[128,1024]{1,0:T(8,128)(2,1)}, f32[8,128]{1,0:T(8,128)}, bf16[2,8,64,512]{3,2,1,0:T(8,128)(2,1)}, bf16[128,1024]{1,0:T(8,128)(2,1)}, bf16[3072,1024]{1,0:T(8,128)(2,1)}) custom-call(bf16[128,1024]{1,0:T(8,128)(2,1)} %x_ref.3, bf16[128,1024]{1,0:T(8,128)(2,1)} %dy_ref.3, f32[128,1024]{1,0:T(8,128)} %get-tuple-element.56.d_rows_ref, ...), custom_call_target="tpu_custom_call" | custom-call | flops 10000000000 | bytes 20000000 | tf_op jit(solution)/shard_map/pallas_call | solution.py:1898
  257.1 9.1 %shard_map.284 = (f32[2,1024,512]{2,1,0:T(8,128)}, f32[2,1024,512]{2,1,0:T(8,128)}, f32[2,512,1024]{2,1,0:T(8,128)}, bf16[128,1024]{1,0:T(8,128)(2,1)}, bf16[128...) custom-call(bf16[3072,1024]{1,0:T(8,128)(2,1)} %get-tuple-element.71, ...), custom_call_target="tpu_custom_call" | custom-call | tf_op jit(solution)/shard_map/pallas_call | solution.py:2070
